TPU v7x, 256 devices: a whole 4x4x8 slice. The times are simulated.
256 devices in a mesh: seq: 64 (over y, x, z_hi), cand: 4 (over z_lo, core).
Axes of the slice: x: 4, y: 4, z: 8 (z_hi: 4, z_lo: 2; z = z_hi * 2 + z_lo), core: 2. Of those that a mesh axis runs over, the one named last changes fastest.
Arguments:
- history_embed: bfloat16 [32768, 512], P('seq'), may hold values from -6 to 6
- candidate_embed: bfloat16 [2048, 512], P(('seq', 'cand')), may hold values from -6 to 6
- query_weight: bfloat16 [512, 512], replicated, may hold values from -0.25 to 0.25
- unit_weight: bfloat16 [512, 512], replicated, may hold values from -0.25 to 0.25
- keyval_weight: bfloat16 [512, 1024], replicated, may hold values from -0.25 to 0.25
- output_weight: bfloat16 [512, 512], replicated, may hold values from -0.25 to 0.25
- block_user: int32 [64], P('seq'), may hold values from 0 to 1, as said below
- block_length: int32 [64], P('seq'), may hold values from 128 to 512, as said below
- candidate_user: int32 [2048], P(('seq', 'cand')), may hold values from 0 to 1
- grad_output: bfloat16 [2048, 512], P(('seq', 'cand')), may hold values from -6 to 6
Outputs:
- candidate_output: bfloat16 [2048, 512], P(('seq', 'cand'))
- history_grad: bfloat16 [32768, 512], P('seq')
- candidate_grad: bfloat16 [2048, 512], P(('seq', 'cand'))
Inputs may be any that keep to these rules, and one draw needn't show every extreme that they name: block_user never falls from one block to the next; each of the 2 users owns at least one block. block_length is a multiple of 128; the valid events of a block are its first block_length ones; some block is full.
All inputs are finite; a program needn't handle non-finite values.
Results may differ from a plain program's by a relative error of at most 0.008.
Values may be sent and summed in bfloat16 or wider, within the bound.
No kernel may reach another device: no remote copies, remote signals or barrier semaphores. Data moves between devices by JAX's collectives and lax.ppermute only.
A program may use at most 64 MiB of HBM per device.

v0:
```python
from functools import partial

import jax
import jax.numpy as jnp
from jax import lax
from jax.sharding import PartitionSpec as P

HEADS = 8
TILE = 128


def head_split(values):
    return values.reshape(values.shape[0], HEADS, values.shape[1] // HEADS)


def silu_slope(linear):
    sigmoid_part = jax.nn.sigmoid(linear)
    return sigmoid_part * (1.0 + linear * (1.0 - sigmoid_part))


def normalize(attention):
    row_mean = jnp.mean(attention, axis=1, keepdims=True)
    centered = attention - row_mean
    inverse = lax.rsqrt(jnp.mean(centered * centered, axis=1, keepdims=True) + 1e-05)
    return (centered * inverse, inverse)


def attention_grad(normed, inverse, d_gated, unit_gate):
    grad_normed = d_gated * unit_gate.astype(jnp.float32)
    centered = (
        grad_normed
        - jnp.mean(grad_normed, axis=1, keepdims=True)
        - normed * jnp.mean(grad_normed * normed, axis=1, keepdims=True)
    )
    return (inverse * centered).astype(jnp.bfloat16)


def shards(
    history_embed,
    candidate_embed,
    query_weight,
    unit_weight,
    keyval_weight,
    output_weight,
    block_user,
    block_length,
    candidate_user,
    grad_output,
):
    model_width = candidate_embed.shape[1]
    cand_rows = candidate_embed.shape[0]
    score_scale = (model_width // HEADS) ** (-0.5)
    query = jnp.dot(candidate_embed, query_weight, preferred_element_type=jnp.float32).astype(
        jnp.bfloat16
    )
    unit_linear = jnp.dot(candidate_embed, unit_weight, preferred_element_type=jnp.float32)
    unit_gate = jax.nn.silu(unit_linear).astype(jnp.bfloat16)
    keyval = jnp.dot(history_embed, keyval_weight, preferred_element_type=jnp.float32).astype(
        jnp.bfloat16
    )
    events = history_embed.shape[0]
    blocks = block_user.shape[0]
    block_size = events // blocks
    all_query, all_unit, all_grad, all_users = (
        lax.all_gather(query, "seq", axis=0, tiled=True),
        lax.all_gather(unit_gate, "seq", axis=0, tiled=True),
        lax.all_gather(grad_output, "seq", axis=0, tiled=True),
        lax.all_gather(candidate_user, "seq", axis=0, tiled=True),
    )
    query_heads = head_split(all_query)
    total_rows = all_query.shape[0]
    position = jnp.arange(TILE, dtype=jnp.int32)

    def tile_inputs(block_index, tile_step):
        row_start = block_index * block_size + tile_step * TILE
        kv_piece = lax.dynamic_slice_in_dim(keyval, row_start, TILE, 0)
        key_tile = head_split(kv_piece[:, :model_width])
        value_tile = head_split(kv_piece[:, model_width:])
        live_mask = (
            (all_users[:, None] == block_user[block_index])
            & (tile_step * TILE + position[None, :] < block_length[block_index])
        ).astype(jnp.float32)[:, None, :]
        scores = (
            jnp.einsum("ghd,thd->ght", query_heads, key_tile, preferred_element_type=jnp.float32)
            * score_scale
        )
        return (row_start, key_tile, value_tile, live_mask, scores)

    def tile_count():
        return block_size // TILE

    def forward_tile(block_index, tile_step, running):
        row_start, key_tile, value_tile, live_mask, scores = tile_inputs(block_index, tile_step)
        weights = (jax.nn.silu(scores) * live_mask).astype(jnp.bfloat16)
        return running + jnp.einsum(
            "ght,thd->ghd", weights, value_tile, preferred_element_type=jnp.float32
        ).reshape(total_rows, model_width)

    attention_part = jnp.zeros((total_rows, model_width), jnp.float32)
    block_index = 0
    attention_part = lax.fori_loop(
        0, tile_count(), partial(forward_tile, block_index), attention_part
    )
    own_start = lax.axis_index("seq") * cand_rows
    attention = lax.psum(attention_part, "seq")
    normed, inverse = normalize(attention)
    d_gated_all = jnp.dot(all_grad, output_weight.T, preferred_element_type=jnp.float32)
    d_attention = attention_grad(normed, inverse, d_gated_all, all_unit)
    normed_own = lax.dynamic_slice_in_dim(normed, own_start, cand_rows, 0)
    d_gated_own = lax.dynamic_slice_in_dim(d_gated_all, own_start, cand_rows, 0)
    gated = (normed_own * unit_gate.astype(jnp.float32)).astype(jnp.bfloat16)
    candidate_output = (
        candidate_embed.astype(jnp.float32)
        + jnp.dot(gated, output_weight, preferred_element_type=jnp.float32)
    ).astype(jnp.bfloat16)
    d_unit = (d_gated_own * normed_own * silu_slope(unit_linear)).astype(jnp.bfloat16)
    grad_heads = head_split(d_attention)

    def backward_tile(block_index, tile_step, state_pair):
        sum_query, kv_grads = state_pair
        row_start, key_tile, value_tile, live_mask, scores = tile_inputs(block_index, tile_step)
        weights = (jax.nn.silu(scores) * live_mask).astype(jnp.bfloat16)
        grad_weights = jnp.einsum(
            "ghd,thd->ght", grad_heads, value_tile, preferred_element_type=jnp.float32
        )
        d_scores = (grad_weights * silu_slope(scores) * live_mask * score_scale).astype(
            jnp.bfloat16
        )
        sum_query = sum_query + jnp.einsum(
            "ght,thd->ghd", d_scores, key_tile, preferred_element_type=jnp.float32
        ).reshape(total_rows, model_width)
        key_grads = jnp.einsum(
            "ght,ghd->thd", d_scores, query_heads, preferred_element_type=jnp.float32
        ).reshape(TILE, model_width)
        value_grads = jnp.einsum(
            "ght,ghd->thd", weights, grad_heads, preferred_element_type=jnp.float32
        ).reshape(TILE, model_width)
        kv_grads = lax.dynamic_update_slice_in_dim(
            kv_grads, jnp.concatenate([key_grads, value_grads], axis=1), row_start, 0
        )
        return (sum_query, kv_grads)

    state_pair = (
        jnp.zeros((total_rows, model_width), jnp.float32),
        jnp.zeros((events, 2 * model_width), jnp.float32),
    )
    block_index = 0
    state_pair = lax.fori_loop(0, tile_count(), partial(backward_tile, block_index), state_pair)
    sum_query, kv_grads = state_pair
    weight_full = keyval_weight.astype(jnp.float32)
    d_keyval = lax.psum(kv_grads, "cand")
    history_grad = jnp.dot(
        d_keyval, weight_full.T, precision=lax.Precision.HIGHEST, preferred_element_type=jnp.float32
    ).astype(jnp.bfloat16)
    d_query_low = lax.psum_scatter(sum_query, "seq", scatter_dimension=0, tiled=True).astype(
        jnp.bfloat16
    )
    candidate_grad = (
        grad_output.astype(jnp.float32)
        + jnp.dot(d_query_low, query_weight.T, preferred_element_type=jnp.float32)
        + jnp.dot(d_unit, unit_weight.T, preferred_element_type=jnp.float32)
    ).astype(jnp.bfloat16)
    return (candidate_output, history_grad, candidate_grad)


def solution(mesh):
    in_specs = (
        P("seq", None),
        P(("seq", "cand"), None),
        P(),
        P(),
        P(),
        P(),
        P("seq"),
        P("seq"),
        P(("seq", "cand")),
        P(("seq", "cand"), None),
    )
    out_specs = (P(("seq", "cand"), None), P("seq", None), P(("seq", "cand"), None))
    return jax.shard_map(shards, mesh=mesh, in_specs=in_specs, out_specs=out_specs, check_vma=False)
```

profile of v0, /device:TPU:1, one launch (start us, length us, event | category | flops | bytes accessed | tf_op | source)
XLA Modules:
  0.0 1477.2 jit_solution(13916334790794293277)
XLA Ops:
  7.2 1.3 dynamic-slice
  10.1 24.7 %all-reduce = s32[512]{0:T(512)S(1)} all-reduce(s32[512]{0:T(512)S(1)} %dynamic-update-slice), channel_id=1, replica_groups=mesh['seq'=64,'cand'=4] {'seq'}, use_global_device_ids=true, to_apply=%add | all-reduce | flops 512 | bytes 4096
  34.8 1.2 convolution_convert_fusion.2
  36.0 160.7 %all_gather.12 = bf16[512,512]{1,0:T(8,128)(2,1)S(1)} all-gather(bf16[8,512]{1,0:T(8,128)(2,1)S(1)} %convolution_convert_fusion.2), channel_id=1, replica_groups=mesh['seq'=64,'cand'=4] {'seq'}, dimensions={0}, use_global_device_ids=true | all-gather | bytes 532480 | tf_op jit(solution)/shard_map/all_gather | solution.py:65
  196.9 2.8 convolution_convert_fusion
  199.7 2.3 copy.41
  202.0 24.5 %while.30 = (s32[]{:T(128)}, f32[512,512]{0,1:T(8,128)S(1)}, bf16[512,1024]{0,1:T(8,128)(2,1)}, bf16[512,8,64]{0,2,1:T(8,128)(2,1)S(1)}, s32[1]{0:T(128)}, /*ind...) while((s32[]{:T(128)}, f32[512,512]{0,1:T(8,128)S(1)}, ...), condition=%wide.region_1.2_spmd.clone, body=%wide.region_0.1_spmd.clone.sunk | while | flops 138543872 | bytes 6032853 | solution.py:101
  204.4 2.1 fusion.98
  206.5 1.6 bitcast_add_fusion.4
  210.5 2.1 fusion.98
  212.6 1.6 bitcast_add_fusion.4
  216.6 2.1 fusion.98
  218.8 1.6 bitcast_add_fusion.4
  222.8 2.1 fusion.98
  224.9 1.6 bitcast_add_fusion.4
  226.5 1.3 copy.42
  228.1 161.9 %all_gather.15 = bf16[512,512]{1,0:T(8,128)(2,1)S(1)} all-gather(bf16[8,512]{1,0:T(8,128)(2,1)S(1)} %get-tuple-element.460), channel_id=1, replica_groups=mesh['seq'=64,'cand'=4] {'seq'}, dimensions={0}, use_global_device_ids=true | all-gather | bytes 532480 | tf_op jit(solution)/shard_map/all_gather | solution.py:66
  390.0 171.6 %all_gather.14 = bf16[512,512]{1,0:T(8,128)(2,1)} all-gather(bf16[8,512]{1,0:T(8,128)(2,1)S(1)} %copy-done.8), channel_id=1, replica_groups=mesh['seq'=64,'cand'=4] {'seq'}, dimensions={0}, use_global_device_ids=true | all-gather | bytes 532480 | tf_op jit(solution)/shard_map/all_gather | solution.py:67
  561.7 379.0 %all-reduce.4.cloned.1.call-done = f32[512,512]{1,0:T(8,128)} async-done(((f32[512,512]{1,0:T(8,128)}), f32[512,512]{1,0:T(8,128)}) %all-reduce.4.cloned.1.call-update) | async-done | bytes 1048592 | tf_op jit(solution)/shard_map/psum | solution.py:105
  940.6 1.4 reduce_sum.36
  942.0 1.5 multiply_reduce_fusion.1
  943.5 2.2 fusion.35
  948.1 1.3 copy.44
  949.4 1.6 broadcast_in_dim.25
  950.9 27.1 %while.31 = (s32[]{:T(128)}, f32[512,512]{0,1:T(8,128)S(1)}, f32[512,1024]{0,1:T(8,128)}, bf16[512,1024]{0,1:T(8,128)(2,1)}, bf16[512,8,64]{0,2,1:T(8,128)(2,1)S...) while((s32[]{:T(128)}, f32[512,512]{0,1:T(8,128)S(1)}, ...), condition=%wide.region_8.9_spmd.clone, body=%wide.region_7.8_spmd.clone.sunk | while | flops 346292992 | bytes 19009000 | solution.py:148
  954.6 1.1 fusion.112
  961.4 1.1 fusion.112
  978.1 1.3 copy.52
  980.5 1.5 fusion.34
  982.9 371.2 %reduce-scatter.4.cloned.1.call-done = f32[8,512]{1,0:T(8,128)} async-done(((f32[512,512]{1,0:T(8,128)}), f32[8,512]{1,0:T(8,128)}) %reduce-scatter.4.cloned.1.call-update) | async-done | bytes 16400
  1355.9 108.9 %all-reduce.6.cloned.1.call-done = f32[512,1024]{0,1:T(8,128)} async-done(((f32[512,1024]{0,1:T(8,128)}), f32[512,1024]{0,1:T(8,128)}) %all-reduce.6.cloned.1.call-update) | async-done | bytes 2097168 | tf_op jit(solution)/shard_map/psum | solution.py:151
  1464.9 5.9 convolution_convert_fusion.1
  (95 shorter events, 41.8 us)
Async XLA Ops:
  7.2 189.8 %copy-start = (bf16[512,1024]{1,0:T(8,128)(2,1)S(1)}, bf16[512,1024]{1,0:T(8,128)(2,1)}, u32[]{:S(2)}) copy-start(bf16[512,1024]{1,0:T(8,128)(2,1)} %param.18) | copy-start | bytes 3145732
  7.2 933.4 %all-reduce.4.cloned.1.call-start = ((), (), s32[]{:S(2)}) async-start(), calls=%async_computation.1 | async-start | bytes 2097152 | tf_op jit(solution)/shard_map/psum | solution.py:105
  226.5 1.4 copy-start.4
  226.5 1.4 copy-start.7
  226.5 163.5 %copy-start.8 = (bf16[8,512]{1,0:T(8,128)(2,1)S(1)}, bf16[8,512]{1,0:T(8,128)(2,1)}, u32[]{:S(2)}) copy-start(bf16[8,512]{1,0:T(8,128)(2,1)} %param.23) | copy-start | bytes 24580
  227.9 1126.3 %reduce-scatter.4.cloned.1.call-start = ((), (), s32[]{:S(2)}) async-start(), calls=%async_computation.3 | async-start | bytes 1064960
  945.7 1.0 copy-start.1
  945.7 1.3 copy-start.2
  979.4 1.0 copy-start.3
  979.4 2.5 copy-start.5
  979.4 375.6 %copy-start.6 = (bf16[512,512]{1,0:T(8,128)(2,1)S(1)}, bf16[512,512]{1,0:T(8,128)(2,1)}, u32[]{:S(2)}) copy-start(bf16[512,512]{1,0:T(8,128)(2,1)} %param.16) | copy-start | bytes 1572868
  979.4 485.4 %all-reduce.6.cloned.1.call-start = ((), (), s32[]{:S(2)}) async-start(), calls=%async_computation.2 | async-start | bytes 4194304 | tf_op jit(solution)/shard_map/psum | solution.py:151
Sparse Core Ops, SparseCore 0:
  228.0 712.5 all-reduce.3
  979.6 374.5 reduce-scatter.3
  1356.8 107.9 all-reduce.5
where the time goes:
time: 1480 us
  waiting for transfers between devices  860 us (58%)
  blocking collectives  519 us (35%)
  matrix products  36.8 us (2%)
  other arithmetic  26 us (2%)
  local copies, waits for them, and re-layouts  20.6 us (1%)
    psum x1, waiting for transfers between devices, shards(): attention = lax.psum(attention_part, 'seq')  379 us
    unnamed x4, waiting for transfers between devices  372 us
    all_gather x1, blocking collectives, shards(): lax.all_gather(grad_output, 'seq', axis=0, tiled=True)  172 us
    all_gather x1, blocking collectives, shards(): lax.all_gather(unit_gate, 'seq', axis=0, tiled=True)  162 us
    all_gather x1, blocking collectives, shards(): lax.all_gather(query, 'seq', axis=0, tiled=True)  161 us
    psum x1, waiting for transfers between devices, shards(): d_keyval = lax.psum(kv_grads, 'cand')  109 us
  transfers between devices with their start and end apart: 3, of which 3 were waited for; matrix products, arithmetic and copies ran while one was open for 0% of the time, Pallas kernels for 0%

commit v1 on v0

v1 whole, which is shorter than its diff:
```python
from functools import partial

import jax
import jax.numpy as jnp
from jax import lax
from jax.experimental import pallas as pl
from jax.experimental.pallas import tpu as pltpu
from jax.sharding import PartitionSpec as P

HEADS = 8
PAIRS = 4
LANES = 128
F32 = jnp.float32
BF16 = jnp.bfloat16
VMEM_BYTES = 48 * 1024 * 1024


def nn(a, b):
    return lax.dot_general(a, b, (((1,), (0,)), ((), ())), preferred_element_type=F32)


def nt(a, b):
    return lax.dot_general(a, b, (((1,), (1,)), ((), ())), preferred_element_type=F32)


def call(body, outs, scratch=(), smem=(), count=0, flops=0):
    spec = pl.BlockSpec(memory_space=pltpu.VMEM)
    sspec = pl.BlockSpec(memory_space=pltpu.SMEM)
    return pl.pallas_call(
        body,
        out_shape=outs,
        in_specs=[sspec if i in smem else spec for i in range(count)],
        out_specs=jax.tree.map(lambda _: spec, outs),
        scratch_shapes=list(scratch),
        compiler_params=pltpu.CompilerParams(vmem_limit_bytes=VMEM_BYTES),
        cost_estimate=pl.CostEstimate(flops=flops, bytes_accessed=1 << 20, transcendentals=0),
    )


def keyval_kernel(length_ref, hist_ref, weight_ref, key_ref, value_ref):
    events = hist_ref.shape[0]
    keyval = nn(hist_ref[...], weight_ref[...])
    row = lax.broadcasted_iota(jnp.int32, (events, LANES), 0)
    lane = lax.broadcasted_iota(jnp.int32, (events, LANES), 1)
    live = row < length_ref[0]
    half = LANES // 2
    for p in range(PAIRS):
        for ref, base in ((key_ref, 0), (value_ref, PAIRS * LANES)):
            part = keyval[:, base + p * LANES : base + (p + 1) * LANES]
            ref[p, :events, :] = jnp.where(live & (lane < half), part, 0.0).astype(BF16)
            ref[p, events:, :] = jnp.where(live & (lane >= half), part, 0.0).astype(BF16)


def forward_kernel(user_ref, pay_ref, weight_ref, key_ref, value_ref, query_ref, att_ref):
    rows, width = query_ref.shape
    chunk = 128
    owner = user_ref[0].astype(F32)

    def step(i, carry):
        r = pl.ds(pl.multiple_of(i * chunk, chunk), chunk)
        pay = pay_ref[r, :]
        mine = pay[:, width : width + 1].astype(F32) == owner
        query = nn(pay[:, :width], weight_ref[...]).astype(BF16).astype(F32)
        scaled = jnp.where(mine, query * 0.0625, 0.0).astype(BF16)
        query_ref[r, :] = scaled
        for p in range(PAIRS):
            cols = slice(p * LANES, (p + 1) * LANES)
            u = nt(scaled[:, cols], key_ref[p])
            w = (u + u * jnp.tanh(u)).astype(BF16)
            att_ref[r, cols] = nn(w, value_ref[p]).astype(BF16)
        return carry

    lax.fori_loop(0, rows // chunk, step, 0)


def slope_kernel(query_ref, key_ref, slope_ref, slope_t_ref, weight_t_ref):
    rows = query_ref.shape[0]
    both = key_ref.shape[1]
    chunk = 128

    def one(u):
        t = jnp.tanh(u)
        return t, (1.0 + t) + u * (1.0 - t * t)

    for p in range(PAIRS):
        cols = slice(p * LANES, (p + 1) * LANES)

        def step(i, carry, p=p, cols=cols):
            r = pl.ds(pl.multiple_of(i * chunk, chunk), chunk)
            u = nt(query_ref[r, cols], key_ref[p])
            slope_ref[p, r, :] = one(u)[1].astype(BF16)
            return carry

        lax.fori_loop(0, rows // chunk, step, 0)

        def step_t(i, carry, p=p, cols=cols):
            r = pl.ds(pl.multiple_of(i * chunk, chunk), chunk)
            u = nt(key_ref[p, r, :], query_ref[:, cols])
            t, slope = one(u)
            slope_t_ref[p, r, :] = slope.astype(BF16)
            weight_t_ref[p, r, :] = (u + u * t).astype(BF16)
            return carry

        lax.fori_loop(0, both // chunk, step_t, 0)


def own_kernel(pay_ref, grad_ref, unit_ref, out_ref, gate_ref, uslope_ref, dgated_ref):
    width = grad_ref.shape[1]
    linear = nn(pay_ref[...][:, :width], unit_ref[...])
    sig = jax.nn.sigmoid(linear)
    gate_ref[...] = (linear * sig).astype(BF16).astype(F32)
    uslope_ref[...] = sig * (1.0 + linear * (1.0 - sig))
    dgated_ref[...] = nt(grad_ref[...], out_ref[...])


def norm_kernel(part_ref, gate_ref, dgated_ref, uslope_ref, datt_ref, gated_ref, dunit_ref):
    own, width = gate_ref.shape
    total = part_ref.shape[0]
    att = jnp.sum(part_ref[...].astype(F32).reshape(total // own, own, width), axis=0)
    mean = jnp.mean(att, axis=1, keepdims=True)
    centered = att - mean
    inverse = lax.rsqrt(jnp.mean(centered * centered, axis=1, keepdims=True) + 1e-05)
    normed = centered * inverse
    gate = gate_ref[...]
    dgated = dgated_ref[...]
    g = dgated * gate
    datt = inverse * (
        g
        - jnp.mean(g, axis=1, keepdims=True)
        - normed * jnp.mean(g * normed, axis=1, keepdims=True)
    )
    datt_ref[...] = datt.astype(BF16)
    gated_ref[...] = (normed * gate).astype(BF16)
    dunit_ref[...] = (dgated * normed * uslope_ref[...]).astype(BF16)


def output_kernel(embed_ref, grad_ref, gated_ref, dunit_ref, out_ref, unit_ref, result_ref, base_ref):
    result_ref[...] = (embed_ref[...].astype(F32) + nn(gated_ref[...], out_ref[...])).astype(BF16)
    base_ref[...] = grad_ref[...].astype(F32) + nt(dunit_ref[...], unit_ref[...])


def backward_kernel(user_ref, pay_ref, datt_ref, key_ref, value_ref, slope_ref, masked_ref, dq_ref):
    rows, width = datt_ref.shape
    chunk = 128
    owner = user_ref[0].astype(F32)

    def step(i, carry):
        r = pl.ds(pl.multiple_of(i * chunk, chunk), chunk)
        mine = pay_ref[r, width : width + 1].astype(F32) == owner
        datt = jnp.where(mine, datt_ref[r, :].astype(F32), 0.0).astype(BF16)
        masked_ref[r, :] = datt
        for p in range(PAIRS):
            cols = slice(p * LANES, (p + 1) * LANES)
            dw = nt(datt[:, cols], value_ref[p])
            ds = (dw * slope_ref[p, r, :].astype(F32)).astype(BF16)
            dq_ref[r, cols] = nn(ds, key_ref[p]).astype(BF16)
        return carry

    lax.fori_loop(0, rows // chunk, step, 0)


def keyval_grad_kernel(
    query_ref, datt_ref, value_ref, slope_t_ref, weight_t_ref, kvw_ref, grad_ref, dkv_ref
):
    events = value_ref.shape[1] // 2
    width = datt_ref.shape[1]
    chunk = 128
    low = lax.broadcasted_iota(jnp.int32, (chunk, LANES), 1) < LANES // 2

    def step(i, carry):
        r = pl.ds(pl.multiple_of(i * chunk, chunk), chunk)
        r2 = pl.ds(pl.multiple_of(events + i * chunk, chunk), chunk)
        for p in range(PAIRS):
            cols = slice(p * LANES, (p + 1) * LANES)
            datt = datt_ref[:, cols]
            query = query_ref[:, cols]
            dks, dvs = [], []
            for rr in (r, r2):
                dw = nt(value_ref[p, rr, :], datt)
                ds = (dw * slope_t_ref[p, rr, :].astype(F32)).astype(BF16)
                dks.append(nn(ds, query))
                dvs.append(nn(weight_t_ref[p, rr, :], datt))
            dkv_ref[r, cols] = jnp.where(low, dks[0], dks[1]).astype(BF16)
            vcols = slice(width + p * LANES, width + (p + 1) * LANES)
            dkv_ref[r, vcols] = jnp.where(low, dvs[0], dvs[1]).astype(BF16)
        grad_ref[r, :] = nt(dkv_ref[r, :], kvw_ref[...]).astype(BF16)
        return carry

    lax.fori_loop(0, events // chunk, step, 0)


def final_kernel(part_ref, base_ref, weight_ref, result_ref):
    own, width = base_ref.shape
    total = part_ref.shape[0]
    dq = jnp.sum(part_ref[...].astype(F32).reshape(total // own, own, width), axis=0) * 0.0625
    result_ref[...] = (base_ref[...] + nt(dq.astype(BF16), weight_ref[...])).astype(BF16)


def shards(
    history_embed,
    candidate_embed,
    query_weight,
    unit_weight,
    keyval_weight,
    output_weight,
    block_user,
    block_length,
    candidate_user,
    grad_output,
):
    own, width = candidate_embed.shape
    events = history_embed.shape[0]
    groups = lax.axis_size("seq")
    rows = own * groups
    s = jax.ShapeDtypeStruct

    user = jnp.broadcast_to(candidate_user.astype(BF16)[:, None], (own, LANES))
    pay = jnp.concatenate([candidate_embed, user], axis=1)
    pay_all = lax.all_to_all(
        jnp.broadcast_to(pay, (groups, own, width + LANES)), "seq", 0, 0
    ).reshape(rows, width + LANES)

    wide = s((PAIRS, 2 * events, LANES), BF16)
    keys, values = call(keyval_kernel, [wide, wide], smem=(0,), count=3, flops=1 << 30)(
        block_length, history_embed, keyval_weight
    )
    own_f32 = s((own, width), F32)
    own_b16 = s((own, width), BF16)
    gate, uslope, dgated = call(own_kernel, [own_f32] * 3, count=4, flops=1 << 26)(
        candidate_embed, grad_output, unit_weight, output_weight
    )
    big = s((rows, width), BF16)
    query, att = call(forward_kernel, [big, big], smem=(0,), count=5, flops=1 << 31)(
        block_user, pay_all, query_weight, keys, values
    )
    att_all = lax.all_to_all(att.reshape(groups, own, width), "seq", 0, 0).reshape(rows, width)
    slope, slope_t, weight_t = call(
        slope_kernel,
        [
            s((PAIRS, rows, 2 * events), BF16),
            s((PAIRS, 2 * events, rows), BF16),
            s((PAIRS, 2 * events, rows), BF16),
        ],
        count=2,
        flops=1 << 32,
    )(query, keys)
    datt, gated, dunit = call(norm_kernel, [own_b16] * 3, count=4, flops=1 << 20)(
        att_all, gate, dgated, uslope
    )
    datt_all = lax.all_to_all(
        jnp.broadcast_to(datt, (groups, own, width)), "seq", 0, 0
    ).reshape(rows, width)
    candidate_output, base = call(output_kernel, [own_b16, own_f32], count=6, flops=1 << 26)(
        candidate_embed, grad_output, gated, dunit, output_weight, unit_weight
    )
    masked, dq = call(backward_kernel, [big, big], smem=(0,), count=6, flops=1 << 31)(
        block_user, pay_all, datt_all, keys, values, slope
    )
    dq_all = lax.all_to_all(dq.reshape(groups, own, width), "seq", 0, 0).reshape(rows, width)
    hist_part = call(
        keyval_grad_kernel,
        s((events, width), BF16),
        scratch=[pltpu.VMEM((events, 2 * width), BF16)],
        count=6,
        flops=1 << 32,
    )(query, masked, values, slope_t, weight_t, keyval_weight)

    cand = lax.axis_index("cand")
    core = cand % 2
    half = events // 2
    mine = lax.dynamic_slice_in_dim(hist_part, core * half, half, 0)
    other = lax.dynamic_slice_in_dim(hist_part, (1 - core) * half, half, 0)
    swap_core = [(i, i ^ 1) for i in range(4)]
    swap_chip = [(i, i ^ 2) for i in range(4)]
    got = lax.ppermute(other, "cand", swap_core)
    pair = (mine.astype(F32) + got.astype(F32)).astype(BF16)
    got = lax.ppermute(pair, "cand", swap_chip)
    quad = (pair.astype(F32) + got.astype(F32)).astype(BF16)
    got = lax.ppermute(quad, "cand", swap_core)
    history_grad = jnp.where(
        core == 0,
        jnp.concatenate([quad, got], axis=0),
        jnp.concatenate([got, quad], axis=0),
    )
    candidate_grad = call(final_kernel, own_b16, count=3, flops=1 << 26)(
        dq_all, base, query_weight
    )
    return (candidate_output, history_grad, candidate_grad)


def solution(mesh):
    in_specs = (
        P("seq", None),
        P(("seq", "cand"), None),
        P(),
        P(),
        P(),
        P(),
        P("seq"),
        P("seq"),
        P(("seq", "cand")),
        P(("seq", "cand"), None),
    )
    out_specs = (P(("seq", "cand"), None), P("seq", None), P(("seq", "cand"), None))
    return jax.shard_map(shards, mesh=mesh, in_specs=in_specs, out_specs=out_specs, check_vma=False)
```

time: 1480 us -> 157 us (0.11)
  waiting for transfers between devices: 860 us -> 48.2 us
  blocking collectives: 519 us -> 0 us
  Pallas kernels: 0 us -> 44.2 us
  starting transfers between devices: 0.3 us -> 43.9 us
  matrix products: 36.8 us -> 0 us
  other arithmetic: 26 us -> 3.51 us
    all_gather x3 -> x0, blocking collectives: 494 us -> none  [the longest x1 172 us: shards(): lax.all_gather(grad_output, 'seq', axis=0, tiled=True)]
    psum x2 -> x0, waiting for transfers between devices: 488 us -> none  [the longest x1 379 us: shards(): attention = lax.psum(attention_part, 'seq')]
    unnamed x4 -> x0, waiting for transfers between devices: 372 us -> none
    pallas_call x0 -> x9, Pallas kernels: none -> 44.2 us  [the longest x1 16 us: shards(): call(slope_kernel, [s((PAIRS, rows, 2 * events), BF16), s((PAIRS, 2 * eve...]
    all_to_all x0 -> x4, starting transfers between devices: none -> 41.2 us  [the longest x1 15.1 us: shards(): lax.all_to_all(jnp.broadcast_to(pay, (groups, own, width + LANES)), 'seq'...]
    dot_general x32 -> x0, matrix products: 36.8 us -> none  [the longest x4 8.42 us: forward_tile(): jnp.einsum('ght,thd->ghd', weights, value_tile, preferred_element_type=jn...]
    all_to_all x0 -> x4, waiting for transfers between devices: none -> 32.1 us  [the longest x1 17.3 us: shards(): lax.all_to_all(att.reshape(groups, own, width), 'seq', 0, 0)]
    unnamed x1 -> x0, blocking collectives: 24.7 us -> none
  transfers between devices with their start and end apart: 3 -> 7, of which waited for: 3 -> 4; matrix products, arithmetic and copies ran while one was open for 0% -> 1% of each run, Pallas kernels for 0% -> 11%
where the time goes in v1:
time: 157 us; the launch traced here: 156 us
  waiting for transfers between devices  48.2 us (31%)
  Pallas kernels  44.2 us (28%)
  starting transfers between devices  43.9 us (28%)
  local copies, waits for them, and re-layouts  14.3 us (9%)
  other arithmetic  3.51 us (2%)
  between operations  2.11 us (1%)
    all_to_all x1, waiting for transfers between devices, shards(): lax.all_to_all(att.reshape(groups, own, width), 'seq', 0, 0)  17.3 us
    pallas_call x1, Pallas kernels, shards(): call(slope_kernel, [s((PAIRS, rows, 2 * events), BF16), s((PAIRS, 2 * eve...  16 us
    ppermute x1, waiting for transfers between devices, shards(): got = lax.ppermute(pair, 'cand', swap_chip)  15.7 us
    all_to_all x1, starting transfers between devices, shards(): lax.all_to_all(jnp.broadcast_to(pay, (groups, own, width + LANES)), 'seq'...  15.1 us
    all_to_all x1, waiting for transfers between devices, shards(): lax.all_to_all(jnp.broadcast_to(pay, (groups, own, width + LANES)), 'seq'...  14.8 us
    all_to_all x1, starting transfers between devices, shards(): lax.all_to_all(dq.reshape(groups, own, width), 'seq', 0, 0)  12.5 us
    unnamed x32, local copies, waits for them, and re-layouts  12.5 us
    pallas_call x1, Pallas kernels, shards(): call(keyval_grad_kernel, s((events, width), BF16), scratch=[pltpu.VMEM((e...  12.3 us
  transfers between devices with their start and end apart: 7, of which 4 were waited for; matrix products, arithmetic and copies ran while one was open for 1% of the time, Pallas kernels for 11%

profile of v1, /device:TPU:1, one launch (start us, length us, event | category | flops | bytes accessed | tf_op | source)
XLA Modules:
  0.0 156.3 jit_solution(7416115539333168611)
XLA Ops:
  0.6 0.7 convert_element_type.21
  1.4 0.7 pad_maximum_fusion
  2.1 0.9 broadcast_in_dim.13
  3.0 15.1 %all-to-all-start = ((bf16[64,8,640]{2,1,0:T(8,128)(2,1)}), bf16[64,8,640]{2,1,0:T(8,128)(2,1)S(1)}, u32[]{:S(2)}, u32[]{:S(2)}) async-start(bf16[64,8,640]{2,1,0:T(8,128)(2,1)} %broadcast_in_dim.13), calls=%async_computation | async-start | bytes 1310720 | tf_op jit(solution)/shard_map/all_to_all | solution.py:219
  19.4 1.2 copy-done.5
  20.7 1.0 copy-done.7
  21.7 0.8 shard_map.121
  22.5 1.0 copy-done.9
  23.5 1.0 copy-done.12
  24.4 14.8 %all-to-all-done = bf16[64,8,640]{2,1,0:T(8,128)(2,1)S(1)} async-done(((bf16[64,8,640]{2,1,0:T(8,128)(2,1)}), bf16[64,8,640]{2,1,0:T(8,128)(2,1)S(1)}, u32[]{:S(2)}, u32[]{:S(2)}) %all-to-all-start) | async-done | bytes 655392 | tf_op jit(solution)/shard_map/all_to_all | solution.py:219
  39.2 1.2 copy-done.10
  40.5 1.2 copy-done.13
  41.7 5.7 %shard_map.122 = (bf16[512,512]{1,0:T(8,128)(2,1)S(1)}, bf16[512,512]{1,0:T(8,128)(2,1)}) custom-call(s32[1]{0:T(128)S(6)} %copy.13.user_ref, bf16[512,640]{1,0:T(8,128)(2,1)S(1)} %bitcast.8, bf16[512,512]{1,0:T(8,128)(2,1)S(1)} %copy-done.2, bf16[4,1024,128]{2,1,0:T(8,128)(2,1)S(1)} %copy-done.13, bf16[4,1024,128]{2,1,0:T(8,128)(2,1)S(1)} %copy-done.10), custom_call_target="tpu_custom_call" | custom-call | flops 2147483648 | bytes 1048576 | tf_op jit(solution)/shard_map/pallas_call | solution.py:233
  47.4 6.3 %all-to-all-start.1 = ((bf16[64,8,512]{2,1,0:T(8,128)(2,1)}), bf16[64,8,512]{2,1,0:T(8,128)(2,1)S(1)}, u32[]{:S(2)}, u32[]{:S(2)}) async-start(bf16[64,8,512]{2,1,0:T(8,128)(2,1)} %bitcast.1), calls=%async_computation.1 | async-start | bytes 1048576 | tf_op jit(solution)/shard_map/all_to_all | solution.py:236
  54.1 17.3 %all-to-all-done.1 = bf16[64,8,512]{2,1,0:T(8,128)(2,1)S(1)} async-done(((bf16[64,8,512]{2,1,0:T(8,128)(2,1)}), bf16[64,8,512]{2,1,0:T(8,128)(2,1)S(1)}, u32[]{:S(2)}, u32[]{:S(2)}) %all-to-all-start.1) | async-done | bytes 524320 | tf_op jit(solution)/shard_map/all_to_all | solution.py:236
  71.7 0.8 broadcast_in_dim.14
  72.6 7.3 %all-to-all-start.2 = ((bf16[64,8,512]{2,1,0:T(8,128)(2,1)}), bf16[64,8,512]{2,1,0:T(8,128)(2,1)S(1)}, u32[]{:S(2)}, u32[]{:S(2)}) async-start(bf16[64,8,512]{2,1,0:T(8,128)(2,1)} %broadcast_in_dim.14), calls=%async_computation.2 | async-start | bytes 1048576 | tf_op jit(solution)/shard_map/all_to_all | solution.py:250
  79.9 1.2 copy-done.14
  81.1 16.0 %shard_map.126 = (bf16[4,512,1024]{2,1,0:T(8,128)(2,1)S(1)}, bf16[4,1024,512]{2,1,0:T(8,128)(2,1)}, bf16[4,1024,512]{2,1,0:T(8,128)(2,1)}) custom-call(bf16[512,512]{1,0:T(8,128)(2,1)S(1)} %get-tuple-element.29.query_ref, bf16[4,1024,128]{2,1,0:T(8,128)(2,1)S(1)} %copy-done.14), custom_call_target="tpu_custom_call" | custom-call | flops 4294967296 | bytes 1048576 | tf_op jit(solution)/shard_map/pallas_call | solution.py:237
  97.1 2.0 %copy-done.8 = bf16[4,512,1024]{2,1,0:T(8,128)(2,1)} copy-done((bf16[4,512,1024]{2,1,0:T(8,128)(2,1)}, bf16[4,512,1024]{2,1,0:T(8,128)(2,1)S(1)}, u32[]{:S(2)}) %copy-start.8) | copy-done | bytes 4194328
  99.1 1.3 copy-done.11
  100.5 1.2 copy-done.15
  101.7 7.2 %shard_map.127 = (bf16[512,512]{1,0:T(8,128)(2,1)S(1)}, bf16[512,512]{1,0:T(8,128)(2,1)}) custom-call(s32[1]{0:T(128)S(6)} %copy.13.user_ref, bf16[512,640]{1,0:T(8,128)(2,1)S(1)} %bitcast.9, bf16[512,512]{1,0:T(8,128)(2,1)S(1)} %bitcast.10, bf16[4,1024,128]{2,1,0:T(8,128)(2,1)S(1)} %copy-done.15, bf16[4,1024,128]{2,1,0:T(8,128)(2,1)S(1)} %copy-done.11, ...), custom_call_target="tpu_custom_call" | custom-call | flops 2147483648 | bytes 1048576 | tf_op jit(solution)/shard_map/pallas_call | solution.py:256
  108.9 12.3 %shard_map.128 = bf16[512,512]{1,0:T(8,128)(2,1)S(1)} custom-call(bf16[512,512]{1,0:T(8,128)(2,1)S(1)} %get-tuple-element.29.query_ref, bf16[512,512]{1,0:T(8,128)(2,1)S(1)} %get-tuple-element.32.datt_ref, bf16[4,1024,128]{2,1,0:T(8,128)(2,1)S(1)} %copy-done.11, bf16[4,1024,512]{2,1,0:T(8,128)(2,1)} %get-tuple-element.33.slope_t_ref, ...), custom_call_target="tpu_custom_call" | custom-call | flops 4294967296 | bytes 1048576 | tf_op jit(solution)/shard_map/pallas_call | solution.py:260
  121.2 1.7 %collective-permute-start = (bf16[256,512]{1,0:T(8,128)(2,1)S(1)}, bf16[256,512]{1,0:T(8,128)(2,1)}, u32[]{:S(2)}, u32[]{:S(2)}) collective-permute-start(bf16[256,512]{1,0:T(8,128)(2,1)S(1)} %constant_dynamic-slice_fusion), channel_id=1, source_target_pairs={{0,1},{1,0},{2,3},{3,2},{4,5},{5,4},{6,7},{7,6},{8,9},{9,8},{10,11... | collective-permute-start | bytes 786440 | tf_op jit(solution)/shard_map/ppermute | solution.py:275
  122.9 12.5 %all-to-all-start.3 = ((bf16[64,8,512]{2,1,0:T(8,128)(2,1)}), bf16[64,8,512]{2,1,0:T(8,128)(2,1)S(1)}, u32[]{:S(2)}, u32[]{:S(2)}) async-start(bf16[64,8,512]{2,1,0:T(8,128)(2,1)} %bitcast.4), calls=%async_computation.3 | async-start | bytes 1048576 | tf_op jit(solution)/shard_map/all_to_all | solution.py:259
  135.4 1.0 add_convert_fusion.1
  136.5 15.7 %collective-permute-done.1 = bf16[256,512]{1,0:T(8,128)(2,1)S(1)} collective-permute-done((bf16[256,512]{1,0:T(8,128)(2,1)S(1)}, bf16[256,512]{1,0:T(8,128)(2,1)S(1)}, u32[]{:S(2)}, u32[]{:S(2)}) %collective-permute-start.1) | collective-permute-done | bytes 262176 | tf_op jit(solution)/shard_map/ppermute | solution.py:277
  152.3 0.9 collective-permute-start.2
  153.2 0.8 shard_map.125
  154.3 1.0 maximum_select_fusion
  155.3 0.9 shard_map.129
  (32 shorter events, 1.3 us)
Async XLA Ops:
  0.6 38.6 %copy-start.2 = (bf16[512,512]{1,0:T(8,128)(2,1)S(1)}, bf16[512,512]{1,0:T(8,128)(2,1)}, u32[]{:S(2)}) copy-start(bf16[512,512]{1,0:T(8,128)(2,1)} %weight_ref.5) | copy-start | bytes 1572868
  3.0 36.2 %all-to-all-start = ((bf16[64,8,640]{2,1,0:T(8,128)(2,1)}), bf16[64,8,640]{2,1,0:T(8,128)(2,1)S(1)}, u32[]{:S(2)}, u32[]{:S(2)}) async-start(bf16[64,8,640]{2,1,0:T(8,128)(2,1)} %broadcast_in_dim.13), calls=%async_computation | async-start | bytes 1310720 | tf_op jit(solution)/shard_map/all_to_all | solution.py:219
  19.4 1.2 copy-start.5
  20.7 1.0 copy-start.7
  22.5 1.0 copy-start.9
  23.5 1.0 copy-start.12
  39.2 1.2 copy-start.10
  40.5 1.2 copy-start.13
  41.7 12.0 %copy-start = (bf16[512,512]{1,0:T(8,128)(2,1)S(1)}, bf16[512,512]{1,0:T(8,128)(2,1)}, u32[]{:S(2)}) copy-start(bf16[512,512]{1,0:T(8,128)(2,1)} %unit_ref.3) | copy-start | bytes 1572868
  41.7 12.0 %copy-start.1 = (bf16[512,512]{1,0:T(8,128)(2,1)S(1)}, bf16[512,512]{1,0:T(8,128)(2,1)}, u32[]{:S(2)}) copy-start(bf16[512,512]{1,0:T(8,128)(2,1)} %out_ref.3) | copy-start | bytes 1572868
  41.7 12.0 %copy-start.3 = (bf16[8,512]{1,0:T(8,128)(2,1)S(1)}, bf16[8,512]{1,0:T(8,128)(2,1)}, u32[]{:S(2)}) copy-start(bf16[8,512]{1,0:T(8,128)(2,1)} %embed_ref.1) | copy-start | bytes 24580
  41.7 12.1 %copy-start.4 = (bf16[8,512]{1,0:T(8,128)(2,1)S(1)}, bf16[8,512]{1,0:T(8,128)(2,1)}, u32[]{:S(2)}) copy-start(bf16[8,512]{1,0:T(8,128)(2,1)} %grad_ref.3) | copy-start | bytes 24580
  47.4 24.0 %all-to-all-start.1 = ((bf16[64,8,512]{2,1,0:T(8,128)(2,1)}), bf16[64,8,512]{2,1,0:T(8,128)(2,1)S(1)}, u32[]{:S(2)}, u32[]{:S(2)}) async-start(bf16[64,8,512]{2,1,0:T(8,128)(2,1)} %bitcast.1), calls=%async_computation.1 | async-start | bytes 1048576 | tf_op jit(solution)/shard_map/all_to_all | solution.py:236
  72.6 26.6 %all-to-all-start.2 = ((bf16[64,8,512]{2,1,0:T(8,128)(2,1)}), bf16[64,8,512]{2,1,0:T(8,128)(2,1)S(1)}, u32[]{:S(2)}, u32[]{:S(2)}) async-start(bf16[64,8,512]{2,1,0:T(8,128)(2,1)} %broadcast_in_dim.14), calls=%async_computation.2 | async-start | bytes 1048576 | tf_op jit(solution)/shard_map/all_to_all | solution.py:250
  79.9 1.2 copy-start.14
  97.1 2.0 %copy-start.8 = (bf16[4,512,1024]{2,1,0:T(8,128)(2,1)}, bf16[4,512,1024]{2,1,0:T(8,128)(2,1)S(1)}, u32[]{:S(2)}) copy-start(bf16[4,512,1024]{2,1,0:T(8,128)(2,1)S(1)} %get-tuple-element.31.slope_ref) | copy-start | bytes 12582916
  99.1 9.7 %copy-start.6 = (bf16[512,1024]{1,0:T(8,128)(2,1)S(1)}, bf16[512,1024]{1,0:T(8,128)(2,1)}, u32[]{:S(2)}) copy-start(bf16[512,1024]{1,0:T(8,128)(2,1)} %kvw_ref.1) | copy-start | bytes 3145732
  99.1 1.3 copy-start.11
  100.5 1.2 copy-start.15
  121.2 14.2 %collective-permute-start = (bf16[256,512]{1,0:T(8,128)(2,1)S(1)}, bf16[256,512]{1,0:T(8,128)(2,1)}, u32[]{:S(2)}, u32[]{:S(2)}) collective-permute-start(bf16[256,512]{1,0:T(8,128)(2,1)S(1)} %constant_dynamic-slice_fusion), channel_id=1, source_target_pairs={{0,1},{1,0},{2,3},{3,2},{4,5},{5,4},{6,7},{7,6},{8,9},{9,8},{10,11... | collective-permute-start | bytes 786440 | tf_op jit(solution)/shard_map/ppermute | solution.py:275
  122.9 32.5 %all-to-all-start.3 = ((bf16[64,8,512]{2,1,0:T(8,128)(2,1)}), bf16[64,8,512]{2,1,0:T(8,128)(2,1)S(1)}, u32[]{:S(2)}, u32[]{:S(2)}) async-start(bf16[64,8,512]{2,1,0:T(8,128)(2,1)} %bitcast.4), calls=%async_computation.3 | async-start | bytes 1048576 | tf_op jit(solution)/shard_map/all_to_all | solution.py:259
  136.4 15.8 %collective-permute-start.1 = (bf16[256,512]{1,0:T(8,128)(2,1)S(1)}, bf16[256,512]{1,0:T(8,128)(2,1)S(1)}, u32[]{:S(2)}, u32[]{:S(2)}) collective-permute-start(bf16[256,512]{1,0:T(8,128)(2,1)S(1)} %add_convert_fusion.1), channel_id=1, source_target_pairs={{0,2},{1,3},{2,0},{3,1},{4,6},{5,7},{6,4},{7,5},{8,10},{9,11},{10,... | collective-permute-start | bytes 786440 | tf_op jit(solution)/shard_map/ppermute | solution.py:277
  152.3 2.1 %collective-permute-start.2 = (bf16[256,512]{1,0:T(8,128)(2,1)S(1)}, bf16[256,512]{1,0:T(8,128)(2,1)S(1)}, u32[]{:S(2)}, u32[]{:S(2)}) collective-permute-start(bf16[256,512]{1,0:T(8,128)(2,1)S(1)} %add_convert_fusion), channel_id=1, source_target_pairs={{0,1},{1,0},{2,3},{3,2},{4,5},{5,4},{6,7},{7,6},{8,9},{9,8},{10,11... | collective-permute-start | bytes 786440 | tf_op jit(solution)/shard_map/ppermute | solution.py:279

commit v2 on v1

v2 whole, which is shorter than its diff:
```python
import jax
import jax.numpy as jnp
from jax import lax
from jax.experimental import pallas as pl
from jax.experimental.pallas import tpu as pltpu
from jax.sharding import Mesh, PartitionSpec as P

HEADS = 8
PAIRS = 4
LANES = 128
F32 = jnp.float32
BF16 = jnp.bfloat16
SMALL = 8 * 1024 * 1024
WHOLE = 65600000
HIGH = 4
STEP = 256


def nn(a, b):
    return lax.dot_general(a, b, (((1,), (0,)), ((), ())), preferred_element_type=F32)


def nt(a, b):
    return lax.dot_general(a, b, (((1,), (1,)), ((), ())), preferred_element_type=F32)


def call(body, ins, outs, scratch=(), flops=0, limit=SMALL):
    place = {"v": pltpu.VMEM, "s": pltpu.SMEM, "h": pltpu.HBM}
    spec = [pl.BlockSpec(memory_space=place[i]) for i in ins]
    shapes = [shape for shape, _ in outs]
    out_spec = [pl.BlockSpec(memory_space=place[i]) for _, i in outs]
    return pl.pallas_call(
        body,
        out_shape=shapes,
        in_specs=spec,
        out_specs=out_spec,
        scratch_shapes=list(scratch),
        compiler_params=pltpu.CompilerParams(vmem_limit_bytes=limit),
        cost_estimate=pl.CostEstimate(flops=flops, bytes_accessed=1 << 20, transcendentals=0),
    )


def start(sems, *pairs):
    copies = [pltpu.make_async_copy(src, dst, sems.at[i]) for i, (src, dst) in enumerate(pairs)]
    for copy in copies:
        copy.start()
    return copies


def pack_kernel(user_hbm, embed_hbm, grad_hbm, out_ref, user_ref, embed_ref, grad_ref, sems):
    copies = start(sems, (user_hbm, user_ref), (embed_hbm, embed_ref), (grad_hbm, grad_ref))
    for copy in copies:
        copy.wait()
    own, width = embed_ref.shape
    row = lax.broadcasted_iota(jnp.int32, (own, own), 0)
    lane = lax.broadcasted_iota(jnp.int32, (own, own), 1)
    user = jnp.broadcast_to(user_ref[...].astype(F32), (own, own))
    user = jnp.sum(jnp.where(row == lane, user, 0.0), axis=1, keepdims=True)
    out_ref[:, :width] = embed_ref[...]
    out_ref[:, width : width + LANES] = jnp.broadcast_to(user, (own, LANES)).astype(BF16)
    out_ref[:, width + LANES :] = grad_ref[...]


def spread_kernel(own_ref, one_ref, two_ref, three_ref, after_hbm, column_ref, plane_ref):
    refs = (own_ref, one_ref, two_ref, three_ref)
    column = jnp.concatenate([r[...].astype(F32) for r in refs], axis=0).astype(BF16)
    column_ref[...] = column
    for i in range(plane_ref.shape[0]):
        plane_ref[i] = column[:, : plane_ref.shape[2]]


def keyval_kernel(length_ref, hist_ref, weight_ref, key_ref, value_ref):
    events = hist_ref.shape[0]
    keyval = nn(hist_ref[...], weight_ref[...])
    row = lax.broadcasted_iota(jnp.int32, (events, LANES), 0)
    lane = lax.broadcasted_iota(jnp.int32, (events, LANES), 1)
    live = row < length_ref[0]
    half = LANES // 2
    for p in range(PAIRS):
        for ref, base in ((key_ref, 0), (value_ref, PAIRS * LANES)):
            part = keyval[:, base + p * LANES : base + (p + 1) * LANES]
            ref[p, :events, :] = jnp.where(live & (lane < half), part, 0.0).astype(BF16)
            ref[p, events:, :] = jnp.where(live & (lane >= half), part, 0.0).astype(BF16)


def forward_kernel(user_ref, pay_ref, weight_ref, key_ref, value_ref, query_ref, att_ref):
    rows, width = query_ref.shape
    pay = pay_ref[...]
    mine = pay[:, width : width + 1].astype(F32) == user_ref[0].astype(F32)
    query = nn(pay[:, :width], weight_ref[...]).astype(BF16).astype(F32)
    query_ref[...] = jnp.where(mine, query * 0.0625, 0.0).astype(BF16)
    for p in range(PAIRS):
        cols = slice(p * LANES, (p + 1) * LANES)
        for r in range(0, rows, STEP):
            r = slice(r, r + STEP)
            u = nt(query_ref[r, cols], key_ref[p])
            w = (u + u * jnp.tanh(u)).astype(BF16)
            att_ref[r, cols] = nn(w, value_ref[p]).astype(BF16)


def own_kernel(pay_ref, unit_ref, out_ref, gate_ref, uslope_ref, dgated_ref):
    width = unit_ref.shape[0]
    pay = pay_ref[...]
    linear = nn(pay[:, :width], unit_ref[...])
    sig = jax.nn.sigmoid(linear)
    gate_ref[...] = (linear * sig).astype(BF16).astype(F32)
    uslope_ref[...] = sig * (1.0 + linear * (1.0 - sig))
    dgated_ref[...] = nt(pay[:, width + LANES :], out_ref[...])


def sum_kernel(part_ref, out_ref):
    own, width = out_ref.shape
    parts = part_ref.shape[0] // own
    total = jnp.sum(part_ref[...].astype(F32).reshape(parts, own, width), axis=0)
    out_ref[...] = total.astype(out_ref.dtype)


def norm_kernel(
    own_ref, one_ref, two_ref, three_ref, gate_ref, dgated_ref, uslope_ref, datt_ref, gated_ref, dunit_ref
):
    own, width = gate_ref.shape
    block = own // HIGH
    att = own_ref[...].astype(F32)
    for k, ref in ((1, one_ref), (2, two_ref), (3, three_ref)):
        part = ref[...].astype(F32)
        att = att + jnp.concatenate([part[(HIGH - k) * block :], part[: (HIGH - k) * block]], axis=0)
    mean = jnp.mean(att, axis=1, keepdims=True)
    centered = att - mean
    inverse = lax.rsqrt(jnp.mean(centered * centered, axis=1, keepdims=True) + 1e-05)
    normed = centered * inverse
    gate = gate_ref[...]
    dgated = dgated_ref[...]
    g = dgated * gate
    datt = inverse * (
        g
        - jnp.mean(g, axis=1, keepdims=True)
        - normed * jnp.mean(g * normed, axis=1, keepdims=True)
    )
    datt = datt.astype(BF16)
    for i in range(datt_ref.shape[0]):
        datt_ref[i] = datt
    gated_ref[...] = (normed * gate)[:block].astype(BF16)
    dunit_ref[...] = (dgated * normed * uslope_ref[...])[:block].astype(BF16)


def output_kernel(embed_ref, grad_ref, gated_ref, dunit_ref, out_ref, unit_ref, result_ref, base_ref):
    result_ref[...] = (embed_ref[...].astype(F32) + nn(gated_ref[...], out_ref[...])).astype(BF16)
    base_ref[...] = grad_ref[...].astype(F32) + nt(dunit_ref[...], unit_ref[...])


def silu_pair(u):
    t = jnp.tanh(u)
    return u + u * t, (1.0 + t) + u * (1.0 - t * t)


def backward_kernel(user_ref, pay_ref, query_ref, datt_ref, key_ref, value_ref, masked_ref, dq_ref):
    rows, width = datt_ref.shape
    mine = pay_ref[...][:, width : width + 1].astype(F32) == user_ref[0].astype(F32)
    masked_ref[...] = jnp.where(mine, datt_ref[...].astype(F32), 0.0).astype(BF16)
    for p in range(PAIRS):
        cols = slice(p * LANES, (p + 1) * LANES)
        for r in range(0, rows, STEP):
            r = slice(r, r + STEP)
            slope = silu_pair(nt(query_ref[r, cols], key_ref[p]))[1]
            ds = (nt(masked_ref[r, cols], value_ref[p]) * slope).astype(BF16)
            dq_ref[r, cols] = nn(ds, key_ref[p]).astype(BF16)


def keyval_grad_kernel(
    core_ref, query_ref, datt_ref, key_ref, value_ref, kvw_ref, mine_ref, other_ref, dkv_ref
):
    events = value_ref.shape[1] // 2
    width = datt_ref.shape[1]
    low = lax.broadcasted_iota(jnp.int32, (events, LANES), 1) < LANES // 2
    for p in range(PAIRS):
        cols = slice(p * LANES, (p + 1) * LANES)
        vcols = slice(width + p * LANES, width + (p + 1) * LANES)
        datt = datt_ref[:, cols]
        query = query_ref[:, cols]
        dks, dvs = [], []
        for r in (slice(0, events), slice(events, 2 * events)):
            weight, slope = silu_pair(nt(key_ref[p, r, :], query))
            ds = (nt(value_ref[p, r, :], datt) * slope).astype(BF16)
            dks.append(nn(ds, query))
            dvs.append(nn(weight.astype(BF16), datt))
        dkv_ref[:, cols] = jnp.where(low, dks[0], dks[1]).astype(BF16)
        dkv_ref[:, vcols] = jnp.where(low, dvs[0], dvs[1]).astype(BF16)
    half = events // 2
    core = core_ref[0]
    mine = pl.ds(pl.multiple_of(core * half, half), half)
    other = pl.ds(pl.multiple_of((1 - core) * half, half), half)
    other_ref[...] = nt(dkv_ref[other, :], kvw_ref[...]).astype(BF16)
    mine_ref[...] = nt(dkv_ref[mine, :], kvw_ref[...])


def add_kernel(one_ref, two_ref, *rest):
    rest[-1][...] = (one_ref[...].astype(F32) + two_ref[...].astype(F32)).astype(BF16)


def final_kernel(own_ref, one_ref, two_ref, three_ref, base_ref, weight_ref, result_ref):
    dq = (own_ref[...] + one_ref[...]) + (two_ref[...] + three_ref[...])
    dq = (dq * 0.0625).astype(BF16)
    result_ref[...] = (base_ref[...] + nt(dq, weight_ref[...])).astype(BF16)


def shards(
    history_embed,
    candidate_embed,
    query_weight,
    unit_weight,
    keyval_weight,
    output_weight,
    block_user,
    block_length,
    candidate_user,
    grad_output,
):
    own, width = candidate_embed.shape
    events = history_embed.shape[0]
    plane = lax.axis_size("plane")
    column = own * HIGH
    rows = column * plane
    s = jax.ShapeDtypeStruct

    def from_up(value, k):
        return lax.ppermute(value, "high", [((i + k) % HIGH, i) for i in range(HIGH)])

    def exchange(value):
        parts = value.reshape(plane, column, value.shape[-1])
        return lax.all_to_all(parts, "plane", 0, 0).reshape(rows, value.shape[-1])

    sems = pltpu.SemaphoreType.DMA
    full = width + LANES + width
    pack = call(
        pack_kernel,
        "hhh",
        [(s((own, full), BF16), "v")],
        [pltpu.VMEM((1, own), jnp.int32), pltpu.VMEM((own, width), BF16), pltpu.VMEM((own, width), BF16), sems((3,))],
        limit=WHOLE,
    )(candidate_user.reshape(1, own), candidate_embed, grad_output)[0]
    wide = (s((PAIRS, 2 * events, LANES), BF16), "v")
    keys, values = call(keyval_kernel, "svv", [wide, wide], flops=1 << 30)(
        block_length, history_embed, keyval_weight
    )
    pay, spread = call(
        spread_kernel,
        "vvvvh",
        [(s((column, full), BF16), "v"), (s((plane, column, width + LANES), BF16), "v")],
    )(pack, *[from_up(pack, k) for k in (1, 2, 3)], keys)
    pay_all = exchange(spread)

    col_f32 = (s((column, width), F32), "v")
    col_b16 = (s((column, width), BF16), "v")
    own_f32 = (s((own, width), F32), "v")
    own_b16 = (s((own, width), BF16), "v")
    big = (s((rows, width), BF16), "v")
    gate, uslope, dgated = call(own_kernel, "vvv", [col_f32] * 3, flops=1 << 26)(
        pay, unit_weight, output_weight
    )
    query, att = call(forward_kernel, "svvvv", [big, big], flops=1 << 31)(
        block_user, pay_all, query_weight, keys, values
    )
    att_all = exchange(att)
    att_col = call(sum_kernel, "v", [col_b16], flops=1 << 20)(att_all)[0]
    datt, gated, dunit = call(
        norm_kernel, "v" * 7, [(s((plane, column, width), BF16), "v"), own_b16, own_b16], flops=1 << 20
    )(att_col, *[from_up(att_col, k) for k in (1, 2, 3)], gate, dgated, uslope)
    datt_all = exchange(datt)
    candidate_output, base = call(output_kernel, "v" * 6, [own_b16, own_f32], flops=1 << 26)(
        candidate_embed, grad_output, gated, dunit, output_weight, unit_weight
    )
    masked, dq = call(backward_kernel, "svvvvv", [big, big], flops=1 << 31)(
        block_user, pay_all, query, datt_all, keys, values
    )
    dq_all = exchange(dq)
    dq_col = call(sum_kernel, "v", [col_f32], flops=1 << 20)(dq_all)[0]
    dq_parts = [
        lax.ppermute(
            dq_col[k * own : (k + 1) * own], "high", [(i, (i + k) % HIGH) for i in range(HIGH)]
        )
        for k in (1, 2, 3)
    ]

    half = events // 2
    core = lax.axis_index("cand") % 2
    half_b16 = (s((half, width), BF16), "v")
    mine, other = call(
        keyval_grad_kernel,
        "svvvvv",
        [(s((half, width), F32), "v"), half_b16],
        [pltpu.VMEM((events, 2 * width), BF16)],
        flops=1 << 32,
    )(core.reshape(1), query, masked, keys, values, keyval_weight)
    swap_core = [(i, i ^ 1) for i in range(4)]
    swap_chip = [(i, i ^ 2) for i in range(4)]
    got = lax.ppermute(other, "cand", swap_core)
    pair = call(add_kernel, "vvh", [half_b16])(mine, got, dq_all)[0]
    got = lax.ppermute(pair, "cand", swap_chip)
    quad = call(add_kernel, "vvhhh", [half_b16])(pair, got, *dq_parts)[0]
    got = lax.ppermute(quad, "cand", swap_core)
    history_grad = jnp.where(
        core == 0,
        jnp.concatenate([quad, got], axis=0),
        jnp.concatenate([got, quad], axis=0),
    )
    candidate_grad = call(final_kernel, "v" * 6, [own_b16], flops=1 << 26)(
        dq_col[:own], *dq_parts, base, query_weight
    )[0]
    return (candidate_output, history_grad, candidate_grad)


def solution(mesh):
    seq, cand = mesh.shape["seq"], mesh.shape["cand"]
    fine = Mesh(mesh.devices.reshape(seq // HIGH, HIGH, cand), ("plane", "high", "cand"))
    hist, full = ("plane", "high"), ("plane", "high", "cand")
    in_specs = (
        P(hist, None),
        P(full, None),
        P(),
        P(),
        P(),
        P(),
        P(hist),
        P(hist),
        P(full),
        P(full, None),
    )
    out_specs = (P(full, None), P(hist, None), P(full, None))
    return jax.shard_map(shards, mesh=fine, in_specs=in_specs, out_specs=out_specs, check_vma=False)
```

time: 157 us -> 121 us (0.77)
  Pallas kernels: 44.2 us -> 18.9 us
  waiting for transfers between devices: 48.2 us -> 29.8 us
  blocking collectives: 0 us -> 12.2 us
  local copies, waits for them, and re-layouts: 14.3 us -> 11.7 us
  other arithmetic: 3.51 us -> 1.01 us
    all_to_all x4 -> x3, starting transfers between devices: 41.2 us -> 14.2 us  [exchange(): return lax.all_to_all(parts, 'plane', 0, 0).reshape(rows, value.shape[-1])]
    pallas_call x9 -> x14, Pallas kernels: 44.2 us -> 18.9 us  [the longest x1 6.04 us: shards(): call(keyval_grad_kernel, 'svvvvv', [(s((half, width), F32), 'v'), half_b1...]
    ppermute x0 -> x9, starting transfers between devices: none -> 20.5 us  [the longest x6 16.5 us: from_up(): lax.ppermute(value, 'high', [((i + k) % HIGH, i) for i in range(HIGH)])]
    ppermute x1, waiting for transfers between devices: 15.7 us -> 0.01 us  [shards(): got = lax.ppermute(pair, 'cand', swap_chip)]
    all_to_all x4 -> x3, waiting for transfers between devices: 32.1 us -> 19.2 us  [exchange(): return lax.all_to_all(parts, 'plane', 0, 0).reshape(rows, value.shape[-1])]
    all_to_all x0 -> x1, blocking collectives: none -> 12.2 us  [exchange(): return lax.all_to_all(parts, 'plane', 0, 0).reshape(rows, value.shape[-1])]
    ppermute x0 -> x9, waiting for transfers between devices: none -> 9.48 us  [the longest x3 4.95 us: shards(): lax.ppermute(dq_col[k * own:(k + 1) * own], 'high', [(i, (i + k) % HIGH)...]
    ppermute x1, starting transfers between devices: 1.7 us -> 6.31 us  [shards(): got = lax.ppermute(other, 'cand', swap_core)]
  transfers between devices with their start and end apart: 7 -> 15, of which waited for: 4 -> 7; matrix products, arithmetic and copies ran while one was open for 1% -> 0% of each run, Pallas kernels for 11% -> 7%
where the time goes in v2:
time: 121 us; the launch traced here: 120 us
  starting transfers between devices  44.3 us (37%)
  waiting for transfers between devices  29.8 us (25%)
  Pallas kernels  18.9 us (16%)
  blocking collectives  12.2 us (10%)
  local copies, waits for them, and re-layouts  11.7 us (10%)
  between operations  2.13 us (2%)
    all_to_all x3, waiting for transfers between devices, exchange(): return lax.all_to_all(parts, 'plane', 0, 0).reshape(rows, value.shape[-1])  19.2 us
    ppermute x6, starting transfers between devices, from_up(): lax.ppermute(value, 'high', [((i + k) % HIGH, i) for i in range(HIGH)])  16.5 us
    all_to_all x3, starting transfers between devices, exchange(): return lax.all_to_all(parts, 'plane', 0, 0).reshape(rows, value.shape[-1])  14.2 us
    all_to_all x1, blocking collectives, exchange(): return lax.all_to_all(parts, 'plane', 0, 0).reshape(rows, value.shape[-1])  12.2 us
    unnamed x38, local copies, waits for them, and re-layouts  11.7 us
    ppermute x1, starting transfers between devices, shards(): got = lax.ppermute(other, 'cand', swap_core)  6.31 us
    pallas_call x1, Pallas kernels, shards(): call(keyval_grad_kernel, 'svvvvv', [(s((half, width), F32), 'v'), half_b1...  6.04 us
    ppermute x3, waiting for transfers between devices, shards(): lax.ppermute(dq_col[k * own:(k + 1) * own], 'high', [(i, (i + k) % HIGH)...  4.95 us
  transfers between devices with their start and end apart: 15, of which 7 were waited for; matrix products, arithmetic and copies ran while one was open for 0% of the time, Pallas kernels for 7%

profile of v2, /device:TPU:1, one launch (start us, length us, event | category | flops | bytes accessed | tf_op | source)
XLA Modules:
  0.0 120.0 jit_solution(2716111646782718462)
XLA Ops:
  0.6 1.4 %shard_map.121.own_ref = bf16[8,1152]{1,0:T(8,128)(2,1)} custom-call(s32[1,8]{1,0:T(1,128)} %bitcast.16, bf16[8,512]{1,0:T(8,128)(2,1)} %embed_ref.1, bf16[8,512]{1,0:T(8,128)(2,1)} %grad_ref.1), custom_call_target="tpu_custom_call" | custom-call | bytes 1048576 | tf_op jit(solution)/shard_map/pallas_call | solution.py:234
  2.1 6.9 %collective-permute-start = (bf16[8,1152]{1,0:T(8,128)(2,1)}, bf16[8,1152]{1,0:T(8,128)(2,1)S(1)}, u32[]{:S(2)}, u32[]{:S(2)}) collective-permute-start(bf16[8,1152]{1,0:T(8,128)(2,1)} %shard_map.121.own_ref), channel_id=1, source_target_pairs={{4,0},{8,4},{12,8},{0,12},{5,1},{9,5},{13,9},{1,13},{6,2},{10,6},{... | collective-permute-start | bytes 55304 | tf_op jit(solution)/shard_map/ppermute | solution.py:226
  10.0 2.3 %collective-permute-start.2 = (bf16[8,1152]{1,0:T(8,128)(2,1)}, bf16[8,1152]{1,0:T(8,128)(2,1)S(1)}, u32[]{:S(2)}, u32[]{:S(2)}) collective-permute-start(bf16[8,1152]{1,0:T(8,128)(2,1)} %shard_map.121.own_ref), channel_id=1, source_target_pairs={{12,0},{0,4},{4,8},{8,12},{13,1},{1,5},{5,9},{9,13},{14,2},{2,6},{... | collective-permute-start | bytes 55304 | tf_op jit(solution)/shard_map/ppermute | solution.py:226
  12.9 1.2 %copy-done.8 = bf16[512,1024]{1,0:T(8,128)(2,1)S(1)} copy-done((bf16[512,1024]{1,0:T(8,128)(2,1)S(1)}, bf16[512,1024]{1,0:T(8,128)(2,1)}, u32[]{:S(2)}) %copy-start.8) | copy-done | bytes 1048600
  14.1 1.0 copy-done.10
  17.0 6.9 %all-to-all-start = ((bf16[16,32,640]{2,1,0:T(8,128)(2,1)}), bf16[16,32,640]{2,1,0:T(8,128)(2,1)S(1)}, u32[]{:S(2)}, u32[]{:S(2)}) async-start(bf16[16,32,640]{2,1,0:T(8,128)(2,1)} %get-tuple-element.22), calls=%async_computation | async-start | bytes 1310720 | tf_op jit(solution)/shard_map/all_to_all | solution.py:230
  24.5 10.4 %all-to-all-done = bf16[16,32,640]{2,1,0:T(8,128)(2,1)S(1)} async-done(((bf16[16,32,640]{2,1,0:T(8,128)(2,1)}), bf16[16,32,640]{2,1,0:T(8,128)(2,1)S(1)}, u32[]{:S(2)}, u32[]{:S(2)}) %all-to-all-start) | async-done | bytes 655392 | tf_op jit(solution)/shard_map/all_to_all | solution.py:230
  34.9 2.7 %shard_map.124 = (bf16[512,512]{1,0:T(8,128)(2,1)S(1)}, bf16[512,512]{1,0:T(8,128)(2,1)S(1)}) custom-call(s32[1]{0:T(128)S(6)} %copy.13.user_ref, bf16[512,640]{1,0:T(8,128)(2,1)S(1)} %bitcast.11, bf16[512,512]{1,0:T(8,128)(2,1)S(1)} %copy-done.2, bf16[4,1024,128]{2,1,0:T(8,128)(2,1)S(1)} %get-tuple-element.21.after_hbm.key_ref, ...), custom_call_target="tpu_custom_call" | custom-call | flops 2147483648 | bytes 1048576 | tf_op jit(solution)/shard_map/pallas_call | solution.py:260
  38.4 12.2 %all_to_all.20 = bf16[16,32,512]{2,1,0:T(8,128)(2,1)S(1)} all-to-all(bf16[16,32,512]{2,1,0:T(8,128)(2,1)S(1)} %bitcast.15), channel_id=1, replica_groups=mesh['plane'=16,'high'=4,'cand'=4] {'plane'}, dimensions={0} | all-to-all | bytes 1048576 | tf_op jit(solution)/shard_map/all_to_all | solution.py:230
  50.7 1.7 %collective-permute-start.3 = (bf16[32,512]{1,0:T(8,128)(2,1)S(1)}, bf16[32,512]{1,0:T(8,128)(2,1)S(1)}, u32[]{:S(2)}, u32[]{:S(2)}) collective-permute-start(bf16[32,512]{1,0:T(8,128)(2,1)S(1)} %shard_map.125.own_ref), channel_id=1, source_target_pairs={{4,0},{8,4},{12,8},{0,12},{5,1},{9,5},{13,9},{1,13},{6,2},{10,6},{... | collective-permute-start | bytes 98312 | tf_op jit(solution)/shard_map/ppermute | solution.py:226
  52.3 4.6 %collective-permute-start.4 = (bf16[32,512]{1,0:T(8,128)(2,1)S(1)}, bf16[32,512]{1,0:T(8,128)(2,1)S(1)}, u32[]{:S(2)}, u32[]{:S(2)}) collective-permute-start(bf16[32,512]{1,0:T(8,128)(2,1)S(1)} %shard_map.125.own_ref), channel_id=1, source_target_pairs={{8,0},{12,4},{0,8},{4,12},{9,1},{13,5},{1,9},{5,13},{10,2},{14,6},... | collective-permute-start | bytes 98312 | tf_op jit(solution)/shard_map/ppermute | solution.py:226
  57.3 1.7 %collective-permute-done.4.two_ref = bf16[32,512]{1,0:T(8,128)(2,1)S(1)} collective-permute-done((bf16[32,512]{1,0:T(8,128)(2,1)S(1)}, bf16[32,512]{1,0:T(8,128)(2,1)S(1)}, u32[]{:S(2)}, u32[]{:S(2)}) %collective-permute-start.4) | collective-permute-done | bytes 32800 | tf_op jit(solution)/shard_map/ppermute | solution.py:226
  59.0 2.8 %collective-permute-done.5.three_ref = bf16[32,512]{1,0:T(8,128)(2,1)S(1)} collective-permute-done((bf16[32,512]{1,0:T(8,128)(2,1)S(1)}, bf16[32,512]{1,0:T(8,128)(2,1)S(1)}, u32[]{:S(2)}, u32[]{:S(2)}) %collective-permute-start.5) | collective-permute-done | bytes 32800 | tf_op jit(solution)/shard_map/ppermute | solution.py:226
  61.9 1.1 shard_map.127
  63.0 3.8 %all-to-all-start.2 = ((bf16[16,32,512]{2,1,0:T(8,128)(2,1)}), bf16[16,32,512]{2,1,0:T(8,128)(2,1)S(1)}, u32[]{:S(2)}, u32[]{:S(2)}) async-start(bf16[16,32,512]{2,1,0:T(8,128)(2,1)} %get-tuple-element.33), calls=%async_computation.2 | async-start | bytes 1048576 | tf_op jit(solution)/shard_map/all_to_all | solution.py:230
  66.7 8.8 %all-to-all-done.2 = bf16[16,32,512]{2,1,0:T(8,128)(2,1)S(1)} async-done(((bf16[16,32,512]{2,1,0:T(8,128)(2,1)}), bf16[16,32,512]{2,1,0:T(8,128)(2,1)S(1)}, u32[]{:S(2)}, u32[]{:S(2)}) %all-to-all-start.2) | async-done | bytes 524320 | tf_op jit(solution)/shard_map/all_to_all | solution.py:230
  75.5 1.2 %copy-done.12 = bf16[4,1024,128]{2,1,0:T(8,128)(2,1)S(1)} copy-done((bf16[4,1024,128]{2,1,0:T(8,128)(2,1)S(1)}, bf16[4,1024,128]{2,1,0:T(8,128)(2,1)}, u32[]{:S(2)}) %copy-start.12) | copy-done | bytes 1048600
  76.7 1.0 copy-done.15
  77.8 3.7 %shard_map.129 = (bf16[512,512]{1,0:T(8,128)(2,1)S(1)}, bf16[512,512]{1,0:T(8,128)(2,1)S(1)}) custom-call(s32[1]{0:T(128)S(6)} %copy.13.user_ref, bf16[512,640]{1,0:T(8,128)(2,1)S(1)} %bitcast.12, bf16[512,512]{1,0:T(8,128)(2,1)S(1)} %copy-done.15, bf16[512,512]{1,0:T(8,128)(2,1)S(1)} %bitcast.13, ...), custom_call_target="tpu_custom_call" | custom-call | flops 2147483648 | bytes 1048576 | tf_op jit(solution)/shard_map/pallas_call | solution.py:272
  83.0 3.6 %all-to-all-start.3 = ((bf16[16,32,512]{2,1,0:T(8,128)(2,1)}), bf16[16,32,512]{2,1,0:T(8,128)(2,1)S(1)}, u32[]{:S(2)}, u32[]{:S(2)}) async-start(bf16[16,32,512]{2,1,0:T(8,128)(2,1)} %bitcast.14), calls=%async_computation.3 | async-start | bytes 1048576 | tf_op jit(solution)/shard_map/all_to_all | solution.py:230
  86.6 1.2 %copy-done.9 = bf16[512,1024]{1,0:T(8,128)(2,1)S(1)} copy-done((bf16[512,1024]{1,0:T(8,128)(2,1)S(1)}, bf16[512,1024]{1,0:T(8,128)(2,1)}, u32[]{:S(2)}) %copy-start.9) | copy-done | bytes 1048600
  87.9 1.2 %copy-done.13 = bf16[4,1024,128]{2,1,0:T(8,128)(2,1)S(1)} copy-done((bf16[4,1024,128]{2,1,0:T(8,128)(2,1)S(1)}, bf16[4,1024,128]{2,1,0:T(8,128)(2,1)}, u32[]{:S(2)}) %copy-start.13) | copy-done | bytes 1048600
  89.1 1.0 copy-done.16
  90.1 1.0 copy-done.18
  91.2 6.0 %shard_map.130 = (f32[256,512]{1,0:T(8,128)S(1)}, bf16[256,512]{1,0:T(8,128)(2,1)S(1)}) custom-call(s32[1]{0:T(128)} %bitcast.4.core_ref, bf16[512,512]{1,0:T(8,128)(2,1)S(1)} %copy-done.16, bf16[512,512]{1,0:T(8,128)(2,1)S(1)} %copy-done.18, bf16[4,1024,128]{2,1,0:T(8,128)(2,1)S(1)} %get-tuple-element.21.after_hbm.key_ref, ...), custom_call_target="tpu_custom_call" | custom-call | flops 4294967296 | bytes 1048576 | tf_op jit(solution)/shard_map/pallas_call | solution.py:287
  97.2 6.3 %collective-permute-start.6 = (bf16[256,512]{1,0:T(8,128)(2,1)S(1)}, bf16[256,512]{1,0:T(8,128)(2,1)S(1)}, u32[]{:S(2)}, u32[]{:S(2)}) collective-permute-start(bf16[256,512]{1,0:T(8,128)(2,1)S(1)} %get-tuple-element.36), channel_id=1, source_target_pairs={{0,1},{1,0},{2,3},{3,2},{4,5},{5,4},{6,7},{7,6},{8,9},{9,8},{10,11... | collective-permute-start | bytes 786440 | tf_op jit(solution)/shard_map/ppermute | solution.py:296
  103.5 1.2 collective-permute-done.6.two_ref
  105.8 2.4 %collective-permute-start.8 = (f32[8,512]{1,0:T(8,128)S(1)}, f32[8,512]{1,0:T(8,128)S(1)}, u32[]{:S(2)}, u32[]{:S(2)}) collective-permute-start(f32[8,512]{1,0:T(8,128)S(1)} %get-tuple-element.42), channel_id=1, source_target_pairs={{0,4},{4,8},{8,12},{12,0},{1,5},{5,9},{9,13},{13,1},{2,6},{6,10},{... | collective-permute-start | bytes 49160 | tf_op jit(solution)/shard_map/ppermute | solution.py:278
  108.1 1.5 %collective-permute-start.9 = (f32[8,512]{1,0:T(8,128)S(1)}, f32[8,512]{1,0:T(8,128)S(1)}, u32[]{:S(2)}, u32[]{:S(2)}) collective-permute-start(f32[8,512]{1,0:T(8,128)S(1)} %get-tuple-element.41), channel_id=1, source_target_pairs={{0,8},{4,12},{8,0},{12,4},{1,9},{5,13},{9,1},{13,5},{2,10},{6,14},... | collective-permute-start | bytes 49160 | tf_op jit(solution)/shard_map/ppermute | solution.py:278
  109.6 1.9 %collective-permute-done.8.rest_0_.one_ref = f32[8,512]{1,0:T(8,128)S(1)} collective-permute-done((f32[8,512]{1,0:T(8,128)S(1)}, f32[8,512]{1,0:T(8,128)S(1)}, u32[]{:S(2)}, u32[]{:S(2)}) %collective-permute-start.8) | collective-permute-done | bytes 16416 | tf_op jit(solution)/shard_map/ppermute | solution.py:278
  111.6 3.0 %collective-permute-done.9.rest_1_.two_ref = f32[8,512]{1,0:T(8,128)S(1)} collective-permute-done((f32[8,512]{1,0:T(8,128)S(1)}, f32[8,512]{1,0:T(8,128)S(1)}, u32[]{:S(2)}, u32[]{:S(2)}) %collective-permute-start.9) | collective-permute-done | bytes 16416 | tf_op jit(solution)/shard_map/ppermute | solution.py:278
  114.7 2.5 %collective-permute-start.11 = (bf16[256,512]{1,0:T(8,128)(2,1)S(1)}, bf16[256,512]{1,0:T(8,128)(2,1)S(1)}, u32[]{:S(2)}, u32[]{:S(2)}) collective-permute-start(bf16[256,512]{1,0:T(8,128)(2,1)S(1)} %shard_map.133), channel_id=1, source_target_pairs={{0,1},{1,0},{2,3},{3,2},{4,5},{5,4},{6,7},{7,6},{8,9},{9,8},{10,11... | collective-permute-start | bytes 786440 | tf_op jit(solution)/shard_map/ppermute | solution.py:300
  (53 shorter events, 9.6 us)
Async XLA Ops:
  2.1 13.9 %collective-permute-start = (bf16[8,1152]{1,0:T(8,128)(2,1)}, bf16[8,1152]{1,0:T(8,128)(2,1)S(1)}, u32[]{:S(2)}, u32[]{:S(2)}) collective-permute-start(bf16[8,1152]{1,0:T(8,128)(2,1)} %shard_map.121.own_ref), channel_id=1, source_target_pairs={{4,0},{8,4},{12,8},{0,12},{5,1},{9,5},{13,9},{1,13},{6,2},{10,6},{... | collective-permute-start | bytes 55304 | tf_op jit(solution)/shard_map/ppermute | solution.py:226
  9.0 7.0 %collective-permute-start.1 = (bf16[8,1152]{1,0:T(8,128)(2,1)}, bf16[8,1152]{1,0:T(8,128)(2,1)S(1)}, u32[]{:S(2)}, u32[]{:S(2)}) collective-permute-start(bf16[8,1152]{1,0:T(8,128)(2,1)} %shard_map.121.own_ref), channel_id=1, source_target_pairs={{8,0},{12,4},{0,8},{4,12},{9,1},{13,5},{1,9},{5,13},{10,2},{14,6},... | collective-permute-start | bytes 55304 | tf_op jit(solution)/shard_map/ppermute | solution.py:226
  10.0 6.0 %collective-permute-start.2 = (bf16[8,1152]{1,0:T(8,128)(2,1)}, bf16[8,1152]{1,0:T(8,128)(2,1)S(1)}, u32[]{:S(2)}, u32[]{:S(2)}) collective-permute-start(bf16[8,1152]{1,0:T(8,128)(2,1)} %shard_map.121.own_ref), channel_id=1, source_target_pairs={{12,0},{0,4},{4,8},{8,12},{13,1},{1,5},{5,9},{9,13},{14,2},{2,6},{... | collective-permute-start | bytes 55304 | tf_op jit(solution)/shard_map/ppermute | solution.py:226
  12.9 1.2 %copy-start.8 = (bf16[512,1024]{1,0:T(8,128)(2,1)S(1)}, bf16[512,1024]{1,0:T(8,128)(2,1)}, u32[]{:S(2)}) copy-start(bf16[512,1024]{1,0:T(8,128)(2,1)} %kvw_ref.1) | copy-start | bytes 3145732
  14.1 1.0 copy-start.10
  15.2 0.8 copy-start.5
  15.9 19.0 %copy-start.11 = (bf16[4,1024,128]{2,1,0:T(8,128)(2,1)}, bf16[4,1024,128]{2,1,0:T(8,128)(2,1)S(1)}, u32[]{:S(2)}) copy-start(bf16[4,1024,128]{2,1,0:T(8,128)(2,1)S(1)} %get-tuple-element.23.value_ref) | copy-start | bytes 3145732
  17.0 17.9 %copy-start.2 = (bf16[512,512]{1,0:T(8,128)(2,1)S(1)}, bf16[512,512]{1,0:T(8,128)(2,1)}, u32[]{:S(2)}) copy-start(bf16[512,512]{1,0:T(8,128)(2,1)} %weight_ref.5) | copy-start | bytes 1572868
  17.0 17.9 %all-to-all-start = ((bf16[16,32,640]{2,1,0:T(8,128)(2,1)}), bf16[16,32,640]{2,1,0:T(8,128)(2,1)S(1)}, u32[]{:S(2)}, u32[]{:S(2)}) async-start(bf16[16,32,640]{2,1,0:T(8,128)(2,1)} %get-tuple-element.22), calls=%async_computation | async-start | bytes 1310720 | tf_op jit(solution)/shard_map/all_to_all | solution.py:230
  37.6 0.8 copy-start.14
  38.4 18.6 %copy-start.1 = (bf16[512,512]{1,0:T(8,128)(2,1)S(1)}, bf16[512,512]{1,0:T(8,128)(2,1)}, u32[]{:S(2)}) copy-start(bf16[512,512]{1,0:T(8,128)(2,1)} %out_ref.3) | copy-start | bytes 1572868
  50.6 6.4 %copy-start = (bf16[512,512]{1,0:T(8,128)(2,1)S(1)}, bf16[512,512]{1,0:T(8,128)(2,1)}, u32[]{:S(2)}) copy-start(bf16[512,512]{1,0:T(8,128)(2,1)} %unit_ref.3) | copy-start | bytes 1572868
  50.7 6.7 %collective-permute-start.3 = (bf16[32,512]{1,0:T(8,128)(2,1)S(1)}, bf16[32,512]{1,0:T(8,128)(2,1)S(1)}, u32[]{:S(2)}, u32[]{:S(2)}) collective-permute-start(bf16[32,512]{1,0:T(8,128)(2,1)S(1)} %shard_map.125.own_ref), channel_id=1, source_target_pairs={{4,0},{8,4},{12,8},{0,12},{5,1},{9,5},{13,9},{1,13},{6,2},{10,6},{... | collective-permute-start | bytes 98312 | tf_op jit(solution)/shard_map/ppermute | solution.py:226
  52.3 6.7 %collective-permute-start.4 = (bf16[32,512]{1,0:T(8,128)(2,1)S(1)}, bf16[32,512]{1,0:T(8,128)(2,1)S(1)}, u32[]{:S(2)}, u32[]{:S(2)}) collective-permute-start(bf16[32,512]{1,0:T(8,128)(2,1)S(1)} %shard_map.125.own_ref), channel_id=1, source_target_pairs={{8,0},{12,4},{0,8},{4,12},{9,1},{13,5},{1,9},{5,13},{10,2},{14,6},... | collective-permute-start | bytes 98312 | tf_op jit(solution)/shard_map/ppermute | solution.py:226
  57.0 4.9 %collective-permute-start.5 = (bf16[32,512]{1,0:T(8,128)(2,1)S(1)}, bf16[32,512]{1,0:T(8,128)(2,1)S(1)}, u32[]{:S(2)}, u32[]{:S(2)}) collective-permute-start(bf16[32,512]{1,0:T(8,128)(2,1)S(1)} %shard_map.125.own_ref), channel_id=1, source_target_pairs={{12,0},{0,4},{4,8},{8,12},{13,1},{1,5},{5,9},{9,13},{14,2},{2,6},{... | collective-permute-start | bytes 98312 | tf_op jit(solution)/shard_map/ppermute | solution.py:226
  63.0 12.5 %all-to-all-start.2 = ((bf16[16,32,512]{2,1,0:T(8,128)(2,1)}), bf16[16,32,512]{2,1,0:T(8,128)(2,1)S(1)}, u32[]{:S(2)}, u32[]{:S(2)}) async-start(bf16[16,32,512]{2,1,0:T(8,128)(2,1)} %get-tuple-element.33), calls=%async_computation.2 | async-start | bytes 1048576 | tf_op jit(solution)/shard_map/all_to_all | solution.py:230
  75.5 1.2 %copy-start.12 = (bf16[4,1024,128]{2,1,0:T(8,128)(2,1)S(1)}, bf16[4,1024,128]{2,1,0:T(8,128)(2,1)}, u32[]{:S(2)}) copy-start(bf16[4,1024,128]{2,1,0:T(8,128)(2,1)} %copy-done.11) | copy-start | bytes 3145732
  76.7 1.0 copy-start.15
  83.0 21.6 %all-to-all-start.3 = ((bf16[16,32,512]{2,1,0:T(8,128)(2,1)}), bf16[16,32,512]{2,1,0:T(8,128)(2,1)S(1)}, u32[]{:S(2)}, u32[]{:S(2)}) async-start(bf16[16,32,512]{2,1,0:T(8,128)(2,1)} %bitcast.14), calls=%async_computation.3 | async-start | bytes 1048576 | tf_op jit(solution)/shard_map/all_to_all | solution.py:230
  86.6 1.2 %copy-start.9 = (bf16[512,1024]{1,0:T(8,128)(2,1)S(1)}, bf16[512,1024]{1,0:T(8,128)(2,1)}, u32[]{:S(2)}) copy-start(bf16[512,1024]{1,0:T(8,128)(2,1)} %kvw_ref.1) | copy-start | bytes 3145732
  87.9 1.2 %copy-start.13 = (bf16[4,1024,128]{2,1,0:T(8,128)(2,1)S(1)}, bf16[4,1024,128]{2,1,0:T(8,128)(2,1)}, u32[]{:S(2)}) copy-start(bf16[4,1024,128]{2,1,0:T(8,128)(2,1)} %copy-done.11) | copy-start | bytes 3145732
  89.1 1.0 copy-start.16
  90.1 1.0 copy-start.18
  97.2 7.5 %collective-permute-start.6 = (bf16[256,512]{1,0:T(8,128)(2,1)S(1)}, bf16[256,512]{1,0:T(8,128)(2,1)S(1)}, u32[]{:S(2)}, u32[]{:S(2)}) collective-permute-start(bf16[256,512]{1,0:T(8,128)(2,1)S(1)} %get-tuple-element.36), channel_id=1, source_target_pairs={{0,1},{1,0},{2,3},{3,2},{4,5},{5,4},{6,7},{7,6},{8,9},{9,8},{10,11... | collective-permute-start | bytes 786440 | tf_op jit(solution)/shard_map/ppermute | solution.py:296
  104.7 9.9 %collective-permute-start.7 = (bf16[256,512]{1,0:T(8,128)(2,1)S(1)}, bf16[256,512]{1,0:T(8,128)(2,1)S(1)}, u32[]{:S(2)}, u32[]{:S(2)}) collective-permute-start(bf16[256,512]{1,0:T(8,128)(2,1)S(1)} %shard_map.131.one_ref), channel_id=1, source_target_pairs={{0,2},{1,3},{2,0},{3,1},{4,6},{5,7},{6,4},{7,5},{8,10},{9,11},{10,... | collective-permute-start | bytes 786440 | tf_op jit(solution)/shard_map/ppermute | solution.py:298
  105.7 4.0 %collective-permute-start.10 = (f32[8,512]{1,0:T(8,128)S(1)}, f32[8,512]{1,0:T(8,128)S(1)}, u32[]{:S(2)}, u32[]{:S(2)}) collective-permute-start(f32[8,512]{1,0:T(8,128)S(1)} %get-tuple-element.40), channel_id=1, source_target_pairs={{0,12},{4,0},{8,4},{12,8},{1,13},{5,1},{9,5},{13,9},{2,14},{6,2},{... | collective-permute-start | bytes 49160 | tf_op jit(solution)/shard_map/ppermute | solution.py:278
  105.8 5.8 %collective-permute-start.8 = (f32[8,512]{1,0:T(8,128)S(1)}, f32[8,512]{1,0:T(8,128)S(1)}, u32[]{:S(2)}, u32[]{:S(2)}) collective-permute-start(f32[8,512]{1,0:T(8,128)S(1)} %get-tuple-element.42), channel_id=1, source_target_pairs={{0,4},{4,8},{8,12},{12,0},{1,5},{5,9},{9,13},{13,1},{2,6},{6,10},{... | collective-permute-start | bytes 49160 | tf_op jit(solution)/shard_map/ppermute | solution.py:278
  108.1 6.5 %collective-permute-start.9 = (f32[8,512]{1,0:T(8,128)S(1)}, f32[8,512]{1,0:T(8,128)S(1)}, u32[]{:S(2)}, u32[]{:S(2)}) collective-permute-start(f32[8,512]{1,0:T(8,128)S(1)} %get-tuple-element.41), channel_id=1, source_target_pairs={{0,8},{4,12},{8,0},{12,4},{1,9},{5,13},{9,1},{13,5},{2,10},{6,14},... | collective-permute-start | bytes 49160 | tf_op jit(solution)/shard_map/ppermute | solution.py:278
  114.6 2.5 %copy-start.6 = (bf16[8,512]{1,0:T(8,128)(2,1)S(1)}, bf16[8,512]{1,0:T(8,128)(2,1)}, u32[]{:S(2)}) copy-start(bf16[8,512]{1,0:T(8,128)(2,1)} %embed_ref.1) | copy-start | bytes 24580
  114.6 2.5 %copy-start.7 = (bf16[8,512]{1,0:T(8,128)(2,1)S(1)}, bf16[8,512]{1,0:T(8,128)(2,1)}, u32[]{:S(2)}) copy-start(bf16[8,512]{1,0:T(8,128)(2,1)} %grad_ref.1) | copy-start | bytes 24580
  114.7 4.4 %collective-permute-start.11 = (bf16[256,512]{1,0:T(8,128)(2,1)S(1)}, bf16[256,512]{1,0:T(8,128)(2,1)S(1)}, u32[]{:S(2)}, u32[]{:S(2)}) collective-permute-start(bf16[256,512]{1,0:T(8,128)(2,1)S(1)} %shard_map.133), channel_id=1, source_target_pairs={{0,1},{1,0},{2,3},{3,2},{4,5},{5,4},{6,7},{7,6},{8,9},{9,8},{10,11... | collective-permute-start | bytes 786440 | tf_op jit(solution)/shard_map/ppermute | solution.py:300
  117.1 1.0 copy-start.3
  (2 other events, 1.6 us)

commit v3 on v2

--- a/solution.py
+++ b/solution.py
@@ -10,7 +10,7 @@
 LANES = 128
 F32 = jnp.float32
 BF16 = jnp.bfloat16
-SMALL = 8 * 1024 * 1024
+SMALL = 16 * 1024 * 1024
 WHOLE = 65600000
 HIGH = 4
 STEP = 256
@@ -61,7 +61,8 @@
     out_ref[:, width + LANES :] = grad_ref[...]
 
 
-def spread_kernel(own_ref, one_ref, two_ref, three_ref, after_hbm, column_ref, plane_ref):
+def spread_kernel(own_ref, one_ref, two_ref, three_ref, *rest):
+    column_ref, plane_ref = rest[-2:]
     refs = (own_ref, one_ref, two_ref, three_ref)
     column = jnp.concatenate([r[...].astype(F32) for r in refs], axis=0).astype(BF16)
     column_ref[...] = column
@@ -153,36 +154,29 @@
     return u + u * t, (1.0 + t) + u * (1.0 - t * t)
 
 
-def backward_kernel(user_ref, pay_ref, query_ref, datt_ref, key_ref, value_ref, masked_ref, dq_ref):
-    rows, width = datt_ref.shape
-    mine = pay_ref[...][:, width : width + 1].astype(F32) == user_ref[0].astype(F32)
-    masked_ref[...] = jnp.where(mine, datt_ref[...].astype(F32), 0.0).astype(BF16)
-    for p in range(PAIRS):
-        cols = slice(p * LANES, (p + 1) * LANES)
-        for r in range(0, rows, STEP):
-            r = slice(r, r + STEP)
-            slope = silu_pair(nt(query_ref[r, cols], key_ref[p]))[1]
-            ds = (nt(masked_ref[r, cols], value_ref[p]) * slope).astype(BF16)
-            dq_ref[r, cols] = nn(ds, key_ref[p]).astype(BF16)
-
-
-def keyval_grad_kernel(
-    core_ref, query_ref, datt_ref, key_ref, value_ref, kvw_ref, mine_ref, other_ref, dkv_ref
+def backward_kernel(
+    user_ref, core_ref, pay_ref, query_ref, datt_ref, key_ref, value_ref, kvw_ref,
+    dq_ref, mine_ref, other_ref, masked_ref, dkv_ref,
 ):
+    width = datt_ref.shape[1]
     events = value_ref.shape[1] // 2
-    width = datt_ref.shape[1]
+    owned = pay_ref[...][:, width : width + 1].astype(F32) == user_ref[0].astype(F32)
+    masked_ref[...] = jnp.where(owned, datt_ref[...].astype(F32), 0.0).astype(BF16)
     low = lax.broadcasted_iota(jnp.int32, (events, LANES), 1) < LANES // 2
     for p in range(PAIRS):
         cols = slice(p * LANES, (p + 1) * LANES)
         vcols = slice(width + p * LANES, width + (p + 1) * LANES)
-        datt = datt_ref[:, cols]
+        datt = masked_ref[:, cols]
         query = query_ref[:, cols]
-        dks, dvs = [], []
+        dks, dvs, dqs = [], [], []
         for r in (slice(0, events), slice(events, 2 * events)):
-            weight, slope = silu_pair(nt(key_ref[p, r, :], query))
+            key = key_ref[p, r, :]
+            weight, slope = silu_pair(nt(key, query))
             ds = (nt(value_ref[p, r, :], datt) * slope).astype(BF16)
             dks.append(nn(ds, query))
             dvs.append(nn(weight.astype(BF16), datt))
+            dqs.append(nn(key.T, ds))
+        dq_ref[:, cols] = (dqs[0] + dqs[1]).T.astype(BF16)
         dkv_ref[:, cols] = jnp.where(low, dks[0], dks[1]).astype(BF16)
         dkv_ref[:, vcols] = jnp.where(low, dvs[0], dvs[1]).astype(BF16)
     half = events // 2
@@ -195,6 +189,15 @@
 
 def add_kernel(one_ref, two_ref, *rest):
     rest[-1][...] = (one_ref[...].astype(F32) + two_ref[...].astype(F32)).astype(BF16)
+
+
+def halves_kernel(core_ref, mine_ref, other_ref, out_hbm, sems):
+    half = mine_ref.shape[0]
+    core = core_ref[0]
+    mine = out_hbm.at[pl.ds(pl.multiple_of(core * half, half), half)]
+    other = out_hbm.at[pl.ds(pl.multiple_of((1 - core) * half, half), half)]
+    for copy in start(sems, (mine_ref, mine), (other_ref, other)):
+        copy.wait()
 
 
 def final_kernel(own_ref, one_ref, two_ref, three_ref, base_ref, weight_ref, result_ref):
@@ -242,11 +245,12 @@
     keys, values = call(keyval_kernel, "svv", [wide, wide], flops=1 << 30)(
         block_length, history_embed, keyval_weight
     )
+    core = (lax.axis_index("cand") & 1).reshape(1)
     pay, spread = call(
         spread_kernel,
-        "vvvvh",
+        "vvvvhss",
         [(s((column, full), BF16), "v"), (s((plane, column, width + LANES), BF16), "v")],
-    )(pack, *[from_up(pack, k) for k in (1, 2, 3)], keys)
+    )(pack, *[from_up(pack, k) for k in (1, 2, 3)], keys, block_user, core)
     pay_all = exchange(spread)
 
     col_f32 = (s((column, width), F32), "v")
@@ -269,9 +273,15 @@
     candidate_output, base = call(output_kernel, "v" * 6, [own_b16, own_f32], flops=1 << 26)(
         candidate_embed, grad_output, gated, dunit, output_weight, unit_weight
     )
-    masked, dq = call(backward_kernel, "svvvvv", [big, big], flops=1 << 31)(
-        block_user, pay_all, query, datt_all, keys, values
-    )
+    half = events // 2
+    half_b16 = (s((half, width), BF16), "v")
+    dq, mine, other = call(
+        backward_kernel,
+        "ssvvvvvv",
+        [big, (s((half, width), F32), "v"), half_b16],
+        [pltpu.VMEM((rows, width), BF16), pltpu.VMEM((events, 2 * width), BF16)],
+        flops=1 << 32,
+    )(block_user, core, pay_all, query, datt_all, keys, values, keyval_weight)
     dq_all = exchange(dq)
     dq_col = call(sum_kernel, "v", [col_f32], flops=1 << 20)(dq_all)[0]
     dq_parts = [
@@ -281,28 +291,16 @@
         for k in (1, 2, 3)
     ]
 
-    half = events // 2
-    core = lax.axis_index("cand") % 2
-    half_b16 = (s((half, width), BF16), "v")
-    mine, other = call(
-        keyval_grad_kernel,
-        "svvvvv",
-        [(s((half, width), F32), "v"), half_b16],
-        [pltpu.VMEM((events, 2 * width), BF16)],
-        flops=1 << 32,
-    )(core.reshape(1), query, masked, keys, values, keyval_weight)
     swap_core = [(i, i ^ 1) for i in range(4)]
     swap_chip = [(i, i ^ 2) for i in range(4)]
     got = lax.ppermute(other, "cand", swap_core)
-    pair = call(add_kernel, "vvh", [half_b16])(mine, got, dq_all)[0]
+    pair = call(add_kernel, "vv", [half_b16])(mine, got)[0]
     got = lax.ppermute(pair, "cand", swap_chip)
-    quad = call(add_kernel, "vvhhh", [half_b16])(pair, got, *dq_parts)[0]
+    quad = call(add_kernel, "vv", [half_b16])(pair, got)[0]
     got = lax.ppermute(quad, "cand", swap_core)
-    history_grad = jnp.where(
-        core == 0,
-        jnp.concatenate([quad, got], axis=0),
-        jnp.concatenate([got, quad], axis=0),
-    )
+    history_grad = call(halves_kernel, "svv", [(s((events, width), BF16), "h")], [sems((2,))])(
+        core, quad, got
+    )[0]
     candidate_grad = call(final_kernel, "v" * 6, [own_b16], flops=1 << 26)(
         dq_col[:own], *dq_parts, base, query_weight
     )[0]

time: 121 us -> 113 us (0.934)
  blocking collectives: 12.2 us -> 41.6 us
  waiting for transfers between devices: 29.8 us -> 16.2 us
  starting transfers between devices: 44.3 us -> 32.5 us
  local copies, waits for them, and re-layouts: 11.7 us -> 3.28 us
  Pallas kernels: 18.9 us -> 15.7 us
    all_to_all x1 -> x3, blocking collectives: 12.2 us -> 41.6 us  [exchange(): return lax.all_to_all(parts, 'plane', 0, 0).reshape(rows, value.shape[-1])]
    all_to_all x3 -> x1, waiting for transfers between devices: 19.2 us -> 2.34 us  [exchange(): return lax.all_to_all(parts, 'plane', 0, 0).reshape(rows, value.shape[-1])]
    all_to_all x3 -> x1, starting transfers between devices: 14.2 us -> 3.57 us  [exchange(): return lax.all_to_all(parts, 'plane', 0, 0).reshape(rows, value.shape[-1])]
    unnamed x38 -> x22, local copies, waits for them, and re-layouts: 11.7 us -> 3.27 us
    ppermute x1, waiting for transfers between devices: 0.01 us -> 7.21 us  [shards(): got = lax.ppermute(pair, 'cand', swap_chip)]
    ppermute x3, waiting for transfers between devices: 4.95 us -> 2.18 us  [shards(): lax.ppermute(dq_col[k * own:(k + 1) * own], 'high', [(i, (i + k) % HIGH)...]
    pallas_call x5, Pallas kernels: 10.8 us -> 8.4 us  [the longest x1 7.43 us: shards(): call(backward_kernel, 'ssvvvvvv', [big, (s((half, width), F32), 'v'), hal...]
    ppermute x1, starting transfers between devices: 2.45 us -> 0.87 us  [shards(): got = lax.ppermute(quad, 'cand', swap_core)]
  transfers between devices with their start and end apart: 15 -> 13, of which waited for: 7 -> 6; matrix products, arithmetic and copies ran while one was open for 0% -> 0% of each run, Pallas kernels for 7% -> 3%
where the time goes in v3:
time: 113 us; the launch traced here: 112 us
  blocking collectives  41.6 us (37%)
  starting transfers between devices  32.5 us (29%)
  waiting for transfers between devices  16.2 us (14%)
  Pallas kernels  15.7 us (14%)
  local copies, waits for them, and re-layouts  3.28 us (3%)
  between operations  2.29 us (2%)
    all_to_all x3, blocking collectives, exchange(): return lax.all_to_all(parts, 'plane', 0, 0).reshape(rows, value.shape[-1])  41.6 us
    ppermute x6, starting transfers between devices, from_up(): lax.ppermute(value, 'high', [((i + k) % HIGH, i) for i in range(HIGH)])  16 us
    pallas_call x1, Pallas kernels, shards(): call(backward_kernel, 'ssvvvvvv', [big, (s((half, width), F32), 'v'), hal...  7.43 us
    ppermute x1, waiting for transfers between devices, shards(): got = lax.ppermute(pair, 'cand', swap_chip)  7.21 us
    ppermute x1, starting transfers between devices, shards(): got = lax.ppermute(other, 'cand', swap_core)  7.2 us
    ppermute x6, waiting for transfers between devices, from_up(): lax.ppermute(value, 'high', [((i + k) % HIGH, i) for i in range(HIGH)])  4.51 us
    ppermute x3, starting transfers between devices, shards(): lax.ppermute(dq_col[k * own:(k + 1) * own], 'high', [(i, (i + k) % HIGH)...  4.1 us
    all_to_all x1, starting transfers between devices, exchange(): return lax.all_to_all(parts, 'plane', 0, 0).reshape(rows, value.shape[-1])  3.57 us
  transfers between devices with their start and end apart: 13, of which 6 were waited for; matrix products, arithmetic and copies ran while one was open for 0% of the time, Pallas kernels for 3%

profile of v3, /device:TPU:1, one launch (start us, length us, event | category | flops | bytes accessed | tf_op | source)
XLA Modules:
  0.0 111.6 jit_solution(1502609738904068725)
XLA Ops:
  0.6 1.4 %shard_map.121.own_ref = bf16[8,1152]{1,0:T(8,128)(2,1)} custom-call(s32[1,8]{1,0:T(1,128)} %bitcast.14, bf16[8,512]{1,0:T(8,128)(2,1)} %embed_ref.1, bf16[8,512]{1,0:T(8,128)(2,1)} %grad_ref.1), custom_call_target="tpu_custom_call" | custom-call | bytes 1048576 | tf_op jit(solution)/shard_map/pallas_call | solution.py:237
  2.1 6.9 %collective-permute-start = (bf16[8,1152]{1,0:T(8,128)(2,1)}, bf16[8,1152]{1,0:T(8,128)(2,1)S(1)}, u32[]{:S(2)}, u32[]{:S(2)}) collective-permute-start(bf16[8,1152]{1,0:T(8,128)(2,1)} %shard_map.121.own_ref), channel_id=1, source_target_pairs={{4,0},{8,4},{12,8},{0,12},{5,1},{9,5},{13,9},{1,13},{6,2},{10,6},{... | collective-permute-start | bytes 55304 | tf_op jit(solution)/shard_map/ppermute | solution.py:229
  9.0 1.0 collective-permute-start.1
  10.0 2.3 %collective-permute-start.2 = (bf16[8,1152]{1,0:T(8,128)(2,1)}, bf16[8,1152]{1,0:T(8,128)(2,1)S(1)}, u32[]{:S(2)}, u32[]{:S(2)}) collective-permute-start(bf16[8,1152]{1,0:T(8,128)(2,1)} %shard_map.121.own_ref), channel_id=1, source_target_pairs={{12,0},{0,4},{4,8},{8,12},{13,1},{1,5},{5,9},{9,13},{14,2},{2,6},{... | collective-permute-start | bytes 55304 | tf_op jit(solution)/shard_map/ppermute | solution.py:229
  12.9 1.2 %copy-done.6 = bf16[512,1024]{1,0:T(8,128)(2,1)S(1)} copy-done((bf16[512,1024]{1,0:T(8,128)(2,1)S(1)}, bf16[512,1024]{1,0:T(8,128)(2,1)}, u32[]{:S(2)}) %copy-start.6) | copy-done | bytes 1048600
  14.1 1.0 copy-done.8
  15.2 0.8 shard_map.122
  16.0 1.0 copy-done.9
  17.7 17.9 %all_to_all.20 = bf16[16,32,640]{2,1,0:T(8,128)(2,1)S(1)} all-to-all(bf16[16,32,640]{2,1,0:T(8,128)(2,1)S(1)} %get-tuple-element.21), channel_id=1, replica_groups=mesh['plane'=16,'high'=4,'cand'=4] {'plane'}, dimensions={0} | all-to-all | bytes 1310720 | tf_op jit(solution)/shard_map/all_to_all | solution.py:233
  35.7 2.7 %shard_map.124 = (bf16[512,512]{1,0:T(8,128)(2,1)S(1)}, bf16[512,512]{1,0:T(8,128)(2,1)S(1)}) custom-call(s32[1]{0:T(128)S(6)} %copy.13.rest_1_.user_ref, bf16[512,640]{1,0:T(8,128)(2,1)S(1)} %bitcast.10, bf16[512,512]{1,0:T(8,128)(2,1)S(1)} %copy-done.2, bf16[4,1024,128]{2,1,0:T(8,128)(2,1)S(1)} %get-tuple-element.20.rest_0_.key_ref, ...), custom_call_target="tpu_custom_call" | custom-call | flops 2147483648 | bytes 1048576 | tf_op jit(solution)/shard_map/pallas_call | solution.py:264
  38.3 12.0 %all_to_all.21 = bf16[16,32,512]{2,1,0:T(8,128)(2,1)S(1)} all-to-all(bf16[16,32,512]{2,1,0:T(8,128)(2,1)S(1)} %bitcast.13), channel_id=1, replica_groups=mesh['plane'=16,'high'=4,'cand'=4] {'plane'}, dimensions={0} | all-to-all | bytes 1048576 | tf_op jit(solution)/shard_map/all_to_all | solution.py:233
  50.4 1.4 %collective-permute-start.3 = (bf16[32,512]{1,0:T(8,128)(2,1)S(1)}, bf16[32,512]{1,0:T(8,128)(2,1)S(1)}, u32[]{:S(2)}, u32[]{:S(2)}) collective-permute-start(bf16[32,512]{1,0:T(8,128)(2,1)S(1)} %shard_map.125.own_ref), channel_id=1, source_target_pairs={{4,0},{8,4},{12,8},{0,12},{5,1},{9,5},{13,9},{1,13},{6,2},{10,6},{... | collective-permute-start | bytes 98312 | tf_op jit(solution)/shard_map/ppermute | solution.py:229
  51.8 4.4 %collective-permute-start.4 = (bf16[32,512]{1,0:T(8,128)(2,1)S(1)}, bf16[32,512]{1,0:T(8,128)(2,1)S(1)}, u32[]{:S(2)}, u32[]{:S(2)}) collective-permute-start(bf16[32,512]{1,0:T(8,128)(2,1)S(1)} %shard_map.125.own_ref), channel_id=1, source_target_pairs={{8,0},{12,4},{0,8},{4,12},{9,1},{13,5},{1,9},{5,13},{10,2},{14,6},... | collective-permute-start | bytes 98312 | tf_op jit(solution)/shard_map/ppermute | solution.py:229
  56.2 0.3 shard_map.126
  56.6 2.3 %collective-permute-done.4.two_ref = bf16[32,512]{1,0:T(8,128)(2,1)S(1)} collective-permute-done((bf16[32,512]{1,0:T(8,128)(2,1)S(1)}, bf16[32,512]{1,0:T(8,128)(2,1)S(1)}, u32[]{:S(2)}, u32[]{:S(2)}) %collective-permute-start.4) | collective-permute-done | bytes 32800 | tf_op jit(solution)/shard_map/ppermute | solution.py:229
  58.9 2.2 %collective-permute-done.5.three_ref = bf16[32,512]{1,0:T(8,128)(2,1)S(1)} collective-permute-done((bf16[32,512]{1,0:T(8,128)(2,1)S(1)}, bf16[32,512]{1,0:T(8,128)(2,1)S(1)}, u32[]{:S(2)}, u32[]{:S(2)}) %collective-permute-start.5) | collective-permute-done | bytes 32800 | tf_op jit(solution)/shard_map/ppermute | solution.py:229
  61.4 11.7 %all_to_all.22 = bf16[16,32,512]{2,1,0:T(8,128)(2,1)S(1)} all-to-all(bf16[16,32,512]{2,1,0:T(8,128)(2,1)S(1)} %get-tuple-element.32), channel_id=1, replica_groups=mesh['plane'=16,'high'=4,'cand'=4] {'plane'}, dimensions={0} | all-to-all | bytes 1048576 | tf_op jit(solution)/shard_map/all_to_all | solution.py:233
  73.0 7.4 %shard_map.129 = (bf16[512,512]{1,0:T(8,128)(2,1)}, f32[256,512]{1,0:T(8,128)S(1)}, bf16[256,512]{1,0:T(8,128)(2,1)S(1)}) custom-call(s32[1]{0:T(128)S(6)} %copy.13.rest_1_.user_ref, s32[1]{0:T(128)} %bitcast.1.rest_2_.core_ref, bf16[512,640]{1,0:T(8,128)(2,1)S(1)} %bitcast.11, bf16[512,512]{1,0:T(8,128)(2,1)S(1)} %get-tuple-element.31.query_ref, ...), custom_call_target="tpu_custom_call" | custom-call | flops 4294967296 | bytes 1048576 | tf_op jit(solution)/shard_map/pallas_call | solution.py:278
  80.5 7.2 %collective-permute-start.6 = (bf16[256,512]{1,0:T(8,128)(2,1)S(1)}, bf16[256,512]{1,0:T(8,128)(2,1)S(1)}, u32[]{:S(2)}, u32[]{:S(2)}) collective-permute-start(bf16[256,512]{1,0:T(8,128)(2,1)S(1)} %get-tuple-element.34), channel_id=1, source_target_pairs={{0,1},{1,0},{2,3},{3,2},{4,5},{5,4},{6,7},{7,6},{8,9},{9,8},{10,11... | collective-permute-start | bytes 786440 | tf_op jit(solution)/shard_map/ppermute | solution.py:296
  87.7 3.6 %all-to-all-start.3 = ((bf16[16,32,512]{2,1,0:T(8,128)(2,1)}), bf16[16,32,512]{2,1,0:T(8,128)(2,1)S(1)}, u32[]{:S(2)}, u32[]{:S(2)}) async-start(bf16[16,32,512]{2,1,0:T(8,128)(2,1)} %bitcast.6), calls=%async_computation.3 | async-start | bytes 1048576 | tf_op jit(solution)/shard_map/all_to_all | solution.py:233
  91.3 0.8 collective-permute-start.7
  92.1 7.2 %collective-permute-done.7.two_ref = bf16[256,512]{1,0:T(8,128)(2,1)S(1)} collective-permute-done((bf16[256,512]{1,0:T(8,128)(2,1)S(1)}, bf16[256,512]{1,0:T(8,128)(2,1)S(1)}, u32[]{:S(2)}, u32[]{:S(2)}) %collective-permute-start.7) | collective-permute-done | bytes 262176 | tf_op jit(solution)/shard_map/ppermute | solution.py:298
  99.4 0.9 collective-permute-start.8
  100.3 2.3 %all-to-all-done.3 = bf16[16,32,512]{2,1,0:T(8,128)(2,1)S(1)} async-done(((bf16[16,32,512]{2,1,0:T(8,128)(2,1)}), bf16[16,32,512]{2,1,0:T(8,128)(2,1)S(1)}, u32[]{:S(2)}, u32[]{:S(2)}) %all-to-all-start.3) | async-done | bytes 524320 | tf_op jit(solution)/shard_map/all_to_all | solution.py:233
  102.7 1.7 %collective-permute-start.10 = (f32[8,512]{1,0:T(8,128)S(1)}, f32[8,512]{1,0:T(8,128)S(1)}, u32[]{:S(2)}, u32[]{:S(2)}) collective-permute-start(f32[8,512]{1,0:T(8,128)S(1)} %get-tuple-element.38), channel_id=1, source_target_pairs={{0,8},{4,12},{8,0},{12,4},{1,9},{5,13},{9,1},{13,5},{2,10},{6,14},... | collective-permute-start | bytes 49160 | tf_op jit(solution)/shard_map/ppermute | solution.py:288
  104.5 0.6 collective-permute-start.11
  105.1 1.7 %collective-permute-start.9 = (f32[8,512]{1,0:T(8,128)S(1)}, f32[8,512]{1,0:T(8,128)S(1)}, u32[]{:S(2)}, u32[]{:S(2)}) collective-permute-start(f32[8,512]{1,0:T(8,128)S(1)} %get-tuple-element.39), channel_id=1, source_target_pairs={{0,4},{4,8},{8,12},{12,0},{1,5},{5,9},{9,13},{13,1},{2,6},{6,10},{... | collective-permute-start | bytes 49160 | tf_op jit(solution)/shard_map/ppermute | solution.py:288
  106.8 0.8 shard_map.128
  107.6 1.7 %collective-permute-done.10.two_ref = f32[8,512]{1,0:T(8,128)S(1)} collective-permute-done((f32[8,512]{1,0:T(8,128)S(1)}, f32[8,512]{1,0:T(8,128)S(1)}, u32[]{:S(2)}, u32[]{:S(2)}) %collective-permute-start.10) | collective-permute-done | bytes 16416 | tf_op jit(solution)/shard_map/ppermute | solution.py:288
  109.3 0.5 collective-permute-done.9.one_ref
  109.8 0.9 shard_map.134
  110.7 0.8 shard_map.132
  (34 shorter events, 0.7 us)
Async XLA Ops:
  2.1 15.5 %collective-permute-start = (bf16[8,1152]{1,0:T(8,128)(2,1)}, bf16[8,1152]{1,0:T(8,128)(2,1)S(1)}, u32[]{:S(2)}, u32[]{:S(2)}) collective-permute-start(bf16[8,1152]{1,0:T(8,128)(2,1)} %shard_map.121.own_ref), channel_id=1, source_target_pairs={{4,0},{8,4},{12,8},{0,12},{5,1},{9,5},{13,9},{1,13},{6,2},{10,6},{... | collective-permute-start | bytes 55304 | tf_op jit(solution)/shard_map/ppermute | solution.py:229
  9.0 8.6 %collective-permute-start.1 = (bf16[8,1152]{1,0:T(8,128)(2,1)}, bf16[8,1152]{1,0:T(8,128)(2,1)S(1)}, u32[]{:S(2)}, u32[]{:S(2)}) collective-permute-start(bf16[8,1152]{1,0:T(8,128)(2,1)} %shard_map.121.own_ref), channel_id=1, source_target_pairs={{8,0},{12,4},{0,8},{4,12},{9,1},{13,5},{1,9},{5,13},{10,2},{14,6},... | collective-permute-start | bytes 55304 | tf_op jit(solution)/shard_map/ppermute | solution.py:229
  10.0 7.6 %collective-permute-start.2 = (bf16[8,1152]{1,0:T(8,128)(2,1)}, bf16[8,1152]{1,0:T(8,128)(2,1)S(1)}, u32[]{:S(2)}, u32[]{:S(2)}) collective-permute-start(bf16[8,1152]{1,0:T(8,128)(2,1)} %shard_map.121.own_ref), channel_id=1, source_target_pairs={{12,0},{0,4},{4,8},{8,12},{13,1},{1,5},{5,9},{9,13},{14,2},{2,6},{... | collective-permute-start | bytes 55304 | tf_op jit(solution)/shard_map/ppermute | solution.py:229
  12.9 1.2 %copy-start.6 = (bf16[512,1024]{1,0:T(8,128)(2,1)S(1)}, bf16[512,1024]{1,0:T(8,128)(2,1)}, u32[]{:S(2)}) copy-start(bf16[512,1024]{1,0:T(8,128)(2,1)} %kvw_ref.1) | copy-start | bytes 3145732
  14.1 1.0 copy-start.8
  15.2 2.4 %copy-start.3 = (bf16[8,1152]{1,0:T(8,128)(2,1)S(1)}, bf16[8,1152]{1,0:T(8,128)(2,1)}, u32[]{:S(2)}) copy-start(bf16[8,1152]{1,0:T(8,128)(2,1)} %shard_map.121.own_ref) | copy-start | bytes 55300
  15.9 1.0 copy-start.9
  17.6 18.0 %copy-start.10 = (bf16[4,1024,128]{2,1,0:T(8,128)(2,1)S(1)}, bf16[4,1024,128]{2,1,0:T(8,128)(2,1)}, u32[]{:S(2)}) copy-start(bf16[4,1024,128]{2,1,0:T(8,128)(2,1)} %copy-done.9) | copy-start | bytes 3145732
  17.7 18.0 %copy-start.2 = (bf16[512,512]{1,0:T(8,128)(2,1)S(1)}, bf16[512,512]{1,0:T(8,128)(2,1)}, u32[]{:S(2)}) copy-start(bf16[512,512]{1,0:T(8,128)(2,1)} %weight_ref.5) | copy-start | bytes 1572868
  38.3 17.9 %copy-start.1 = (bf16[512,512]{1,0:T(8,128)(2,1)S(1)}, bf16[512,512]{1,0:T(8,128)(2,1)}, u32[]{:S(2)}) copy-start(bf16[512,512]{1,0:T(8,128)(2,1)} %out_ref.3) | copy-start | bytes 1572868
  50.3 5.9 %copy-start = (bf16[512,512]{1,0:T(8,128)(2,1)S(1)}, bf16[512,512]{1,0:T(8,128)(2,1)}, u32[]{:S(2)}) copy-start(bf16[512,512]{1,0:T(8,128)(2,1)} %unit_ref.3) | copy-start | bytes 1572868
  50.4 6.1 %collective-permute-start.3 = (bf16[32,512]{1,0:T(8,128)(2,1)S(1)}, bf16[32,512]{1,0:T(8,128)(2,1)S(1)}, u32[]{:S(2)}, u32[]{:S(2)}) collective-permute-start(bf16[32,512]{1,0:T(8,128)(2,1)S(1)} %shard_map.125.own_ref), channel_id=1, source_target_pairs={{4,0},{8,4},{12,8},{0,12},{5,1},{9,5},{13,9},{1,13},{6,2},{10,6},{... | collective-permute-start | bytes 98312 | tf_op jit(solution)/shard_map/ppermute | solution.py:229
  51.8 7.0 %collective-permute-start.4 = (bf16[32,512]{1,0:T(8,128)(2,1)S(1)}, bf16[32,512]{1,0:T(8,128)(2,1)S(1)}, u32[]{:S(2)}, u32[]{:S(2)}) collective-permute-start(bf16[32,512]{1,0:T(8,128)(2,1)S(1)} %shard_map.125.own_ref), channel_id=1, source_target_pairs={{8,0},{12,4},{0,8},{4,12},{9,1},{13,5},{1,9},{5,13},{10,2},{14,6},... | collective-permute-start | bytes 98312 | tf_op jit(solution)/shard_map/ppermute | solution.py:229
  56.2 4.9 %collective-permute-start.5 = (bf16[32,512]{1,0:T(8,128)(2,1)S(1)}, bf16[32,512]{1,0:T(8,128)(2,1)S(1)}, u32[]{:S(2)}, u32[]{:S(2)}) collective-permute-start(bf16[32,512]{1,0:T(8,128)(2,1)S(1)} %shard_map.125.own_ref), channel_id=1, source_target_pairs={{12,0},{0,4},{4,8},{8,12},{13,1},{1,5},{5,9},{9,13},{14,2},{2,6},{... | collective-permute-start | bytes 98312 | tf_op jit(solution)/shard_map/ppermute | solution.py:229
  56.2 16.8 %copy-start.7 = (bf16[512,1024]{1,0:T(8,128)(2,1)S(1)}, bf16[512,1024]{1,0:T(8,128)(2,1)}, u32[]{:S(2)}) copy-start(bf16[512,1024]{1,0:T(8,128)(2,1)} %kvw_ref.1) | copy-start | bytes 3145732
  80.5 10.8 %collective-permute-start.6 = (bf16[256,512]{1,0:T(8,128)(2,1)S(1)}, bf16[256,512]{1,0:T(8,128)(2,1)S(1)}, u32[]{:S(2)}, u32[]{:S(2)}) collective-permute-start(bf16[256,512]{1,0:T(8,128)(2,1)S(1)} %get-tuple-element.34), channel_id=1, source_target_pairs={{0,1},{1,0},{2,3},{3,2},{4,5},{5,4},{6,7},{7,6},{8,9},{9,8},{10,11... | collective-permute-start | bytes 786440 | tf_op jit(solution)/shard_map/ppermute | solution.py:296
  87.7 15.0 %all-to-all-start.3 = ((bf16[16,32,512]{2,1,0:T(8,128)(2,1)}), bf16[16,32,512]{2,1,0:T(8,128)(2,1)S(1)}, u32[]{:S(2)}, u32[]{:S(2)}) async-start(bf16[16,32,512]{2,1,0:T(8,128)(2,1)} %bitcast.6), calls=%async_computation.3 | async-start | bytes 1048576 | tf_op jit(solution)/shard_map/all_to_all | solution.py:233
  91.3 8.0 %collective-permute-start.7 = (bf16[256,512]{1,0:T(8,128)(2,1)S(1)}, bf16[256,512]{1,0:T(8,128)(2,1)S(1)}, u32[]{:S(2)}, u32[]{:S(2)}) collective-permute-start(bf16[256,512]{1,0:T(8,128)(2,1)S(1)} %shard_map.130.one_ref), channel_id=1, source_target_pairs={{0,2},{1,3},{2,0},{3,1},{4,6},{5,7},{6,4},{7,5},{8,10},{9,11},{10,... | collective-permute-start | bytes 786440 | tf_op jit(solution)/shard_map/ppermute | solution.py:298
  99.4 11.3 %collective-permute-start.8 = (bf16[256,512]{1,0:T(8,128)(2,1)S(1)}, bf16[256,512]{1,0:T(8,128)(2,1)S(1)}, u32[]{:S(2)}, u32[]{:S(2)}) collective-permute-start(bf16[256,512]{1,0:T(8,128)(2,1)S(1)} %shard_map.131.mine_ref), channel_id=1, source_target_pairs={{0,1},{1,0},{2,3},{3,2},{4,5},{5,4},{6,7},{7,6},{8,9},{9,8},{10,11... | collective-permute-start | bytes 786440 | tf_op jit(solution)/shard_map/ppermute | solution.py:300
  102.7 4.1 %copy-start.5 = (bf16[8,512]{1,0:T(8,128)(2,1)S(1)}, bf16[8,512]{1,0:T(8,128)(2,1)}, u32[]{:S(2)}) copy-start(bf16[8,512]{1,0:T(8,128)(2,1)} %grad_ref.1) | copy-start | bytes 24580
  102.7 4.1 %copy-start.4 = (bf16[8,512]{1,0:T(8,128)(2,1)S(1)}, bf16[8,512]{1,0:T(8,128)(2,1)}, u32[]{:S(2)}) copy-start(bf16[8,512]{1,0:T(8,128)(2,1)} %embed_ref.1) | copy-start | bytes 24580
  102.7 6.6 %collective-permute-start.10 = (f32[8,512]{1,0:T(8,128)S(1)}, f32[8,512]{1,0:T(8,128)S(1)}, u32[]{:S(2)}, u32[]{:S(2)}) collective-permute-start(f32[8,512]{1,0:T(8,128)S(1)} %get-tuple-element.38), channel_id=1, source_target_pairs={{0,8},{4,12},{8,0},{12,4},{1,9},{5,13},{9,1},{13,5},{2,10},{6,14},... | collective-permute-start | bytes 49160 | tf_op jit(solution)/shard_map/ppermute | solution.py:288
  104.5 4.9 %collective-permute-start.11 = (f32[8,512]{1,0:T(8,128)S(1)}, f32[8,512]{1,0:T(8,128)S(1)}, u32[]{:S(2)}, u32[]{:S(2)}) collective-permute-start(f32[8,512]{1,0:T(8,128)S(1)} %get-tuple-element.37), channel_id=1, source_target_pairs={{0,12},{4,0},{8,4},{12,8},{1,13},{5,1},{9,5},{13,9},{2,14},{6,2},{... | collective-permute-start | bytes 49160 | tf_op jit(solution)/shard_map/ppermute | solution.py:288
  105.1 4.7 %collective-permute-start.9 = (f32[8,512]{1,0:T(8,128)S(1)}, f32[8,512]{1,0:T(8,128)S(1)}, u32[]{:S(2)}, u32[]{:S(2)}) collective-permute-start(f32[8,512]{1,0:T(8,128)S(1)} %get-tuple-element.39), channel_id=1, source_target_pairs={{0,4},{4,8},{8,12},{12,0},{1,5},{5,9},{9,13},{13,1},{2,6},{6,10},{... | collective-permute-start | bytes 49160 | tf_op jit(solution)/shard_map/ppermute | solution.py:288

commit v4 on v3

--- a/solution.py
+++ b/solution.py
@@ -61,10 +61,11 @@
     out_ref[:, width + LANES :] = grad_ref[...]
 
 
-def spread_kernel(own_ref, one_ref, two_ref, three_ref, *rest):
+def spread_kernel(high_ref, own_ref, one_ref, two_ref, three_ref, *rest):
     column_ref, plane_ref = rest[-2:]
     refs = (own_ref, one_ref, two_ref, three_ref)
-    column = jnp.concatenate([r[...].astype(F32) for r in refs], axis=0).astype(BF16)
+    column = jnp.concatenate([r[...].astype(F32) for r in refs], axis=0)
+    column = pltpu.roll(column, high_ref[0] * own_ref.shape[0], 0).astype(BF16)
     column_ref[...] = column
     for i in range(plane_ref.shape[0]):
         plane_ref[i] = column[:, : plane_ref.shape[2]]
@@ -117,14 +118,12 @@
 
 
 def norm_kernel(
-    own_ref, one_ref, two_ref, three_ref, gate_ref, dgated_ref, uslope_ref, datt_ref, gated_ref, dunit_ref
+    high_ref, own_ref, one_ref, two_ref, three_ref, gate_ref, dgated_ref, uslope_ref, datt_ref, gated_ref, dunit_ref
 ):
     own, width = gate_ref.shape
     block = own // HIGH
-    att = own_ref[...].astype(F32)
-    for k, ref in ((1, one_ref), (2, two_ref), (3, three_ref)):
-        part = ref[...].astype(F32)
-        att = att + jnp.concatenate([part[(HIGH - k) * block :], part[: (HIGH - k) * block]], axis=0)
+    refs = (own_ref, one_ref, two_ref, three_ref)
+    att = sum(ref[...].astype(F32) for ref in refs)
     mean = jnp.mean(att, axis=1, keepdims=True)
     centered = att - mean
     inverse = lax.rsqrt(jnp.mean(centered * centered, axis=1, keepdims=True) + 1e-05)
@@ -140,8 +139,9 @@
     datt = datt.astype(BF16)
     for i in range(datt_ref.shape[0]):
         datt_ref[i] = datt
-    gated_ref[...] = (normed * gate)[:block].astype(BF16)
-    dunit_ref[...] = (dgated * normed * uslope_ref[...])[:block].astype(BF16)
+    down = ((HIGH - high_ref[0]) & (HIGH - 1)) * block
+    gated_ref[...] = pltpu.roll(normed * gate, down, 0)[:block].astype(BF16)
+    dunit_ref[...] = pltpu.roll(dgated * normed * uslope_ref[...], down, 0)[:block].astype(BF16)
 
 
 def output_kernel(embed_ref, grad_ref, gated_ref, dunit_ref, out_ref, unit_ref, result_ref, base_ref):
@@ -151,7 +151,8 @@
 
 def silu_pair(u):
     t = jnp.tanh(u)
-    return u + u * t, (1.0 + t) + u * (1.0 - t * t)
+    ut = u * t
+    return u + ut, (1.0 + t) + (u - ut * t)
 
 
 def backward_kernel(
@@ -200,10 +201,11 @@
         copy.wait()
 
 
-def final_kernel(own_ref, one_ref, two_ref, three_ref, base_ref, weight_ref, result_ref):
-    dq = (own_ref[...] + one_ref[...]) + (two_ref[...] + three_ref[...])
-    dq = (dq * 0.0625).astype(BF16)
-    result_ref[...] = (base_ref[...] + nt(dq, weight_ref[...])).astype(BF16)
+def final_kernel(part_ref, base_ref, weight_ref, result_ref):
+    own, width = base_ref.shape
+    parts = part_ref.shape[0] // own
+    dq = jnp.sum(part_ref[...].astype(F32).reshape(parts, own, width), axis=0) * 0.0625
+    result_ref[...] = (base_ref[...] + nt(dq.astype(BF16), weight_ref[...])).astype(BF16)
 
 
 def shards(
@@ -232,6 +234,7 @@
         parts = value.reshape(plane, column, value.shape[-1])
         return lax.all_to_all(parts, "plane", 0, 0).reshape(rows, value.shape[-1])
 
+    high = lax.axis_index("high").reshape(1)
     sems = pltpu.SemaphoreType.DMA
     full = width + LANES + width
     pack = call(
@@ -248,9 +251,9 @@
     core = (lax.axis_index("cand") & 1).reshape(1)
     pay, spread = call(
         spread_kernel,
-        "vvvvhss",
+        "svvvvhss",
         [(s((column, full), BF16), "v"), (s((plane, column, width + LANES), BF16), "v")],
-    )(pack, *[from_up(pack, k) for k in (1, 2, 3)], keys, block_user, core)
+    )(high, pack, *[from_up(pack, k) for k in (1, 2, 3)], keys, block_user, core)
     pay_all = exchange(spread)
 
     col_f32 = (s((column, width), F32), "v")
@@ -267,8 +270,8 @@
     att_all = exchange(att)
     att_col = call(sum_kernel, "v", [col_b16], flops=1 << 20)(att_all)[0]
     datt, gated, dunit = call(
-        norm_kernel, "v" * 7, [(s((plane, column, width), BF16), "v"), own_b16, own_b16], flops=1 << 20
-    )(att_col, *[from_up(att_col, k) for k in (1, 2, 3)], gate, dgated, uslope)
+        norm_kernel, "s" + "v" * 7, [(s((plane, column, width), BF16), "v"), own_b16, own_b16], flops=1 << 20
+    )(high, att_col, *[from_up(att_col, k) for k in (1, 2, 3)], gate, dgated, uslope)
     datt_all = exchange(datt)
     candidate_output, base = call(output_kernel, "v" * 6, [own_b16, own_f32], flops=1 << 26)(
         candidate_embed, grad_output, gated, dunit, output_weight, unit_weight
@@ -282,15 +285,9 @@
         [pltpu.VMEM((rows, width), BF16), pltpu.VMEM((events, 2 * width), BF16)],
         flops=1 << 32,
     )(block_user, core, pay_all, query, datt_all, keys, values, keyval_weight)
-    dq_all = exchange(dq)
-    dq_col = call(sum_kernel, "v", [col_f32], flops=1 << 20)(dq_all)[0]
-    dq_parts = [
-        lax.ppermute(
-            dq_col[k * own : (k + 1) * own], "high", [(i, (i + k) % HIGH) for i in range(HIGH)]
-        )
-        for k in (1, 2, 3)
-    ]
-
+    dq_all = lax.all_to_all(
+        dq.reshape(plane * HIGH, own, width), ("plane", "high"), 0, 0
+    ).reshape(rows, width)
     swap_core = [(i, i ^ 1) for i in range(4)]
     swap_chip = [(i, i ^ 2) for i in range(4)]
     got = lax.ppermute(other, "cand", swap_core)
@@ -301,9 +298,7 @@
     history_grad = call(halves_kernel, "svv", [(s((events, width), BF16), "h")], [sems((2,))])(
         core, quad, got
     )[0]
-    candidate_grad = call(final_kernel, "v" * 6, [own_b16], flops=1 << 26)(
-        dq_col[:own], *dq_parts, base, query_weight
-    )[0]
+    candidate_grad = call(final_kernel, "v" * 3, [own_b16], flops=1 << 26)(dq_all, base, query_weight)[0]
     return (candidate_output, history_grad, candidate_grad)
 
 

time: 113 us -> 109 us (0.965)
  starting transfers between devices: 32.5 us -> 30.7 us
    ppermute x3 -> x0, starting transfers between devices: 4.1 us -> none  [shards(): lax.ppermute(dq_col[k * own:(k + 1) * own], 'high', [(i, (i + k) % HIGH)...]
    ppermute x1, waiting for transfers between devices: 7.21 us -> 10.2 us  [shards(): got = lax.ppermute(pair, 'cand', swap_chip)]
    all_to_all x1, waiting for transfers between devices: 2.34 us -> 0.01 us  [shards(): lax.all_to_all(dq.reshape(plane * HIGH, own, width), ('plane', 'high'), 0...]
    ppermute x3 -> x0, waiting for transfers between devices: 2.18 us -> none  [shards(): lax.ppermute(dq_col[k * own:(k + 1) * own], 'high', [(i, (i + k) % HIGH)...]
    all_to_all x1, starting transfers between devices: 3.57 us -> 5.57 us  [shards(): lax.all_to_all(dq.reshape(plane * HIGH, own, width), ('plane', 'high'), 0...]
    ppermute x1, waiting for transfers between devices: 0.01 us -> 1.16 us  [shards(): got = lax.ppermute(other, 'cand', swap_core)]
  transfers between devices with their start and end apart: 13 -> 10, of which waited for: 6 -> 5; matrix products, arithmetic and copies ran while one was open for 0% -> 0% of each run, Pallas kernels for 3% -> 3%
where the time goes in v4:
time: 109 us
  blocking collectives  41.6 us (38%)
  starting transfers between devices  30.7 us (28%)
  waiting for transfers between devices  16.2 us (15%)
  Pallas kernels  15.6 us (14%)
  local copies, waits for them, and re-layouts  2.31 us (2%)
  between operations  2.19 us (2%)
    all_to_all x3, blocking collectives, exchange(): return lax.all_to_all(parts, 'plane', 0, 0).reshape(rows, value.shape[-1])  41.6 us
    ppermute x6, starting transfers between devices, from_up(): lax.ppermute(value, 'high', [((i + k) % HIGH, i) for i in range(HIGH)])  16 us
    ppermute x1, waiting for transfers between devices, shards(): got = lax.ppermute(pair, 'cand', swap_chip)  10.2 us
    pallas_call x1, Pallas kernels, shards(): call(backward_kernel, 'ssvvvvvv', [big, (s((half, width), F32), 'v'), hal...  7.33 us
    ppermute x1, starting transfers between devices, shards(): got = lax.ppermute(other, 'cand', swap_core)  7.14 us
    all_to_all x1, starting transfers between devices, shards(): lax.all_to_all(dq.reshape(plane * HIGH, own, width), ('plane', 'high'), 0...  5.57 us
    ppermute x6, waiting for transfers between devices, from_up(): lax.ppermute(value, 'high', [((i + k) % HIGH, i) for i in range(HIGH)])  4.5 us
    pallas_call x1, Pallas kernels, shards(): call(forward_kernel, 'svvvv', [big, big], flops=1 << 31)  2.65 us
  transfers between devices with their start and end apart: 10, of which 5 were waited for; matrix products, arithmetic and copies ran while one was open for 0% of the time, Pallas kernels for 3%

profile of v4, /device:TPU:1, one launch (start us, length us, event | category | flops | bytes accessed | tf_op | source)
XLA Modules:
  0.0 108.6 jit_solution(8922229297524658885)
XLA Ops:
  0.6 1.4 %shard_map.121.own_ref = bf16[8,1152]{1,0:T(8,128)(2,1)} custom-call(s32[1,8]{1,0:T(1,128)} %bitcast.15, bf16[8,512]{1,0:T(8,128)(2,1)} %embed_ref.1, bf16[8,512]{1,0:T(8,128)(2,1)} %grad_ref.1), custom_call_target="tpu_custom_call" | custom-call | bytes 1048576 | tf_op jit(solution)/shard_map/pallas_call | solution.py:240
  2.1 6.9 %collective-permute-start = (bf16[8,1152]{1,0:T(8,128)(2,1)}, bf16[8,1152]{1,0:T(8,128)(2,1)S(1)}, u32[]{:S(2)}, u32[]{:S(2)}) collective-permute-start(bf16[8,1152]{1,0:T(8,128)(2,1)} %shard_map.121.own_ref), channel_id=1, source_target_pairs={{4,0},{8,4},{12,8},{0,12},{5,1},{9,5},{13,9},{1,13},{6,2},{10,6},{... | collective-permute-start | bytes 55304 | tf_op jit(solution)/shard_map/ppermute | solution.py:231
  9.0 1.0 collective-permute-start.1
  10.0 2.3 %collective-permute-start.2 = (bf16[8,1152]{1,0:T(8,128)(2,1)}, bf16[8,1152]{1,0:T(8,128)(2,1)S(1)}, u32[]{:S(2)}, u32[]{:S(2)}) collective-permute-start(bf16[8,1152]{1,0:T(8,128)(2,1)} %shard_map.121.own_ref), channel_id=1, source_target_pairs={{12,0},{0,4},{4,8},{8,12},{13,1},{1,5},{5,9},{9,13},{14,2},{2,6},{... | collective-permute-start | bytes 55304 | tf_op jit(solution)/shard_map/ppermute | solution.py:231
  12.9 0.0 copy-start.6
  12.9 1.2 %copy-done.6 = bf16[512,1024]{1,0:T(8,128)(2,1)S(1)} copy-done((bf16[512,1024]{1,0:T(8,128)(2,1)S(1)}, bf16[512,1024]{1,0:T(8,128)(2,1)}, u32[]{:S(2)}) %copy-start.6) | copy-done | bytes 1048600
  14.1 1.0 copy-done.8
  15.2 0.8 shard_map.122
  16.7 0.1 shard_map.123
  16.8 17.9 %all_to_all.20 = bf16[16,32,640]{2,1,0:T(8,128)(2,1)S(1)} all-to-all(bf16[16,32,640]{2,1,0:T(8,128)(2,1)S(1)} %get-tuple-element.21), channel_id=1, replica_groups=mesh['plane'=16,'high'=4,'cand'=4] {'plane'}, dimensions={0} | all-to-all | bytes 1310720 | tf_op jit(solution)/shard_map/all_to_all | solution.py:235
  34.8 2.7 %shard_map.124 = (bf16[512,512]{1,0:T(8,128)(2,1)S(1)}, bf16[512,512]{1,0:T(8,128)(2,1)S(1)}) custom-call(s32[1]{0:T(128)S(6)} %copy.13.rest_1_.user_ref, bf16[512,640]{1,0:T(8,128)(2,1)S(1)} %bitcast.11, bf16[512,512]{1,0:T(8,128)(2,1)S(1)} %copy-done.2, bf16[4,1024,128]{2,1,0:T(8,128)(2,1)S(1)} %get-tuple-element.20.rest_0_.key_ref, ...), custom_call_target="tpu_custom_call" | custom-call | flops 2147483648 | bytes 1048576 | tf_op jit(solution)/shard_map/pallas_call | solution.py:267
  37.4 12.0 %all_to_all.21 = bf16[16,32,512]{2,1,0:T(8,128)(2,1)S(1)} all-to-all(bf16[16,32,512]{2,1,0:T(8,128)(2,1)S(1)} %bitcast.14), channel_id=1, replica_groups=mesh['plane'=16,'high'=4,'cand'=4] {'plane'}, dimensions={0} | all-to-all | bytes 1048576 | tf_op jit(solution)/shard_map/all_to_all | solution.py:235
  49.5 0.1 shard_map.125.own_ref
  49.5 1.4 %collective-permute-start.3 = (bf16[32,512]{1,0:T(8,128)(2,1)S(1)}, bf16[32,512]{1,0:T(8,128)(2,1)S(1)}, u32[]{:S(2)}, u32[]{:S(2)}) collective-permute-start(bf16[32,512]{1,0:T(8,128)(2,1)S(1)} %shard_map.125.own_ref), channel_id=1, source_target_pairs={{4,0},{8,4},{12,8},{0,12},{5,1},{9,5},{13,9},{1,13},{6,2},{10,6},{... | collective-permute-start | bytes 98312 | tf_op jit(solution)/shard_map/ppermute | solution.py:231
  50.9 4.4 %collective-permute-start.4 = (bf16[32,512]{1,0:T(8,128)(2,1)S(1)}, bf16[32,512]{1,0:T(8,128)(2,1)S(1)}, u32[]{:S(2)}, u32[]{:S(2)}) collective-permute-start(bf16[32,512]{1,0:T(8,128)(2,1)S(1)} %shard_map.125.own_ref), channel_id=1, source_target_pairs={{8,0},{12,4},{0,8},{4,12},{9,1},{13,5},{1,9},{5,13},{10,2},{14,6},... | collective-permute-start | bytes 98312 | tf_op jit(solution)/shard_map/ppermute | solution.py:231
  55.3 0.3 shard_map.126
  55.7 1.9 %collective-permute-done.4.two_ref = bf16[32,512]{1,0:T(8,128)(2,1)S(1)} collective-permute-done((bf16[32,512]{1,0:T(8,128)(2,1)S(1)}, bf16[32,512]{1,0:T(8,128)(2,1)S(1)}, u32[]{:S(2)}, u32[]{:S(2)}) %collective-permute-start.4) | collective-permute-done | bytes 32800 | tf_op jit(solution)/shard_map/ppermute | solution.py:231
  57.6 2.6 %collective-permute-done.5.three_ref = bf16[32,512]{1,0:T(8,128)(2,1)S(1)} collective-permute-done((bf16[32,512]{1,0:T(8,128)(2,1)S(1)}, bf16[32,512]{1,0:T(8,128)(2,1)S(1)}, u32[]{:S(2)}, u32[]{:S(2)}) %collective-permute-start.5) | collective-permute-done | bytes 32800 | tf_op jit(solution)/shard_map/ppermute | solution.py:231
  60.2 0.3 shard_map.127
  60.5 11.7 %all_to_all.22 = bf16[16,32,512]{2,1,0:T(8,128)(2,1)S(1)} all-to-all(bf16[16,32,512]{2,1,0:T(8,128)(2,1)S(1)} %get-tuple-element.32), channel_id=1, replica_groups=mesh['plane'=16,'high'=4,'cand'=4] {'plane'}, dimensions={0} | all-to-all | bytes 1048576 | tf_op jit(solution)/shard_map/all_to_all | solution.py:235
  72.2 7.3 %shard_map.129 = (bf16[512,512]{1,0:T(8,128)(2,1)}, f32[256,512]{1,0:T(8,128)S(1)}, bf16[256,512]{1,0:T(8,128)(2,1)S(1)}) custom-call(s32[1]{0:T(128)S(6)} %copy.13.rest_1_.user_ref, s32[1]{0:T(128)} %bitcast.2.rest_2_.core_ref, bf16[512,640]{1,0:T(8,128)(2,1)S(1)} %bitcast.12, bf16[512,512]{1,0:T(8,128)(2,1)S(1)} %get-tuple-element.31.query_ref, ...), custom_call_target="tpu_custom_call" | custom-call | flops 4294967296 | bytes 1048576 | tf_op jit(solution)/shard_map/pallas_call | solution.py:281
  79.5 5.6 %all-to-all-start.3 = ((bf16[64,8,512]{2,1,0:T(8,128)(2,1)}), bf16[64,8,512]{2,1,0:T(8,128)(2,1)S(1)}, u32[]{:S(2)}, u32[]{:S(2)}) async-start(bf16[64,8,512]{2,1,0:T(8,128)(2,1)} %bitcast.7), calls=%async_computation.3 | async-start | bytes 1048576 | tf_op jit(solution)/shard_map/all_to_all | solution.py:288
  85.1 7.1 %collective-permute-start.6 = (bf16[256,512]{1,0:T(8,128)(2,1)S(1)}, bf16[256,512]{1,0:T(8,128)(2,1)S(1)}, u32[]{:S(2)}, u32[]{:S(2)}) collective-permute-start(bf16[256,512]{1,0:T(8,128)(2,1)S(1)} %get-tuple-element.34), channel_id=1, source_target_pairs={{0,1},{1,0},{2,3},{3,2},{4,5},{5,4},{6,7},{7,6},{8,9},{9,8},{10,11... | collective-permute-start | bytes 786440 | tf_op jit(solution)/shard_map/ppermute | solution.py:293
  92.2 1.2 %collective-permute-done.6.two_ref = bf16[256,512]{1,0:T(8,128)(2,1)S(1)} collective-permute-done((bf16[256,512]{1,0:T(8,128)(2,1)S(1)}, bf16[256,512]{1,0:T(8,128)(2,1)S(1)}, u32[]{:S(2)}, u32[]{:S(2)}) %collective-permute-start.6) | collective-permute-done | bytes 262176 | tf_op jit(solution)/shard_map/ppermute | solution.py:293
  93.4 0.7 collective-permute-start.7
  94.1 10.2 %collective-permute-done.7.two_ref = bf16[256,512]{1,0:T(8,128)(2,1)S(1)} collective-permute-done((bf16[256,512]{1,0:T(8,128)(2,1)S(1)}, bf16[256,512]{1,0:T(8,128)(2,1)S(1)}, u32[]{:S(2)}, u32[]{:S(2)}) %collective-permute-start.7) | collective-permute-done | bytes 262176 | tf_op jit(solution)/shard_map/ppermute | solution.py:295
  104.3 0.1 shard_map.131.mine_ref
  104.4 1.3 %collective-permute-start.8 = (bf16[256,512]{1,0:T(8,128)(2,1)S(1)}, bf16[256,512]{1,0:T(8,128)(2,1)S(1)}, u32[]{:S(2)}, u32[]{:S(2)}) collective-permute-start(bf16[256,512]{1,0:T(8,128)(2,1)S(1)} %shard_map.131.mine_ref), channel_id=1, source_target_pairs={{0,1},{1,0},{2,3},{3,2},{4,5},{5,4},{6,7},{7,6},{8,9},{9,8},{10,11... | collective-permute-start | bytes 786440 | tf_op jit(solution)/shard_map/ppermute | solution.py:297
  105.7 0.8 shard_map.128
  106.5 0.4 collective-permute-done.8.other_ref
  106.9 0.8 shard_map.132
  107.7 0.9 shard_map.133
  (26 shorter events, 0.1 us)
Async XLA Ops:
  2.1 14.6 %collective-permute-start = (bf16[8,1152]{1,0:T(8,128)(2,1)}, bf16[8,1152]{1,0:T(8,128)(2,1)S(1)}, u32[]{:S(2)}, u32[]{:S(2)}) collective-permute-start(bf16[8,1152]{1,0:T(8,128)(2,1)} %shard_map.121.own_ref), channel_id=1, source_target_pairs={{4,0},{8,4},{12,8},{0,12},{5,1},{9,5},{13,9},{1,13},{6,2},{10,6},{... | collective-permute-start | bytes 55304 | tf_op jit(solution)/shard_map/ppermute | solution.py:231
  9.0 7.7 %collective-permute-start.1 = (bf16[8,1152]{1,0:T(8,128)(2,1)}, bf16[8,1152]{1,0:T(8,128)(2,1)S(1)}, u32[]{:S(2)}, u32[]{:S(2)}) collective-permute-start(bf16[8,1152]{1,0:T(8,128)(2,1)} %shard_map.121.own_ref), channel_id=1, source_target_pairs={{8,0},{12,4},{0,8},{4,12},{9,1},{13,5},{1,9},{5,13},{10,2},{14,6},... | collective-permute-start | bytes 55304 | tf_op jit(solution)/shard_map/ppermute | solution.py:231
  10.0 6.7 %collective-permute-start.2 = (bf16[8,1152]{1,0:T(8,128)(2,1)}, bf16[8,1152]{1,0:T(8,128)(2,1)S(1)}, u32[]{:S(2)}, u32[]{:S(2)}) collective-permute-start(bf16[8,1152]{1,0:T(8,128)(2,1)} %shard_map.121.own_ref), channel_id=1, source_target_pairs={{12,0},{0,4},{4,8},{8,12},{13,1},{1,5},{5,9},{9,13},{14,2},{2,6},{... | collective-permute-start | bytes 55304 | tf_op jit(solution)/shard_map/ppermute | solution.py:231
  12.9 1.2 %copy-start.6 = (bf16[512,1024]{1,0:T(8,128)(2,1)S(1)}, bf16[512,1024]{1,0:T(8,128)(2,1)}, u32[]{:S(2)}) copy-start(bf16[512,1024]{1,0:T(8,128)(2,1)} %kvw_ref.1) | copy-start | bytes 3145732
  14.1 1.0 copy-start.8
  15.9 18.8 %copy-start.9 = (bf16[4,1024,128]{2,1,0:T(8,128)(2,1)}, bf16[4,1024,128]{2,1,0:T(8,128)(2,1)S(1)}, u32[]{:S(2)}) copy-start(bf16[4,1024,128]{2,1,0:T(8,128)(2,1)S(1)} %get-tuple-element.22.value_ref) | copy-start | bytes 3145732
  16.0 0.8 copy-start.3
  16.8 18.0 %copy-start.2 = (bf16[512,512]{1,0:T(8,128)(2,1)S(1)}, bf16[512,512]{1,0:T(8,128)(2,1)}, u32[]{:S(2)}) copy-start(bf16[512,512]{1,0:T(8,128)(2,1)} %weight_ref.5) | copy-start | bytes 1572868
  37.4 17.9 %copy-start.1 = (bf16[512,512]{1,0:T(8,128)(2,1)S(1)}, bf16[512,512]{1,0:T(8,128)(2,1)}, u32[]{:S(2)}) copy-start(bf16[512,512]{1,0:T(8,128)(2,1)} %out_ref.3) | copy-start | bytes 1572868
  49.5 5.9 %copy-start = (bf16[512,512]{1,0:T(8,128)(2,1)S(1)}, bf16[512,512]{1,0:T(8,128)(2,1)}, u32[]{:S(2)}) copy-start(bf16[512,512]{1,0:T(8,128)(2,1)} %unit_ref.3) | copy-start | bytes 1572868
  49.5 6.2 %collective-permute-start.3 = (bf16[32,512]{1,0:T(8,128)(2,1)S(1)}, bf16[32,512]{1,0:T(8,128)(2,1)S(1)}, u32[]{:S(2)}, u32[]{:S(2)}) collective-permute-start(bf16[32,512]{1,0:T(8,128)(2,1)S(1)} %shard_map.125.own_ref), channel_id=1, source_target_pairs={{4,0},{8,4},{12,8},{0,12},{5,1},{9,5},{13,9},{1,13},{6,2},{10,6},{... | collective-permute-start | bytes 98312 | tf_op jit(solution)/shard_map/ppermute | solution.py:231
  50.9 6.7 %collective-permute-start.4 = (bf16[32,512]{1,0:T(8,128)(2,1)S(1)}, bf16[32,512]{1,0:T(8,128)(2,1)S(1)}, u32[]{:S(2)}, u32[]{:S(2)}) collective-permute-start(bf16[32,512]{1,0:T(8,128)(2,1)S(1)} %shard_map.125.own_ref), channel_id=1, source_target_pairs={{8,0},{12,4},{0,8},{4,12},{9,1},{13,5},{1,9},{5,13},{10,2},{14,6},... | collective-permute-start | bytes 98312 | tf_op jit(solution)/shard_map/ppermute | solution.py:231
  55.3 4.9 %collective-permute-start.5 = (bf16[32,512]{1,0:T(8,128)(2,1)S(1)}, bf16[32,512]{1,0:T(8,128)(2,1)S(1)}, u32[]{:S(2)}, u32[]{:S(2)}) collective-permute-start(bf16[32,512]{1,0:T(8,128)(2,1)S(1)} %shard_map.125.own_ref), channel_id=1, source_target_pairs={{12,0},{0,4},{4,8},{8,12},{13,1},{1,5},{5,9},{9,13},{14,2},{2,6},{... | collective-permute-start | bytes 98312 | tf_op jit(solution)/shard_map/ppermute | solution.py:231
  55.3 16.8 %copy-start.7 = (bf16[512,1024]{1,0:T(8,128)(2,1)S(1)}, bf16[512,1024]{1,0:T(8,128)(2,1)}, u32[]{:S(2)}) copy-start(bf16[512,1024]{1,0:T(8,128)(2,1)} %kvw_ref.1) | copy-start | bytes 3145732
  55.3 16.8 %copy-start.10 = (bf16[4,1024,128]{2,1,0:T(8,128)(2,1)S(1)}, bf16[4,1024,128]{2,1,0:T(8,128)(2,1)}, u32[]{:S(2)}) copy-start(bf16[4,1024,128]{2,1,0:T(8,128)(2,1)} %copy-done.9) | copy-start | bytes 3145732
  79.5 28.2 %all-to-all-start.3 = ((bf16[64,8,512]{2,1,0:T(8,128)(2,1)}), bf16[64,8,512]{2,1,0:T(8,128)(2,1)S(1)}, u32[]{:S(2)}, u32[]{:S(2)}) async-start(bf16[64,8,512]{2,1,0:T(8,128)(2,1)} %bitcast.7), calls=%async_computation.3 | async-start | bytes 1048576 | tf_op jit(solution)/shard_map/all_to_all | solution.py:288
  85.1 8.3 %collective-permute-start.6 = (bf16[256,512]{1,0:T(8,128)(2,1)S(1)}, bf16[256,512]{1,0:T(8,128)(2,1)S(1)}, u32[]{:S(2)}, u32[]{:S(2)}) collective-permute-start(bf16[256,512]{1,0:T(8,128)(2,1)S(1)} %get-tuple-element.34), channel_id=1, source_target_pairs={{0,1},{1,0},{2,3},{3,2},{4,5},{5,4},{6,7},{7,6},{8,9},{9,8},{10,11... | collective-permute-start | bytes 786440 | tf_op jit(solution)/shard_map/ppermute | solution.py:293
  93.4 10.9 %collective-permute-start.7 = (bf16[256,512]{1,0:T(8,128)(2,1)S(1)}, bf16[256,512]{1,0:T(8,128)(2,1)S(1)}, u32[]{:S(2)}, u32[]{:S(2)}) collective-permute-start(bf16[256,512]{1,0:T(8,128)(2,1)S(1)} %shard_map.130.one_ref), channel_id=1, source_target_pairs={{0,2},{1,3},{2,0},{3,1},{4,6},{5,7},{6,4},{7,5},{8,10},{9,11},{10,... | collective-permute-start | bytes 786440 | tf_op jit(solution)/shard_map/ppermute | solution.py:295
  104.3 1.4 %copy-start.4 = (bf16[8,512]{1,0:T(8,128)(2,1)S(1)}, bf16[8,512]{1,0:T(8,128)(2,1)}, u32[]{:S(2)}) copy-start(bf16[8,512]{1,0:T(8,128)(2,1)} %embed_ref.1) | copy-start | bytes 24580
  104.3 1.4 %copy-start.5 = (bf16[8,512]{1,0:T(8,128)(2,1)S(1)}, bf16[8,512]{1,0:T(8,128)(2,1)}, u32[]{:S(2)}) copy-start(bf16[8,512]{1,0:T(8,128)(2,1)} %grad_ref.1) | copy-start | bytes 24580
  104.4 2.5 %collective-permute-start.8 = (bf16[256,512]{1,0:T(8,128)(2,1)S(1)}, bf16[256,512]{1,0:T(8,128)(2,1)S(1)}, u32[]{:S(2)}, u32[]{:S(2)}) collective-permute-start(bf16[256,512]{1,0:T(8,128)(2,1)S(1)} %shard_map.131.mine_ref), channel_id=1, source_target_pairs={{0,1},{1,0},{2,3},{3,2},{4,5},{5,4},{6,7},{7,6},{8,9},{9,8},{10,11... | collective-permute-start | bytes 786440 | tf_op jit(solution)/shard_map/ppermute | solution.py:297

commit v5 on v4

--- a/solution.py
+++ b/solution.py
@@ -11,7 +11,6 @@
 F32 = jnp.float32
 BF16 = jnp.bfloat16
 SMALL = 16 * 1024 * 1024
-WHOLE = 65600000
 HIGH = 4
 STEP = 256
 
@@ -25,7 +24,7 @@
 
 
 def call(body, ins, outs, scratch=(), flops=0, limit=SMALL):
-    place = {"v": pltpu.VMEM, "s": pltpu.SMEM, "h": pltpu.HBM}
+    place = {"v": pltpu.VMEM, "s": pltpu.SMEM, "h": pltpu.HBM, "a": pl.ANY}
     spec = [pl.BlockSpec(memory_space=place[i]) for i in ins]
     shapes = [shape for shape, _ in outs]
     out_spec = [pl.BlockSpec(memory_space=place[i]) for _, i in outs]
@@ -47,18 +46,8 @@
     return copies
 
 
-def pack_kernel(user_hbm, embed_hbm, grad_hbm, out_ref, user_ref, embed_ref, grad_ref, sems):
-    copies = start(sems, (user_hbm, user_ref), (embed_hbm, embed_ref), (grad_hbm, grad_ref))
-    for copy in copies:
-        copy.wait()
-    own, width = embed_ref.shape
-    row = lax.broadcasted_iota(jnp.int32, (own, own), 0)
-    lane = lax.broadcasted_iota(jnp.int32, (own, own), 1)
-    user = jnp.broadcast_to(user_ref[...].astype(F32), (own, own))
-    user = jnp.sum(jnp.where(row == lane, user, 0.0), axis=1, keepdims=True)
-    out_ref[:, :width] = embed_ref[...]
-    out_ref[:, width : width + LANES] = jnp.broadcast_to(user, (own, LANES)).astype(BF16)
-    out_ref[:, width + LANES :] = grad_ref[...]
+def touch_kernel(ref, out_ref):
+    out_ref[...] = ref[:16, :LANES]
 
 
 def spread_kernel(high_ref, own_ref, one_ref, two_ref, three_ref, *rest):
@@ -71,12 +60,12 @@
         plane_ref[i] = column[:, : plane_ref.shape[2]]
 
 
-def keyval_kernel(length_ref, hist_ref, weight_ref, key_ref, value_ref):
+def put_keyval(length, hist_ref, weight_ref, key_ref, value_ref):
     events = hist_ref.shape[0]
     keyval = nn(hist_ref[...], weight_ref[...])
     row = lax.broadcasted_iota(jnp.int32, (events, LANES), 0)
     lane = lax.broadcasted_iota(jnp.int32, (events, LANES), 1)
-    live = row < length_ref[0]
+    live = row < length
     half = LANES // 2
     for p in range(PAIRS):
         for ref, base in ((key_ref, 0), (value_ref, PAIRS * LANES)):
@@ -85,8 +74,11 @@
             ref[p, events:, :] = jnp.where(live & (lane >= half), part, 0.0).astype(BF16)
 
 
-def forward_kernel(user_ref, pay_ref, weight_ref, key_ref, value_ref, query_ref, att_ref):
+def forward_kernel(
+    user_ref, length_ref, pay_ref, weight_ref, hist_ref, kvw_ref, key_ref, value_ref, query_ref, att_ref
+):
     rows, width = query_ref.shape
+    put_keyval(length_ref[0], hist_ref, kvw_ref, key_ref, value_ref)
     pay = pay_ref[...]
     mine = pay[:, width : width + 1].astype(F32) == user_ref[0].astype(F32)
     query = nn(pay[:, :width], weight_ref[...]).astype(BF16).astype(F32)
@@ -237,23 +229,16 @@
     high = lax.axis_index("high").reshape(1)
     sems = pltpu.SemaphoreType.DMA
     full = width + LANES + width
-    pack = call(
-        pack_kernel,
-        "hhh",
-        [(s((own, full), BF16), "v")],
-        [pltpu.VMEM((1, own), jnp.int32), pltpu.VMEM((own, width), BF16), pltpu.VMEM((own, width), BF16), sems((3,))],
-        limit=WHOLE,
-    )(candidate_user.reshape(1, own), candidate_embed, grad_output)[0]
+    user = jnp.broadcast_to(candidate_user[:, None], (own, LANES)).astype(BF16)
+    pack = jnp.concatenate([candidate_embed, user, grad_output], axis=1)
     wide = (s((PAIRS, 2 * events, LANES), BF16), "v")
-    keys, values = call(keyval_kernel, "svv", [wide, wide], flops=1 << 30)(
-        block_length, history_embed, keyval_weight
-    )
     core = (lax.axis_index("cand") & 1).reshape(1)
+    touched = call(touch_kernel, "v", [(s((16, LANES), BF16), "v")])(keyval_weight)[0]
     pay, spread = call(
         spread_kernel,
-        "svvvvhss",
+        "svvvvsssa",
         [(s((column, full), BF16), "v"), (s((plane, column, width + LANES), BF16), "v")],
-    )(high, pack, *[from_up(pack, k) for k in (1, 2, 3)], keys, block_user, core)
+    )(high, pack, *[from_up(pack, k) for k in (1, 2, 3)], block_user, block_length, core, touched)
     pay_all = exchange(spread)
 
     col_f32 = (s((column, width), F32), "v")
@@ -264,8 +249,8 @@
     gate, uslope, dgated = call(own_kernel, "vvv", [col_f32] * 3, flops=1 << 26)(
         pay, unit_weight, output_weight
     )
-    query, att = call(forward_kernel, "svvvv", [big, big], flops=1 << 31)(
-        block_user, pay_all, query_weight, keys, values
+    keys, values, query, att = call(forward_kernel, "ssvvvv", [wide, wide, big, big], flops=1 << 31)(
+        block_user, block_length, pay_all, query_weight, history_embed, keyval_weight
     )
     att_all = exchange(att)
     att_col = call(sum_kernel, "v", [col_b16], flops=1 << 20)(att_all)[0]

time: 109 us -> 108 us (level)
  Pallas kernels: 15.6 us -> 14.1 us
  other arithmetic: 0 us -> 1.38 us
    pallas_call x4 -> x3, Pallas kernels: 4.92 us -> 3.33 us  [the longest x1 3.26 us: shards(): call(forward_kernel, 'ssvvvv', [wide, wide, big, big], flops=1 << 31)]
    unnamed x22 -> x16, local copies, waits for them, and re-layouts: 2.31 us -> 1.25 us
  transfers between devices with their start and end apart: 10 -> 10, of which waited for: 5 -> 6; matrix products, arithmetic and copies ran while one was open for 0% -> 0% of each run, Pallas kernels for 3% -> 2%
where the time goes in v5:
time: 108 us; the launch traced here: 107 us
  blocking collectives  41 us (38%)
  starting transfers between devices  30.6 us (28%)
  waiting for transfers between devices  16.9 us (16%)
  Pallas kernels  14.1 us (13%)
  between operations  2.04 us (2%)
  other arithmetic  1.38 us (1%)
  local copies, waits for them, and re-layouts  1.33 us (1%)
    all_to_all x3, blocking collectives, exchange(): return lax.all_to_all(parts, 'plane', 0, 0).reshape(rows, value.shape[-1])  41 us
    ppermute x6, starting transfers between devices, from_up(): lax.ppermute(value, 'high', [((i + k) % HIGH, i) for i in range(HIGH)])  16.1 us
    ppermute x1, waiting for transfers between devices, shards(): got = lax.ppermute(pair, 'cand', swap_chip)  10.5 us
    pallas_call x1, Pallas kernels, shards(): call(backward_kernel, 'ssvvvvvv', [big, (s((half, width), F32), 'v'), hal...  7.46 us
    ppermute x1, starting transfers between devices, shards(): got = lax.ppermute(other, 'cand', swap_core)  7.43 us
    all_to_all x1, starting transfers between devices, shards(): lax.all_to_all(dq.reshape(plane * HIGH, own, width), ('plane', 'high'), 0...  5.52 us
    ppermute x6, waiting for transfers between devices, from_up(): lax.ppermute(value, 'high', [((i + k) % HIGH, i) for i in range(HIGH)])  4.9 us
    pallas_call x1, Pallas kernels, shards(): call(forward_kernel, 'ssvvvv', [wide, wide, big, big], flops=1 << 31)  3.26 us
  transfers between devices with their start and end apart: 10, of which 6 were waited for; matrix products, arithmetic and copies ran while one was open for 0% of the time, Pallas kernels for 2%

profile of v5, /device:TPU:1, one launch (start us, length us, event | category | flops | bytes accessed | tf_op | source)
XLA Modules:
  0.0 107.4 jit_solution(12378398817411650140)
XLA Ops:
  0.6 0.7 convert_element_type.4
  1.3 0.1 broadcast_in_dim.2
  1.4 0.7 pad_maximum_fusion.own_ref
  2.1 6.8 %collective-permute-start = (bf16[8,1152]{1,0:T(8,128)(2,1)S(1)}, bf16[8,1152]{1,0:T(8,128)(2,1)S(1)}, u32[]{:S(2)}, u32[]{:S(2)}) collective-permute-start(bf16[8,1152]{1,0:T(8,128)(2,1)S(1)} %pad_maximum_fusion.own_ref), channel_id=1, source_target_pairs={{4,0},{8,4},{12,8},{0,12},{5,1},{9,5},{13,9},{1,13},{6,2},{10,6},{... | collective-permute-start | bytes 55304 | tf_op jit(solution)/shard_map/ppermute | solution.py:223
  8.9 0.9 collective-permute-start.1
  9.8 2.4 %collective-permute-start.2 = (bf16[8,1152]{1,0:T(8,128)(2,1)S(1)}, bf16[8,1152]{1,0:T(8,128)(2,1)S(1)}, u32[]{:S(2)}, u32[]{:S(2)}) collective-permute-start(bf16[8,1152]{1,0:T(8,128)(2,1)S(1)} %pad_maximum_fusion.own_ref), channel_id=1, source_target_pairs={{12,0},{0,4},{4,8},{8,12},{13,1},{1,5},{5,9},{9,13},{14,2},{2,6},{... | collective-permute-start | bytes 55304 | tf_op jit(solution)/shard_map/ppermute | solution.py:223
  13.5 1.2 %copy-done.2 = bf16[512,1024]{1,0:T(8,128)(2,1)S(1)} copy-done((bf16[512,1024]{1,0:T(8,128)(2,1)S(1)}, bf16[512,1024]{1,0:T(8,128)(2,1)}, u32[]{:S(2)}) %copy-start.2) | copy-done | bytes 1048600
  14.7 0.7 collective-permute-done.1.two_ref
  15.5 0.1 shard_map.122
  15.6 17.4 %all_to_all.20 = bf16[16,32,640]{2,1,0:T(8,128)(2,1)S(1)} all-to-all(bf16[16,32,640]{2,1,0:T(8,128)(2,1)S(1)} %get-tuple-element.20), channel_id=1, replica_groups=mesh['plane'=16,'high'=4,'cand'=4] {'plane'}, dimensions={0} | all-to-all | bytes 1310720 | tf_op jit(solution)/shard_map/all_to_all | solution.py:227
  32.9 3.3 %shard_map.123 = (bf16[4,1024,128]{2,1,0:T(8,128)(2,1)S(1)}, bf16[4,1024,128]{2,1,0:T(8,128)(2,1)S(1)}, bf16[512,512]{1,0:T(8,128)(2,1)S(1)}, bf16[512,512]{1,0:T(8,128)(2,1)S(1)}) custom-call(s32[1]{0:T(128)S(6)} %copy.13.rest_0_.user_ref, s32[1]{0:T(128)S(6)} %copy.14.rest_1_.length_ref, bf16[512,640]{1,0:T(8,128)(2,1)S(1)} %bitcast.10, ...), custom_call_target="tpu_custom_call" | custom-call | flops 2147483648 | bytes 1048576 | tf_op jit(solution)/shard_map/pallas_call | solution.py:252
  36.2 12.0 %all_to_all.21 = bf16[16,32,512]{2,1,0:T(8,128)(2,1)S(1)} all-to-all(bf16[16,32,512]{2,1,0:T(8,128)(2,1)S(1)} %bitcast.13), channel_id=1, replica_groups=mesh['plane'=16,'high'=4,'cand'=4] {'plane'}, dimensions={0} | all-to-all | bytes 1048576 | tf_op jit(solution)/shard_map/all_to_all | solution.py:227
  48.2 0.1 shard_map.124.own_ref
  48.3 1.5 %collective-permute-start.3 = (bf16[32,512]{1,0:T(8,128)(2,1)S(1)}, bf16[32,512]{1,0:T(8,128)(2,1)S(1)}, u32[]{:S(2)}, u32[]{:S(2)}) collective-permute-start(bf16[32,512]{1,0:T(8,128)(2,1)S(1)} %shard_map.124.own_ref), channel_id=1, source_target_pairs={{4,0},{8,4},{12,8},{0,12},{5,1},{9,5},{13,9},{1,13},{6,2},{10,6},{... | collective-permute-start | bytes 98312 | tf_op jit(solution)/shard_map/ppermute | solution.py:223
  49.8 4.2 %collective-permute-start.4 = (bf16[32,512]{1,0:T(8,128)(2,1)S(1)}, bf16[32,512]{1,0:T(8,128)(2,1)S(1)}, u32[]{:S(2)}, u32[]{:S(2)}) collective-permute-start(bf16[32,512]{1,0:T(8,128)(2,1)S(1)} %shard_map.124.own_ref), channel_id=1, source_target_pairs={{8,0},{12,4},{0,8},{4,12},{9,1},{13,5},{1,9},{5,13},{10,2},{14,6},... | collective-permute-start | bytes 98312 | tf_op jit(solution)/shard_map/ppermute | solution.py:223
  53.9 0.4 collective-permute-start.5
  54.3 0.4 shard_map.125
  54.7 1.8 %collective-permute-done.4.two_ref = bf16[32,512]{1,0:T(8,128)(2,1)S(1)} collective-permute-done((bf16[32,512]{1,0:T(8,128)(2,1)S(1)}, bf16[32,512]{1,0:T(8,128)(2,1)S(1)}, u32[]{:S(2)}, u32[]{:S(2)}) %collective-permute-start.4) | collective-permute-done | bytes 32800 | tf_op jit(solution)/shard_map/ppermute | solution.py:223
  56.4 2.4 %collective-permute-done.5.three_ref = bf16[32,512]{1,0:T(8,128)(2,1)S(1)} collective-permute-done((bf16[32,512]{1,0:T(8,128)(2,1)S(1)}, bf16[32,512]{1,0:T(8,128)(2,1)S(1)}, u32[]{:S(2)}, u32[]{:S(2)}) %collective-permute-start.5) | collective-permute-done | bytes 32800 | tf_op jit(solution)/shard_map/ppermute | solution.py:223
  58.8 0.3 shard_map.126
  59.1 11.7 %all_to_all.22 = bf16[16,32,512]{2,1,0:T(8,128)(2,1)S(1)} all-to-all(bf16[16,32,512]{2,1,0:T(8,128)(2,1)S(1)} %get-tuple-element.30), channel_id=1, replica_groups=mesh['plane'=16,'high'=4,'cand'=4] {'plane'}, dimensions={0} | all-to-all | bytes 1048576 | tf_op jit(solution)/shard_map/all_to_all | solution.py:227
  70.8 7.5 %shard_map.128 = (bf16[512,512]{1,0:T(8,128)(2,1)}, f32[256,512]{1,0:T(8,128)S(1)}, bf16[256,512]{1,0:T(8,128)(2,1)S(1)}) custom-call(s32[1]{0:T(128)S(6)} %copy.13.rest_0_.user_ref, s32[1]{0:T(128)} %bitcast.1.rest_2_.core_ref, bf16[512,640]{1,0:T(8,128)(2,1)S(1)} %bitcast.11, bf16[512,512]{1,0:T(8,128)(2,1)S(1)} %get-tuple-element.29.query_ref, ...), custom_call_target="tpu_custom_call" | custom-call | flops 4294967296 | bytes 1048576 | tf_op jit(solution)/shard_map/pallas_call | solution.py:266
  78.3 5.5 %all-to-all-start.3 = ((bf16[64,8,512]{2,1,0:T(8,128)(2,1)}), bf16[64,8,512]{2,1,0:T(8,128)(2,1)S(1)}, u32[]{:S(2)}, u32[]{:S(2)}) async-start(bf16[64,8,512]{2,1,0:T(8,128)(2,1)} %bitcast.6), calls=%async_computation.3 | async-start | bytes 1048576 | tf_op jit(solution)/shard_map/all_to_all | solution.py:273
  83.8 7.4 %collective-permute-start.6 = (bf16[256,512]{1,0:T(8,128)(2,1)S(1)}, bf16[256,512]{1,0:T(8,128)(2,1)S(1)}, u32[]{:S(2)}, u32[]{:S(2)}) collective-permute-start(bf16[256,512]{1,0:T(8,128)(2,1)S(1)} %get-tuple-element.34), channel_id=1, source_target_pairs={{0,1},{1,0},{2,3},{3,2},{4,5},{5,4},{6,7},{7,6},{8,9},{9,8},{10,11... | collective-permute-start | bytes 786440 | tf_op jit(solution)/shard_map/ppermute | solution.py:278
  91.2 1.2 %collective-permute-done.6.two_ref = bf16[256,512]{1,0:T(8,128)(2,1)S(1)} collective-permute-done((bf16[256,512]{1,0:T(8,128)(2,1)S(1)}, bf16[256,512]{1,0:T(8,128)(2,1)S(1)}, u32[]{:S(2)}, u32[]{:S(2)}) %collective-permute-start.6) | collective-permute-done | bytes 262176 | tf_op jit(solution)/shard_map/ppermute | solution.py:278
  92.4 0.5 collective-permute-start.7
  92.9 10.5 %collective-permute-done.7.two_ref = bf16[256,512]{1,0:T(8,128)(2,1)S(1)} collective-permute-done((bf16[256,512]{1,0:T(8,128)(2,1)S(1)}, bf16[256,512]{1,0:T(8,128)(2,1)S(1)}, u32[]{:S(2)}, u32[]{:S(2)}) %collective-permute-start.7) | collective-permute-done | bytes 262176 | tf_op jit(solution)/shard_map/ppermute | solution.py:280
  103.4 1.0 collective-permute-start.8
  104.5 0.8 shard_map.127
  105.3 0.4 collective-permute-done.8.other_ref
  105.6 0.8 shard_map.131
  106.5 0.9 shard_map.132
  (22 shorter events, 0.2 us)
Async XLA Ops:
  2.1 12.6 %collective-permute-start = (bf16[8,1152]{1,0:T(8,128)(2,1)S(1)}, bf16[8,1152]{1,0:T(8,128)(2,1)S(1)}, u32[]{:S(2)}, u32[]{:S(2)}) collective-permute-start(bf16[8,1152]{1,0:T(8,128)(2,1)S(1)} %pad_maximum_fusion.own_ref), channel_id=1, source_target_pairs={{4,0},{8,4},{12,8},{0,12},{5,1},{9,5},{13,9},{1,13},{6,2},{10,6},{... | collective-permute-start | bytes 55304 | tf_op jit(solution)/shard_map/ppermute | solution.py:223
  8.9 6.5 %collective-permute-start.1 = (bf16[8,1152]{1,0:T(8,128)(2,1)S(1)}, bf16[8,1152]{1,0:T(8,128)(2,1)S(1)}, u32[]{:S(2)}, u32[]{:S(2)}) collective-permute-start(bf16[8,1152]{1,0:T(8,128)(2,1)S(1)} %pad_maximum_fusion.own_ref), channel_id=1, source_target_pairs={{8,0},{12,4},{0,8},{4,12},{9,1},{13,5},{1,9},{5,13},{10,2},{14,6},... | collective-permute-start | bytes 55304 | tf_op jit(solution)/shard_map/ppermute | solution.py:223
  9.8 5.6 %collective-permute-start.2 = (bf16[8,1152]{1,0:T(8,128)(2,1)S(1)}, bf16[8,1152]{1,0:T(8,128)(2,1)S(1)}, u32[]{:S(2)}, u32[]{:S(2)}) collective-permute-start(bf16[8,1152]{1,0:T(8,128)(2,1)S(1)} %pad_maximum_fusion.own_ref), channel_id=1, source_target_pairs={{12,0},{0,4},{4,8},{8,12},{13,1},{1,5},{5,9},{9,13},{14,2},{2,6},{... | collective-permute-start | bytes 55304 | tf_op jit(solution)/shard_map/ppermute | solution.py:223
  13.5 1.2 %copy-start.2 = (bf16[512,1024]{1,0:T(8,128)(2,1)S(1)}, bf16[512,1024]{1,0:T(8,128)(2,1)}, u32[]{:S(2)}) copy-start(bf16[512,1024]{1,0:T(8,128)(2,1)} %kvw_ref.3) | copy-start | bytes 3145732
  14.7 18.2 %copy-start.3 = (bf16[512,1024]{1,0:T(8,128)(2,1)S(1)}, bf16[512,1024]{1,0:T(8,128)(2,1)}, u32[]{:S(2)}) copy-start(bf16[512,1024]{1,0:T(8,128)(2,1)} %kvw_ref.3) | copy-start | bytes 3145732
  15.5 17.4 %copy-start.4 = (bf16[512,512]{1,0:T(8,128)(2,1)S(1)}, bf16[512,512]{1,0:T(8,128)(2,1)}, u32[]{:S(2)}) copy-start(bf16[512,512]{1,0:T(8,128)(2,1)} %weight_ref.3) | copy-start | bytes 1572868
  15.5 17.4 %copy-start.7 = (bf16[512,512]{1,0:T(8,128)(2,1)S(1)}, bf16[512,512]{1,0:T(8,128)(2,1)}, u32[]{:S(2)}) copy-start(bf16[512,512]{1,0:T(8,128)(2,1)} %hist_ref.1) | copy-start | bytes 1572868
  36.2 18.1 %copy-start.1 = (bf16[512,512]{1,0:T(8,128)(2,1)S(1)}, bf16[512,512]{1,0:T(8,128)(2,1)}, u32[]{:S(2)}) copy-start(bf16[512,512]{1,0:T(8,128)(2,1)} %out_ref.3) | copy-start | bytes 1572868
  48.2 6.1 %copy-start = (bf16[512,512]{1,0:T(8,128)(2,1)S(1)}, bf16[512,512]{1,0:T(8,128)(2,1)}, u32[]{:S(2)}) copy-start(bf16[512,512]{1,0:T(8,128)(2,1)} %unit_ref.3) | copy-start | bytes 1572868
  48.3 6.4 %collective-permute-start.3 = (bf16[32,512]{1,0:T(8,128)(2,1)S(1)}, bf16[32,512]{1,0:T(8,128)(2,1)S(1)}, u32[]{:S(2)}, u32[]{:S(2)}) collective-permute-start(bf16[32,512]{1,0:T(8,128)(2,1)S(1)} %shard_map.124.own_ref), channel_id=1, source_target_pairs={{4,0},{8,4},{12,8},{0,12},{5,1},{9,5},{13,9},{1,13},{6,2},{10,6},{... | collective-permute-start | bytes 98312 | tf_op jit(solution)/shard_map/ppermute | solution.py:223
  49.8 6.7 %collective-permute-start.4 = (bf16[32,512]{1,0:T(8,128)(2,1)S(1)}, bf16[32,512]{1,0:T(8,128)(2,1)S(1)}, u32[]{:S(2)}, u32[]{:S(2)}) collective-permute-start(bf16[32,512]{1,0:T(8,128)(2,1)S(1)} %shard_map.124.own_ref), channel_id=1, source_target_pairs={{8,0},{12,4},{0,8},{4,12},{9,1},{13,5},{1,9},{5,13},{10,2},{14,6},... | collective-permute-start | bytes 98312 | tf_op jit(solution)/shard_map/ppermute | solution.py:223
  53.9 4.9 %collective-permute-start.5 = (bf16[32,512]{1,0:T(8,128)(2,1)S(1)}, bf16[32,512]{1,0:T(8,128)(2,1)S(1)}, u32[]{:S(2)}, u32[]{:S(2)}) collective-permute-start(bf16[32,512]{1,0:T(8,128)(2,1)S(1)} %shard_map.124.own_ref), channel_id=1, source_target_pairs={{12,0},{0,4},{4,8},{8,12},{13,1},{1,5},{5,9},{9,13},{14,2},{2,6},{... | collective-permute-start | bytes 98312 | tf_op jit(solution)/shard_map/ppermute | solution.py:223
  78.3 28.2 %all-to-all-start.3 = ((bf16[64,8,512]{2,1,0:T(8,128)(2,1)}), bf16[64,8,512]{2,1,0:T(8,128)(2,1)S(1)}, u32[]{:S(2)}, u32[]{:S(2)}) async-start(bf16[64,8,512]{2,1,0:T(8,128)(2,1)} %bitcast.6), calls=%async_computation.3 | async-start | bytes 1048576 | tf_op jit(solution)/shard_map/all_to_all | solution.py:273
  83.8 8.6 %collective-permute-start.6 = (bf16[256,512]{1,0:T(8,128)(2,1)S(1)}, bf16[256,512]{1,0:T(8,128)(2,1)S(1)}, u32[]{:S(2)}, u32[]{:S(2)}) collective-permute-start(bf16[256,512]{1,0:T(8,128)(2,1)S(1)} %get-tuple-element.34), channel_id=1, source_target_pairs={{0,1},{1,0},{2,3},{3,2},{4,5},{5,4},{6,7},{7,6},{8,9},{9,8},{10,11... | collective-permute-start | bytes 786440 | tf_op jit(solution)/shard_map/ppermute | solution.py:278
  92.4 10.9 %collective-permute-start.7 = (bf16[256,512]{1,0:T(8,128)(2,1)S(1)}, bf16[256,512]{1,0:T(8,128)(2,1)S(1)}, u32[]{:S(2)}, u32[]{:S(2)}) collective-permute-start(bf16[256,512]{1,0:T(8,128)(2,1)S(1)} %shard_map.129.one_ref), channel_id=1, source_target_pairs={{0,2},{1,3},{2,0},{3,1},{4,6},{5,7},{6,4},{7,5},{8,10},{9,11},{10,... | collective-permute-start | bytes 786440 | tf_op jit(solution)/shard_map/ppermute | solution.py:280
  103.4 1.1 %copy-start.5 = (bf16[8,512]{1,0:T(8,128)(2,1)S(1)}, bf16[8,512]{1,0:T(8,128)(2,1)}, u32[]{:S(2)}) copy-start(bf16[8,512]{1,0:T(8,128)(2,1)} %embed_ref.1) | copy-start | bytes 24580
  103.4 1.1 %copy-start.6 = (bf16[8,512]{1,0:T(8,128)(2,1)S(1)}, bf16[8,512]{1,0:T(8,128)(2,1)}, u32[]{:S(2)}) copy-start(bf16[8,512]{1,0:T(8,128)(2,1)} %grad_ref.1) | copy-start | bytes 24580
  103.4 2.2 %collective-permute-start.8 = (bf16[256,512]{1,0:T(8,128)(2,1)S(1)}, bf16[256,512]{1,0:T(8,128)(2,1)S(1)}, u32[]{:S(2)}, u32[]{:S(2)}) collective-permute-start(bf16[256,512]{1,0:T(8,128)(2,1)S(1)} %shard_map.130.mine_ref), channel_id=1, source_target_pairs={{0,1},{1,0},{2,3},{3,2},{4,5},{5,4},{6,7},{7,6},{8,9},{9,8},{10,11... | collective-permute-start | bytes 786440 | tf_op jit(solution)/shard_map/ppermute | solution.py:282

commit v6 on v5

--- a/solution.py
+++ b/solution.py
@@ -10,7 +10,8 @@
 LANES = 128
 F32 = jnp.float32
 BF16 = jnp.bfloat16
-SMALL = 16 * 1024 * 1024
+EARLY = 2
+SMALL = 10 * 1024 * 1024
 HIGH = 4
 STEP = 256
 
@@ -110,7 +111,7 @@
 
 
 def norm_kernel(
-    high_ref, own_ref, one_ref, two_ref, three_ref, gate_ref, dgated_ref, uslope_ref, datt_ref, gated_ref, dunit_ref
+    high_ref, own_ref, one_ref, two_ref, three_ref, gate_ref, dgated_ref, uslope_ref, _, datt_ref, gated_ref, dunit_ref
 ):
     own, width = gate_ref.shape
     block = own // HIGH
@@ -147,8 +148,18 @@
     return u + ut, (1.0 + t) + (u - ut * t)
 
 
+def early_kernel(query_ref, key_ref, weight_ref, slope_ref):
+    events = key_ref.shape[1] // 2
+    for p in range(EARLY):
+        cols = slice(p * LANES, (p + 1) * LANES)
+        for r in (slice(0, events), slice(events, 2 * events)):
+            weight, slope = silu_pair(nt(key_ref[p, r, :], query_ref[:, cols]))
+            weight_ref[p, r, :] = weight.astype(BF16)
+            slope_ref[p, r, :] = slope.astype(BF16)
+
+
 def backward_kernel(
-    user_ref, core_ref, pay_ref, query_ref, datt_ref, key_ref, value_ref, kvw_ref,
+    user_ref, core_ref, pay_ref, query_ref, datt_ref, key_ref, value_ref, kvw_ref, weight_ref, slope_ref,
     dq_ref, mine_ref, other_ref, masked_ref, dkv_ref,
 ):
     width = datt_ref.shape[1]
@@ -164,7 +175,10 @@
         dks, dvs, dqs = [], [], []
         for r in (slice(0, events), slice(events, 2 * events)):
             key = key_ref[p, r, :]
-            weight, slope = silu_pair(nt(key, query))
+            if p < EARLY:
+                weight, slope = weight_ref[p, r, :], slope_ref[p, r, :].astype(F32)
+            else:
+                weight, slope = silu_pair(nt(key, query))
             ds = (nt(value_ref[p, r, :], datt) * slope).astype(BF16)
             dks.append(nn(ds, query))
             dvs.append(nn(weight.astype(BF16), datt))
@@ -253,10 +267,12 @@
         block_user, block_length, pay_all, query_weight, history_embed, keyval_weight
     )
     att_all = exchange(att)
+    early = (s((EARLY, 2 * events, rows), BF16), "v")
+    weight, slope = call(early_kernel, "vv", [early, early], flops=1 << 28)(query, keys)
     att_col = call(sum_kernel, "v", [col_b16], flops=1 << 20)(att_all)[0]
     datt, gated, dunit = call(
-        norm_kernel, "s" + "v" * 7, [(s((plane, column, width), BF16), "v"), own_b16, own_b16], flops=1 << 20
-    )(high, att_col, *[from_up(att_col, k) for k in (1, 2, 3)], gate, dgated, uslope)
+        norm_kernel, "s" + "v" * 7 + "a", [(s((plane, column, width), BF16), "v"), own_b16, own_b16], flops=1 << 20
+    )(high, att_col, *[from_up(att_col, k) for k in (1, 2, 3)], gate, dgated, uslope, weight)
     datt_all = exchange(datt)
     candidate_output, base = call(output_kernel, "v" * 6, [own_b16, own_f32], flops=1 << 26)(
         candidate_embed, grad_output, gated, dunit, output_weight, unit_weight
@@ -265,11 +281,11 @@
     half_b16 = (s((half, width), BF16), "v")
     dq, mine, other = call(
         backward_kernel,
-        "ssvvvvvv",
+        "ssvvvvvvvv",
         [big, (s((half, width), F32), "v"), half_b16],
         [pltpu.VMEM((rows, width), BF16), pltpu.VMEM((events, 2 * width), BF16)],
         flops=1 << 32,
-    )(block_user, core, pay_all, query, datt_all, keys, values, keyval_weight)
+    )(block_user, core, pay_all, query, datt_all, keys, values, keyval_weight, weight, slope)
     dq_all = lax.all_to_all(
         dq.reshape(plane * HIGH, own, width), ("plane", "high"), 0, 0
     ).reshape(rows, width)

time: 108 us -> 108 us (level)
  waiting for transfers between devices: 16.9 us -> 14.7 us
  starting transfers between devices: 30.6 us -> 32.2 us
    ppermute x6, waiting for transfers between devices: 4.9 us -> 3.56 us  [from_up(): lax.ppermute(value, 'high', [((i + k) % HIGH, i) for i in range(HIGH)])]
    pallas_call x2 -> x3, Pallas kernels: 7.77 us -> 8.35 us  [the longest x1 6.57 us: shards(): call(backward_kernel, 'ssvvvvvvvv', [big, (s((half, width), F32), 'v'), h...]
  transfers between devices with their start and end apart: 10 -> 10, of which waited for: 6 -> 6; matrix products, arithmetic and copies ran while one was open for 0% -> 0% of each run, Pallas kernels for 2% -> 3%
where the time goes in v6:
time: 108 us; the launch traced here: 107 us
  blocking collectives  40.8 us (38%)
  starting transfers between devices  32.2 us (30%)
  Pallas kernels  14.7 us (14%)
  waiting for transfers between devices  14.7 us (14%)
  between operations  2.06 us (2%)
  other arithmetic  1.38 us (1%)
  local copies, waits for them, and re-layouts  1.33 us (1%)
    all_to_all x3, blocking collectives, exchange(): return lax.all_to_all(parts, 'plane', 0, 0).reshape(rows, value.shape[-1])  40.8 us
    ppermute x6, starting transfers between devices, from_up(): lax.ppermute(value, 'high', [((i + k) % HIGH, i) for i in range(HIGH)])  16.1 us
    ppermute x1, waiting for transfers between devices, shards(): got = lax.ppermute(pair, 'cand', swap_chip)  9.63 us
    ppermute x1, starting transfers between devices, shards(): got = lax.ppermute(other, 'cand', swap_core)  7.33 us
    pallas_call x1, Pallas kernels, shards(): call(backward_kernel, 'ssvvvvvvvv', [big, (s((half, width), F32), 'v'), h...  6.57 us
    all_to_all x1, starting transfers between devices, shards(): lax.all_to_all(dq.reshape(plane * HIGH, own, width), ('plane', 'high'), 0...  5.69 us
    ppermute x6, waiting for transfers between devices, from_up(): lax.ppermute(value, 'high', [((i + k) % HIGH, i) for i in range(HIGH)])  3.56 us
    pallas_call x1, Pallas kernels, shards(): call(forward_kernel, 'ssvvvv', [wide, wide, big, big], flops=1 << 31)  3.25 us
  transfers between devices with their start and end apart: 10, of which 6 were waited for; matrix products, arithmetic and copies ran while one was open for 0% of the time, Pallas kernels for 3%

profile of v6, /device:TPU:1, one launch (start us, length us, event | category | flops | bytes accessed | tf_op | source)
XLA Modules:
  0.0 107.2 jit_solution(6661265034077407917)
XLA Ops:
  0.6 0.7 convert_element_type.4
  1.3 0.1 broadcast_in_dim.2
  1.4 0.7 pad_maximum_fusion.own_ref
  2.1 6.8 %collective-permute-start = (bf16[8,1152]{1,0:T(8,128)(2,1)S(1)}, bf16[8,1152]{1,0:T(8,128)(2,1)S(1)}, u32[]{:S(2)}, u32[]{:S(2)}) collective-permute-start(bf16[8,1152]{1,0:T(8,128)(2,1)S(1)} %pad_maximum_fusion.own_ref), channel_id=1, source_target_pairs={{4,0},{8,4},{12,8},{0,12},{5,1},{9,5},{13,9},{1,13},{6,2},{10,6},{... | collective-permute-start | bytes 55304 | tf_op jit(solution)/shard_map/ppermute | solution.py:237
  8.9 0.9 collective-permute-start.1
  9.8 2.4 %collective-permute-start.2 = (bf16[8,1152]{1,0:T(8,128)(2,1)S(1)}, bf16[8,1152]{1,0:T(8,128)(2,1)S(1)}, u32[]{:S(2)}, u32[]{:S(2)}) collective-permute-start(bf16[8,1152]{1,0:T(8,128)(2,1)S(1)} %pad_maximum_fusion.own_ref), channel_id=1, source_target_pairs={{12,0},{0,4},{4,8},{8,12},{13,1},{1,5},{5,9},{9,13},{14,2},{2,6},{... | collective-permute-start | bytes 55304 | tf_op jit(solution)/shard_map/ppermute | solution.py:237
  13.5 1.2 %copy-done.2 = bf16[512,1024]{1,0:T(8,128)(2,1)S(1)} copy-done((bf16[512,1024]{1,0:T(8,128)(2,1)S(1)}, bf16[512,1024]{1,0:T(8,128)(2,1)}, u32[]{:S(2)}) %copy-start.2) | copy-done | bytes 1048600
  14.7 0.7 collective-permute-done.1.two_ref
  15.5 17.2 %all_to_all.20 = bf16[16,32,640]{2,1,0:T(8,128)(2,1)S(1)} all-to-all(bf16[16,32,640]{2,1,0:T(8,128)(2,1)S(1)} %get-tuple-element.22), channel_id=1, replica_groups=mesh['plane'=16,'high'=4,'cand'=4] {'plane'}, dimensions={0} | all-to-all | bytes 1310720 | tf_op jit(solution)/shard_map/all_to_all | solution.py:241
  32.8 3.3 %shard_map.123 = (bf16[4,1024,128]{2,1,0:T(8,128)(2,1)S(1)}, bf16[4,1024,128]{2,1,0:T(8,128)(2,1)S(1)}, bf16[512,512]{1,0:T(8,128)(2,1)S(1)}, bf16[512,512]{1,0:T(8,128)(2,1)S(1)}) custom-call(s32[1]{0:T(128)S(6)} %copy.13.rest_0_.user_ref, s32[1]{0:T(128)S(6)} %copy.14.rest_1_.length_ref, bf16[512,640]{1,0:T(8,128)(2,1)S(1)} %bitcast.10, ...), custom_call_target="tpu_custom_call" | custom-call | flops 2147483648 | bytes 1048576 | tf_op jit(solution)/shard_map/pallas_call | solution.py:266
  36.1 11.9 %all_to_all.21 = bf16[16,32,512]{2,1,0:T(8,128)(2,1)S(1)} all-to-all(bf16[16,32,512]{2,1,0:T(8,128)(2,1)S(1)} %bitcast.13), channel_id=1, replica_groups=mesh['plane'=16,'high'=4,'cand'=4] {'plane'}, dimensions={0} | all-to-all | bytes 1048576 | tf_op jit(solution)/shard_map/all_to_all | solution.py:241
  47.9 0.1 shard_map.124.own_ref
  48.0 1.5 %collective-permute-start.3 = (bf16[32,512]{1,0:T(8,128)(2,1)S(1)}, bf16[32,512]{1,0:T(8,128)(2,1)S(1)}, u32[]{:S(2)}, u32[]{:S(2)}) collective-permute-start(bf16[32,512]{1,0:T(8,128)(2,1)S(1)} %shard_map.124.own_ref), channel_id=1, source_target_pairs={{4,0},{8,4},{12,8},{0,12},{5,1},{9,5},{13,9},{1,13},{6,2},{10,6},{... | collective-permute-start | bytes 98312 | tf_op jit(solution)/shard_map/ppermute | solution.py:237
  49.5 4.3 %collective-permute-start.4 = (bf16[32,512]{1,0:T(8,128)(2,1)S(1)}, bf16[32,512]{1,0:T(8,128)(2,1)S(1)}, u32[]{:S(2)}, u32[]{:S(2)}) collective-permute-start(bf16[32,512]{1,0:T(8,128)(2,1)S(1)} %shard_map.124.own_ref), channel_id=1, source_target_pairs={{8,0},{12,4},{0,8},{4,12},{9,1},{13,5},{1,9},{5,13},{10,2},{14,6},... | collective-permute-start | bytes 98312 | tf_op jit(solution)/shard_map/ppermute | solution.py:237
  53.8 0.2 collective-permute-start.5
  54.0 0.3 shard_map.125
  54.4 1.5 %shard_map.126 = (bf16[2,1024,512]{2,1,0:T(8,128)(2,1)S(1)}, bf16[2,1024,512]{2,1,0:T(8,128)(2,1)S(1)}) custom-call(bf16[512,512]{1,0:T(8,128)(2,1)S(1)} %get-tuple-element.28.query_ref, bf16[4,1024,128]{2,1,0:T(8,128)(2,1)S(1)} %get-tuple-element.29.key_ref), custom_call_target="tpu_custom_call" | custom-call | flops 268435456 | bytes 1048576 | tf_op jit(solution)/shard_map/pallas_call | solution.py:271
  55.8 0.3 collective-permute-done.4.two_ref
  56.1 2.5 %collective-permute-done.5.three_ref = bf16[32,512]{1,0:T(8,128)(2,1)S(1)} collective-permute-done((bf16[32,512]{1,0:T(8,128)(2,1)S(1)}, bf16[32,512]{1,0:T(8,128)(2,1)S(1)}, u32[]{:S(2)}, u32[]{:S(2)}) %collective-permute-start.5) | collective-permute-done | bytes 32800 | tf_op jit(solution)/shard_map/ppermute | solution.py:237
  58.7 0.3 shard_map.127
  59.0 11.7 %all_to_all.22 = bf16[16,32,512]{2,1,0:T(8,128)(2,1)S(1)} all-to-all(bf16[16,32,512]{2,1,0:T(8,128)(2,1)S(1)} %get-tuple-element.34), channel_id=1, replica_groups=mesh['plane'=16,'high'=4,'cand'=4] {'plane'}, dimensions={0} | all-to-all | bytes 1048576 | tf_op jit(solution)/shard_map/all_to_all | solution.py:241
  70.7 6.6 %shard_map.129 = (bf16[512,512]{1,0:T(8,128)(2,1)}, f32[256,512]{1,0:T(8,128)S(1)}, bf16[256,512]{1,0:T(8,128)(2,1)S(1)}) custom-call(s32[1]{0:T(128)S(6)} %copy.13.rest_0_.user_ref, s32[1]{0:T(128)} %bitcast.1.rest_2_.core_ref, bf16[512,640]{1,0:T(8,128)(2,1)S(1)} %bitcast.11, bf16[512,512]{1,0:T(8,128)(2,1)S(1)} %get-tuple-element.28.query_ref, ...), custom_call_target="tpu_custom_call" | custom-call | flops 4294967296 | bytes 1048576 | tf_op jit(solution)/shard_map/pallas_call | solution.py:282
  77.2 5.7 %all-to-all-start.3 = ((bf16[64,8,512]{2,1,0:T(8,128)(2,1)}), bf16[64,8,512]{2,1,0:T(8,128)(2,1)S(1)}, u32[]{:S(2)}, u32[]{:S(2)}) async-start(bf16[64,8,512]{2,1,0:T(8,128)(2,1)} %bitcast.6), calls=%async_computation.3 | async-start | bytes 1048576 | tf_op jit(solution)/shard_map/all_to_all | solution.py:289
  82.9 7.3 %collective-permute-start.6 = (bf16[256,512]{1,0:T(8,128)(2,1)S(1)}, bf16[256,512]{1,0:T(8,128)(2,1)S(1)}, u32[]{:S(2)}, u32[]{:S(2)}) collective-permute-start(bf16[256,512]{1,0:T(8,128)(2,1)S(1)} %get-tuple-element.38), channel_id=1, source_target_pairs={{0,1},{1,0},{2,3},{3,2},{4,5},{5,4},{6,7},{7,6},{8,9},{9,8},{10,11... | collective-permute-start | bytes 786440 | tf_op jit(solution)/shard_map/ppermute | solution.py:294
  90.3 1.2 %collective-permute-done.6.two_ref = bf16[256,512]{1,0:T(8,128)(2,1)S(1)} collective-permute-done((bf16[256,512]{1,0:T(8,128)(2,1)S(1)}, bf16[256,512]{1,0:T(8,128)(2,1)S(1)}, u32[]{:S(2)}, u32[]{:S(2)}) %collective-permute-start.6) | collective-permute-done | bytes 262176 | tf_op jit(solution)/shard_map/ppermute | solution.py:294
  91.5 1.2 %collective-permute-start.7 = (bf16[256,512]{1,0:T(8,128)(2,1)S(1)}, bf16[256,512]{1,0:T(8,128)(2,1)S(1)}, u32[]{:S(2)}, u32[]{:S(2)}) collective-permute-start(bf16[256,512]{1,0:T(8,128)(2,1)S(1)} %shard_map.130.one_ref), channel_id=1, source_target_pairs={{0,2},{1,3},{2,0},{3,1},{4,6},{5,7},{6,4},{7,5},{8,10},{9,11},{10,... | collective-permute-start | bytes 786440 | tf_op jit(solution)/shard_map/ppermute | solution.py:296
  92.7 9.6 %collective-permute-done.7.two_ref = bf16[256,512]{1,0:T(8,128)(2,1)S(1)} collective-permute-done((bf16[256,512]{1,0:T(8,128)(2,1)S(1)}, bf16[256,512]{1,0:T(8,128)(2,1)S(1)}, u32[]{:S(2)}, u32[]{:S(2)}) %collective-permute-start.7) | collective-permute-done | bytes 262176 | tf_op jit(solution)/shard_map/ppermute | solution.py:296
  102.4 1.9 %collective-permute-start.8 = (bf16[256,512]{1,0:T(8,128)(2,1)S(1)}, bf16[256,512]{1,0:T(8,128)(2,1)S(1)}, u32[]{:S(2)}, u32[]{:S(2)}) collective-permute-start(bf16[256,512]{1,0:T(8,128)(2,1)S(1)} %shard_map.131.mine_ref), channel_id=1, source_target_pairs={{0,1},{1,0},{2,3},{3,2},{4,5},{5,4},{6,7},{7,6},{8,9},{9,8},{10,11... | collective-permute-start | bytes 786440 | tf_op jit(solution)/shard_map/ppermute | solution.py:298
  104.3 0.8 shard_map.128
  105.1 0.4 collective-permute-done.8.other_ref
  105.4 0.8 shard_map.132
  106.2 0.9 shard_map.133
  (23 shorter events, 0.2 us)
Async XLA Ops:
  2.1 12.7 %collective-permute-start = (bf16[8,1152]{1,0:T(8,128)(2,1)S(1)}, bf16[8,1152]{1,0:T(8,128)(2,1)S(1)}, u32[]{:S(2)}, u32[]{:S(2)}) collective-permute-start(bf16[8,1152]{1,0:T(8,128)(2,1)S(1)} %pad_maximum_fusion.own_ref), channel_id=1, source_target_pairs={{4,0},{8,4},{12,8},{0,12},{5,1},{9,5},{13,9},{1,13},{6,2},{10,6},{... | collective-permute-start | bytes 55304 | tf_op jit(solution)/shard_map/ppermute | solution.py:237
  8.9 6.5 %collective-permute-start.1 = (bf16[8,1152]{1,0:T(8,128)(2,1)S(1)}, bf16[8,1152]{1,0:T(8,128)(2,1)S(1)}, u32[]{:S(2)}, u32[]{:S(2)}) collective-permute-start(bf16[8,1152]{1,0:T(8,128)(2,1)S(1)} %pad_maximum_fusion.own_ref), channel_id=1, source_target_pairs={{8,0},{12,4},{0,8},{4,12},{9,1},{13,5},{1,9},{5,13},{10,2},{14,6},... | collective-permute-start | bytes 55304 | tf_op jit(solution)/shard_map/ppermute | solution.py:237
  9.8 5.6 %collective-permute-start.2 = (bf16[8,1152]{1,0:T(8,128)(2,1)S(1)}, bf16[8,1152]{1,0:T(8,128)(2,1)S(1)}, u32[]{:S(2)}, u32[]{:S(2)}) collective-permute-start(bf16[8,1152]{1,0:T(8,128)(2,1)S(1)} %pad_maximum_fusion.own_ref), channel_id=1, source_target_pairs={{12,0},{0,4},{4,8},{8,12},{13,1},{1,5},{5,9},{9,13},{14,2},{2,6},{... | collective-permute-start | bytes 55304 | tf_op jit(solution)/shard_map/ppermute | solution.py:237
  13.5 1.2 %copy-start.2 = (bf16[512,1024]{1,0:T(8,128)(2,1)S(1)}, bf16[512,1024]{1,0:T(8,128)(2,1)}, u32[]{:S(2)}) copy-start(bf16[512,1024]{1,0:T(8,128)(2,1)} %kvw_ref.3) | copy-start | bytes 3145732
  14.7 18.1 %copy-start.3 = (bf16[512,1024]{1,0:T(8,128)(2,1)S(1)}, bf16[512,1024]{1,0:T(8,128)(2,1)}, u32[]{:S(2)}) copy-start(bf16[512,1024]{1,0:T(8,128)(2,1)} %kvw_ref.3) | copy-start | bytes 3145732
  14.7 18.1 %copy-start.4 = (bf16[512,512]{1,0:T(8,128)(2,1)S(1)}, bf16[512,512]{1,0:T(8,128)(2,1)}, u32[]{:S(2)}) copy-start(bf16[512,512]{1,0:T(8,128)(2,1)} %weight_ref.3) | copy-start | bytes 1572868
  14.7 18.1 %copy-start.7 = (bf16[512,512]{1,0:T(8,128)(2,1)S(1)}, bf16[512,512]{1,0:T(8,128)(2,1)}, u32[]{:S(2)}) copy-start(bf16[512,512]{1,0:T(8,128)(2,1)} %hist_ref.1) | copy-start | bytes 1572868
  32.8 21.2 %copy-start = (bf16[512,512]{1,0:T(8,128)(2,1)S(1)}, bf16[512,512]{1,0:T(8,128)(2,1)}, u32[]{:S(2)}) copy-start(bf16[512,512]{1,0:T(8,128)(2,1)} %unit_ref.3) | copy-start | bytes 1572868
  32.8 21.2 %copy-start.1 = (bf16[512,512]{1,0:T(8,128)(2,1)S(1)}, bf16[512,512]{1,0:T(8,128)(2,1)}, u32[]{:S(2)}) copy-start(bf16[512,512]{1,0:T(8,128)(2,1)} %out_ref.3) | copy-start | bytes 1572868
  48.0 7.8 %collective-permute-start.3 = (bf16[32,512]{1,0:T(8,128)(2,1)S(1)}, bf16[32,512]{1,0:T(8,128)(2,1)S(1)}, u32[]{:S(2)}, u32[]{:S(2)}) collective-permute-start(bf16[32,512]{1,0:T(8,128)(2,1)S(1)} %shard_map.124.own_ref), channel_id=1, source_target_pairs={{4,0},{8,4},{12,8},{0,12},{5,1},{9,5},{13,9},{1,13},{6,2},{10,6},{... | collective-permute-start | bytes 98312 | tf_op jit(solution)/shard_map/ppermute | solution.py:237
  49.5 6.7 %collective-permute-start.4 = (bf16[32,512]{1,0:T(8,128)(2,1)S(1)}, bf16[32,512]{1,0:T(8,128)(2,1)S(1)}, u32[]{:S(2)}, u32[]{:S(2)}) collective-permute-start(bf16[32,512]{1,0:T(8,128)(2,1)S(1)} %shard_map.124.own_ref), channel_id=1, source_target_pairs={{8,0},{12,4},{0,8},{4,12},{9,1},{13,5},{1,9},{5,13},{10,2},{14,6},... | collective-permute-start | bytes 98312 | tf_op jit(solution)/shard_map/ppermute | solution.py:237
  53.8 4.9 %collective-permute-start.5 = (bf16[32,512]{1,0:T(8,128)(2,1)S(1)}, bf16[32,512]{1,0:T(8,128)(2,1)S(1)}, u32[]{:S(2)}, u32[]{:S(2)}) collective-permute-start(bf16[32,512]{1,0:T(8,128)(2,1)S(1)} %shard_map.124.own_ref), channel_id=1, source_target_pairs={{12,0},{0,4},{4,8},{8,12},{13,1},{1,5},{5,9},{9,13},{14,2},{2,6},{... | collective-permute-start | bytes 98312 | tf_op jit(solution)/shard_map/ppermute | solution.py:237
  77.2 27.0 %copy-start.5 = (bf16[8,512]{1,0:T(8,128)(2,1)S(1)}, bf16[8,512]{1,0:T(8,128)(2,1)}, u32[]{:S(2)}) copy-start(bf16[8,512]{1,0:T(8,128)(2,1)} %embed_ref.1) | copy-start | bytes 24580
  77.2 27.0 %copy-start.6 = (bf16[8,512]{1,0:T(8,128)(2,1)S(1)}, bf16[8,512]{1,0:T(8,128)(2,1)}, u32[]{:S(2)}) copy-start(bf16[8,512]{1,0:T(8,128)(2,1)} %grad_ref.1) | copy-start | bytes 24580
  77.2 29.0 %all-to-all-start.3 = ((bf16[64,8,512]{2,1,0:T(8,128)(2,1)}), bf16[64,8,512]{2,1,0:T(8,128)(2,1)S(1)}, u32[]{:S(2)}, u32[]{:S(2)}) async-start(bf16[64,8,512]{2,1,0:T(8,128)(2,1)} %bitcast.6), calls=%async_computation.3 | async-start | bytes 1048576 | tf_op jit(solution)/shard_map/all_to_all | solution.py:289
  82.9 8.5 %collective-permute-start.6 = (bf16[256,512]{1,0:T(8,128)(2,1)S(1)}, bf16[256,512]{1,0:T(8,128)(2,1)S(1)}, u32[]{:S(2)}, u32[]{:S(2)}) collective-permute-start(bf16[256,512]{1,0:T(8,128)(2,1)S(1)} %get-tuple-element.38), channel_id=1, source_target_pairs={{0,1},{1,0},{2,3},{3,2},{4,5},{5,4},{6,7},{7,6},{8,9},{9,8},{10,11... | collective-permute-start | bytes 786440 | tf_op jit(solution)/shard_map/ppermute | solution.py:294
  91.5 10.8 %collective-permute-start.7 = (bf16[256,512]{1,0:T(8,128)(2,1)S(1)}, bf16[256,512]{1,0:T(8,128)(2,1)S(1)}, u32[]{:S(2)}, u32[]{:S(2)}) collective-permute-start(bf16[256,512]{1,0:T(8,128)(2,1)S(1)} %shard_map.130.one_ref), channel_id=1, source_target_pairs={{0,2},{1,3},{2,0},{3,1},{4,6},{5,7},{6,4},{7,5},{8,10},{9,11},{10,... | collective-permute-start | bytes 786440 | tf_op jit(solution)/shard_map/ppermute | solution.py:296
  102.4 3.0 %collective-permute-start.8 = (bf16[256,512]{1,0:T(8,128)(2,1)S(1)}, bf16[256,512]{1,0:T(8,128)(2,1)S(1)}, u32[]{:S(2)}, u32[]{:S(2)}) collective-permute-start(bf16[256,512]{1,0:T(8,128)(2,1)S(1)} %shard_map.131.mine_ref), channel_id=1, source_target_pairs={{0,1},{1,0},{2,3},{3,2},{4,5},{5,4},{6,7},{7,6},{8,9},{9,8},{10,11... | collective-permute-start | bytes 786440 | tf_op jit(solution)/shard_map/ppermute | solution.py:298

commit v7 on v6

--- a/solution.py
+++ b/solution.py
@@ -198,20 +198,18 @@
     rest[-1][...] = (one_ref[...].astype(F32) + two_ref[...].astype(F32)).astype(BF16)
 
 
-def halves_kernel(core_ref, mine_ref, other_ref, out_hbm, sems):
+def final_kernel(core_ref, mine_ref, other_ref, part_ref, base_ref, weight_ref, out_hbm, result_ref, sems):
     half = mine_ref.shape[0]
     core = core_ref[0]
     mine = out_hbm.at[pl.ds(pl.multiple_of(core * half, half), half)]
     other = out_hbm.at[pl.ds(pl.multiple_of((1 - core) * half, half), half)]
-    for copy in start(sems, (mine_ref, mine), (other_ref, other)):
-        copy.wait()
-
-
-def final_kernel(part_ref, base_ref, weight_ref, result_ref):
+    copies = start(sems, (mine_ref, mine), (other_ref, other))
     own, width = base_ref.shape
     parts = part_ref.shape[0] // own
     dq = jnp.sum(part_ref[...].astype(F32).reshape(parts, own, width), axis=0) * 0.0625
     result_ref[...] = (base_ref[...] + nt(dq.astype(BF16), weight_ref[...])).astype(BF16)
+    for copy in copies:
+        copy.wait()
 
 
 def shards(
@@ -294,12 +292,11 @@
     got = lax.ppermute(other, "cand", swap_core)
     pair = call(add_kernel, "vv", [half_b16])(mine, got)[0]
     got = lax.ppermute(pair, "cand", swap_chip)
-    quad = call(add_kernel, "vv", [half_b16])(pair, got)[0]
+    quad = call(add_kernel, "vva", [half_b16])(pair, got, base)[0]
     got = lax.ppermute(quad, "cand", swap_core)
-    history_grad = call(halves_kernel, "svv", [(s((events, width), BF16), "h")], [sems((2,))])(
-        core, quad, got
-    )[0]
-    candidate_grad = call(final_kernel, "v" * 3, [own_b16], flops=1 << 26)(dq_all, base, query_weight)[0]
+    history_grad, candidate_grad = call(
+        final_kernel, "svvvvv", [(s((events, width), BF16), "h"), own_b16], [sems((2,))], flops=1 << 26
+    )(core, quad, got, dq_all, base, query_weight)
     return (candidate_output, history_grad, candidate_grad)
 
 

time: 108 us -> 108 us (level)
  no operation moved by 1% of the time
where the time goes in v7:
time: 108 us; the launch traced here: 107 us
  blocking collectives  40.8 us (38%)
  starting transfers between devices  32.2 us (30%)
  waiting for transfers between devices  14.7 us (14%)
  Pallas kernels  14.4 us (13%)
  between operations  2.2 us (2%)
  other arithmetic  1.38 us (1%)
  local copies, waits for them, and re-layouts  1.33 us (1%)
    all_to_all x3, blocking collectives, exchange(): return lax.all_to_all(parts, 'plane', 0, 0).reshape(rows, value.shape[-1])  40.8 us
    ppermute x6, starting transfers between devices, from_up(): lax.ppermute(value, 'high', [((i + k) % HIGH, i) for i in range(HIGH)])  16.1 us
    ppermute x1, waiting for transfers between devices, shards(): got = lax.ppermute(pair, 'cand', swap_chip)  8.84 us
    ppermute x1, starting transfers between devices, shards(): got = lax.ppermute(other, 'cand', swap_core)  7.33 us
    pallas_call x1, Pallas kernels, shards(): call(backward_kernel, 'ssvvvvvvvv', [big, (s((half, width), F32), 'v'), h...  6.56 us
    all_to_all x1, starting transfers between devices, shards(): lax.all_to_all(dq.reshape(plane * HIGH, own, width), ('plane', 'high'), 0...  5.69 us
    ppermute x6, waiting for transfers between devices, from_up(): lax.ppermute(value, 'high', [((i + k) % HIGH, i) for i in range(HIGH)])  3.56 us
    pallas_call x1, Pallas kernels, shards(): call(forward_kernel, 'ssvvvv', [wide, wide, big, big], flops=1 << 31)  3.25 us
  transfers between devices with their start and end apart: 10, of which 6 were waited for; matrix products, arithmetic and copies ran while one was open for 0% of the time, Pallas kernels for 3%

profile of v7, /device:TPU:1, one launch (start us, length us, event | category | flops | bytes accessed | tf_op | source)
XLA Modules:
  0.0 107.0 jit_solution(18031123814707423956)
XLA Ops:
  0.6 0.7 convert_element_type.4
  1.3 0.1 broadcast_in_dim.2
  1.4 0.7 pad_maximum_fusion.own_ref
  2.1 6.8 %collective-permute-start = (bf16[8,1152]{1,0:T(8,128)(2,1)S(1)}, bf16[8,1152]{1,0:T(8,128)(2,1)S(1)}, u32[]{:S(2)}, u32[]{:S(2)}) collective-permute-start(bf16[8,1152]{1,0:T(8,128)(2,1)S(1)} %pad_maximum_fusion.own_ref), channel_id=1, source_target_pairs={{4,0},{8,4},{12,8},{0,12},{5,1},{9,5},{13,9},{1,13},{6,2},{10,6},{... | collective-permute-start | bytes 55304 | tf_op jit(solution)/shard_map/ppermute | solution.py:235
  8.9 0.9 collective-permute-start.1
  9.8 2.4 %collective-permute-start.2 = (bf16[8,1152]{1,0:T(8,128)(2,1)S(1)}, bf16[8,1152]{1,0:T(8,128)(2,1)S(1)}, u32[]{:S(2)}, u32[]{:S(2)}) collective-permute-start(bf16[8,1152]{1,0:T(8,128)(2,1)S(1)} %pad_maximum_fusion.own_ref), channel_id=1, source_target_pairs={{12,0},{0,4},{4,8},{8,12},{13,1},{1,5},{5,9},{9,13},{14,2},{2,6},{... | collective-permute-start | bytes 55304 | tf_op jit(solution)/shard_map/ppermute | solution.py:235
  13.5 1.2 %copy-done.2 = bf16[512,1024]{1,0:T(8,128)(2,1)S(1)} copy-done((bf16[512,1024]{1,0:T(8,128)(2,1)S(1)}, bf16[512,1024]{1,0:T(8,128)(2,1)}, u32[]{:S(2)}) %copy-start.2) | copy-done | bytes 1048600
  14.7 0.7 collective-permute-done.1.two_ref
  15.5 0.1 shard_map.122
  15.5 17.2 %all_to_all.20 = bf16[16,32,640]{2,1,0:T(8,128)(2,1)S(1)} all-to-all(bf16[16,32,640]{2,1,0:T(8,128)(2,1)S(1)} %get-tuple-element.24), channel_id=1, replica_groups=mesh['plane'=16,'high'=4,'cand'=4] {'plane'}, dimensions={0} | all-to-all | bytes 1310720 | tf_op jit(solution)/shard_map/all_to_all | solution.py:239
  32.8 3.3 %shard_map.123 = (bf16[4,1024,128]{2,1,0:T(8,128)(2,1)S(1)}, bf16[4,1024,128]{2,1,0:T(8,128)(2,1)S(1)}, bf16[512,512]{1,0:T(8,128)(2,1)S(1)}, bf16[512,512]{1,0:T(8,128)(2,1)S(1)}) custom-call(s32[1]{0:T(128)S(6)} %copy.13.rest_0_.user_ref, s32[1]{0:T(128)S(6)} %copy.14.rest_1_.length_ref, bf16[512,640]{1,0:T(8,128)(2,1)S(1)} %bitcast.10, ...), custom_call_target="tpu_custom_call" | custom-call | flops 2147483648 | bytes 1048576 | tf_op jit(solution)/shard_map/pallas_call | solution.py:264
  36.1 11.9 %all_to_all.21 = bf16[16,32,512]{2,1,0:T(8,128)(2,1)S(1)} all-to-all(bf16[16,32,512]{2,1,0:T(8,128)(2,1)S(1)} %bitcast.13), channel_id=1, replica_groups=mesh['plane'=16,'high'=4,'cand'=4] {'plane'}, dimensions={0} | all-to-all | bytes 1048576 | tf_op jit(solution)/shard_map/all_to_all | solution.py:239
  47.9 0.1 shard_map.124.own_ref
  48.0 1.5 %collective-permute-start.3 = (bf16[32,512]{1,0:T(8,128)(2,1)S(1)}, bf16[32,512]{1,0:T(8,128)(2,1)S(1)}, u32[]{:S(2)}, u32[]{:S(2)}) collective-permute-start(bf16[32,512]{1,0:T(8,128)(2,1)S(1)} %shard_map.124.own_ref), channel_id=1, source_target_pairs={{4,0},{8,4},{12,8},{0,12},{5,1},{9,5},{13,9},{1,13},{6,2},{10,6},{... | collective-permute-start | bytes 98312 | tf_op jit(solution)/shard_map/ppermute | solution.py:235
  49.5 4.3 %collective-permute-start.4 = (bf16[32,512]{1,0:T(8,128)(2,1)S(1)}, bf16[32,512]{1,0:T(8,128)(2,1)S(1)}, u32[]{:S(2)}, u32[]{:S(2)}) collective-permute-start(bf16[32,512]{1,0:T(8,128)(2,1)S(1)} %shard_map.124.own_ref), channel_id=1, source_target_pairs={{8,0},{12,4},{0,8},{4,12},{9,1},{13,5},{1,9},{5,13},{10,2},{14,6},... | collective-permute-start | bytes 98312 | tf_op jit(solution)/shard_map/ppermute | solution.py:235
  53.8 0.2 collective-permute-start.5
  54.0 0.3 shard_map.125
  54.4 1.5 %shard_map.126 = (bf16[2,1024,512]{2,1,0:T(8,128)(2,1)S(1)}, bf16[2,1024,512]{2,1,0:T(8,128)(2,1)S(1)}) custom-call(bf16[512,512]{1,0:T(8,128)(2,1)S(1)} %get-tuple-element.30.query_ref, bf16[4,1024,128]{2,1,0:T(8,128)(2,1)S(1)} %get-tuple-element.31.key_ref), custom_call_target="tpu_custom_call" | custom-call | flops 268435456 | bytes 1048576 | tf_op jit(solution)/shard_map/pallas_call | solution.py:269
  55.8 0.3 collective-permute-done.4.two_ref
  56.1 2.5 %collective-permute-done.5.three_ref = bf16[32,512]{1,0:T(8,128)(2,1)S(1)} collective-permute-done((bf16[32,512]{1,0:T(8,128)(2,1)S(1)}, bf16[32,512]{1,0:T(8,128)(2,1)S(1)}, u32[]{:S(2)}, u32[]{:S(2)}) %collective-permute-start.5) | collective-permute-done | bytes 32800 | tf_op jit(solution)/shard_map/ppermute | solution.py:235
  58.7 0.3 shard_map.127
  59.0 11.7 %all_to_all.22 = bf16[16,32,512]{2,1,0:T(8,128)(2,1)S(1)} all-to-all(bf16[16,32,512]{2,1,0:T(8,128)(2,1)S(1)} %get-tuple-element.36), channel_id=1, replica_groups=mesh['plane'=16,'high'=4,'cand'=4] {'plane'}, dimensions={0} | all-to-all | bytes 1048576 | tf_op jit(solution)/shard_map/all_to_all | solution.py:239
  70.7 6.6 %shard_map.129 = (bf16[512,512]{1,0:T(8,128)(2,1)}, f32[256,512]{1,0:T(8,128)S(1)}, bf16[256,512]{1,0:T(8,128)(2,1)S(1)}) custom-call(s32[1]{0:T(128)S(6)} %copy.13.rest_0_.user_ref, s32[1]{0:T(128)} %bitcast.1.rest_2_.core_ref, bf16[512,640]{1,0:T(8,128)(2,1)S(1)} %bitcast.11, bf16[512,512]{1,0:T(8,128)(2,1)S(1)} %get-tuple-element.30.query_ref, ...), custom_call_target="tpu_custom_call" | custom-call | flops 4294967296 | bytes 1048576 | tf_op jit(solution)/shard_map/pallas_call | solution.py:280
  77.2 5.7 %all-to-all-start.3 = ((bf16[64,8,512]{2,1,0:T(8,128)(2,1)}), bf16[64,8,512]{2,1,0:T(8,128)(2,1)S(1)}, u32[]{:S(2)}, u32[]{:S(2)}) async-start(bf16[64,8,512]{2,1,0:T(8,128)(2,1)} %bitcast.6), calls=%async_computation.3 | async-start | bytes 1048576 | tf_op jit(solution)/shard_map/all_to_all | solution.py:287
  82.9 7.3 %collective-permute-start.6 = (bf16[256,512]{1,0:T(8,128)(2,1)S(1)}, bf16[256,512]{1,0:T(8,128)(2,1)S(1)}, u32[]{:S(2)}, u32[]{:S(2)}) collective-permute-start(bf16[256,512]{1,0:T(8,128)(2,1)S(1)} %get-tuple-element.40), channel_id=1, source_target_pairs={{0,1},{1,0},{2,3},{3,2},{4,5},{5,4},{6,7},{7,6},{8,9},{9,8},{10,11... | collective-permute-start | bytes 786440 | tf_op jit(solution)/shard_map/ppermute | solution.py:292
  90.3 1.2 %collective-permute-done.6.two_ref = bf16[256,512]{1,0:T(8,128)(2,1)S(1)} collective-permute-done((bf16[256,512]{1,0:T(8,128)(2,1)S(1)}, bf16[256,512]{1,0:T(8,128)(2,1)S(1)}, u32[]{:S(2)}, u32[]{:S(2)}) %collective-permute-start.6) | collective-permute-done | bytes 262176 | tf_op jit(solution)/shard_map/ppermute | solution.py:292
  91.5 1.2 %collective-permute-start.7 = (bf16[256,512]{1,0:T(8,128)(2,1)S(1)}, bf16[256,512]{1,0:T(8,128)(2,1)S(1)}, u32[]{:S(2)}, u32[]{:S(2)}) collective-permute-start(bf16[256,512]{1,0:T(8,128)(2,1)S(1)} %shard_map.130.one_ref), channel_id=1, source_target_pairs={{0,2},{1,3},{2,0},{3,1},{4,6},{5,7},{6,4},{7,5},{8,10},{9,11},{10,... | collective-permute-start | bytes 786440 | tf_op jit(solution)/shard_map/ppermute | solution.py:294
  92.7 0.8 shard_map.128
  93.5 8.8 %collective-permute-done.7.two_ref = bf16[256,512]{1,0:T(8,128)(2,1)S(1)} collective-permute-done((bf16[256,512]{1,0:T(8,128)(2,1)S(1)}, bf16[256,512]{1,0:T(8,128)(2,1)S(1)}, u32[]{:S(2)}, u32[]{:S(2)}) %collective-permute-start.7) | collective-permute-done | bytes 262176 | tf_op jit(solution)/shard_map/ppermute | solution.py:294
  102.4 1.9 %collective-permute-start.8 = (bf16[256,512]{1,0:T(8,128)(2,1)S(1)}, bf16[256,512]{1,0:T(8,128)(2,1)S(1)}, u32[]{:S(2)}, u32[]{:S(2)}) collective-permute-start(bf16[256,512]{1,0:T(8,128)(2,1)S(1)} %shard_map.131.mine_ref), channel_id=1, source_target_pairs={{0,1},{1,0},{2,3},{3,2},{4,5},{5,4},{6,7},{7,6},{8,9},{9,8},{10,11... | collective-permute-start | bytes 786440 | tf_op jit(solution)/shard_map/ppermute | solution.py:296
  104.3 1.2 %collective-permute-done.8.other_ref = bf16[256,512]{1,0:T(8,128)(2,1)S(1)} collective-permute-done((bf16[256,512]{1,0:T(8,128)(2,1)S(1)}, bf16[256,512]{1,0:T(8,128)(2,1)S(1)}, u32[]{:S(2)}, u32[]{:S(2)}) %collective-permute-start.8) | collective-permute-done | bytes 262176 | tf_op jit(solution)/shard_map/ppermute | solution.py:296
  105.4 1.5 %shard_map.132 = (bf16[512,512]{1,0:T(8,128)(2,1)}, bf16[8,512]{1,0:T(8,128)(2,1)}) custom-call(s32[1]{0:T(128)} %bitcast.1.rest_2_.core_ref, bf16[256,512]{1,0:T(8,128)(2,1)S(1)} %shard_map.131.mine_ref, bf16[256,512]{1,0:T(8,128)(2,1)S(1)} %collective-permute-done.8.other_ref, bf16[512,512]{1,0:T(8,128)(2,1)S(1)} %bitcast.8, ...), custom_call_target="tpu_custom_call" | custom-call | flops 67108864 | bytes 1048576 | tf_op jit(solution)/shard_map/pallas_call | solution.py:297
  (22 shorter events, 0.2 us)
Async XLA Ops:
  2.1 12.7 %collective-permute-start = (bf16[8,1152]{1,0:T(8,128)(2,1)S(1)}, bf16[8,1152]{1,0:T(8,128)(2,1)S(1)}, u32[]{:S(2)}, u32[]{:S(2)}) collective-permute-start(bf16[8,1152]{1,0:T(8,128)(2,1)S(1)} %pad_maximum_fusion.own_ref), channel_id=1, source_target_pairs={{4,0},{8,4},{12,8},{0,12},{5,1},{9,5},{13,9},{1,13},{6,2},{10,6},{... | collective-permute-start | bytes 55304 | tf_op jit(solution)/shard_map/ppermute | solution.py:235
  8.9 6.5 %collective-permute-start.1 = (bf16[8,1152]{1,0:T(8,128)(2,1)S(1)}, bf16[8,1152]{1,0:T(8,128)(2,1)S(1)}, u32[]{:S(2)}, u32[]{:S(2)}) collective-permute-start(bf16[8,1152]{1,0:T(8,128)(2,1)S(1)} %pad_maximum_fusion.own_ref), channel_id=1, source_target_pairs={{8,0},{12,4},{0,8},{4,12},{9,1},{13,5},{1,9},{5,13},{10,2},{14,6},... | collective-permute-start | bytes 55304 | tf_op jit(solution)/shard_map/ppermute | solution.py:235
  9.8 5.6 %collective-permute-start.2 = (bf16[8,1152]{1,0:T(8,128)(2,1)S(1)}, bf16[8,1152]{1,0:T(8,128)(2,1)S(1)}, u32[]{:S(2)}, u32[]{:S(2)}) collective-permute-start(bf16[8,1152]{1,0:T(8,128)(2,1)S(1)} %pad_maximum_fusion.own_ref), channel_id=1, source_target_pairs={{12,0},{0,4},{4,8},{8,12},{13,1},{1,5},{5,9},{9,13},{14,2},{2,6},{... | collective-permute-start | bytes 55304 | tf_op jit(solution)/shard_map/ppermute | solution.py:235
  13.5 1.2 %copy-start.2 = (bf16[512,1024]{1,0:T(8,128)(2,1)S(1)}, bf16[512,1024]{1,0:T(8,128)(2,1)}, u32[]{:S(2)}) copy-start(bf16[512,1024]{1,0:T(8,128)(2,1)} %kvw_ref.3) | copy-start | bytes 3145732
  14.7 18.1 %copy-start.3 = (bf16[512,1024]{1,0:T(8,128)(2,1)S(1)}, bf16[512,1024]{1,0:T(8,128)(2,1)}, u32[]{:S(2)}) copy-start(bf16[512,1024]{1,0:T(8,128)(2,1)} %kvw_ref.3) | copy-start | bytes 3145732
  14.7 18.1 %copy-start.4 = (bf16[512,512]{1,0:T(8,128)(2,1)S(1)}, bf16[512,512]{1,0:T(8,128)(2,1)}, u32[]{:S(2)}) copy-start(bf16[512,512]{1,0:T(8,128)(2,1)} %weight_ref.3) | copy-start | bytes 1572868
  14.7 18.1 %copy-start.7 = (bf16[512,512]{1,0:T(8,128)(2,1)S(1)}, bf16[512,512]{1,0:T(8,128)(2,1)}, u32[]{:S(2)}) copy-start(bf16[512,512]{1,0:T(8,128)(2,1)} %hist_ref.1) | copy-start | bytes 1572868
  32.8 21.2 %copy-start = (bf16[512,512]{1,0:T(8,128)(2,1)S(1)}, bf16[512,512]{1,0:T(8,128)(2,1)}, u32[]{:S(2)}) copy-start(bf16[512,512]{1,0:T(8,128)(2,1)} %unit_ref.3) | copy-start | bytes 1572868
  32.8 21.2 %copy-start.1 = (bf16[512,512]{1,0:T(8,128)(2,1)S(1)}, bf16[512,512]{1,0:T(8,128)(2,1)}, u32[]{:S(2)}) copy-start(bf16[512,512]{1,0:T(8,128)(2,1)} %out_ref.3) | copy-start | bytes 1572868
  48.0 7.8 %collective-permute-start.3 = (bf16[32,512]{1,0:T(8,128)(2,1)S(1)}, bf16[32,512]{1,0:T(8,128)(2,1)S(1)}, u32[]{:S(2)}, u32[]{:S(2)}) collective-permute-start(bf16[32,512]{1,0:T(8,128)(2,1)S(1)} %shard_map.124.own_ref), channel_id=1, source_target_pairs={{4,0},{8,4},{12,8},{0,12},{5,1},{9,5},{13,9},{1,13},{6,2},{10,6},{... | collective-permute-start | bytes 98312 | tf_op jit(solution)/shard_map/ppermute | solution.py:235
  49.5 6.7 %collective-permute-start.4 = (bf16[32,512]{1,0:T(8,128)(2,1)S(1)}, bf16[32,512]{1,0:T(8,128)(2,1)S(1)}, u32[]{:S(2)}, u32[]{:S(2)}) collective-permute-start(bf16[32,512]{1,0:T(8,128)(2,1)S(1)} %shard_map.124.own_ref), channel_id=1, source_target_pairs={{8,0},{12,4},{0,8},{4,12},{9,1},{13,5},{1,9},{5,13},{10,2},{14,6},... | collective-permute-start | bytes 98312 | tf_op jit(solution)/shard_map/ppermute | solution.py:235
  53.8 4.9 %collective-permute-start.5 = (bf16[32,512]{1,0:T(8,128)(2,1)S(1)}, bf16[32,512]{1,0:T(8,128)(2,1)S(1)}, u32[]{:S(2)}, u32[]{:S(2)}) collective-permute-start(bf16[32,512]{1,0:T(8,128)(2,1)S(1)} %shard_map.124.own_ref), channel_id=1, source_target_pairs={{12,0},{0,4},{4,8},{8,12},{13,1},{1,5},{5,9},{9,13},{14,2},{2,6},{... | collective-permute-start | bytes 98312 | tf_op jit(solution)/shard_map/ppermute | solution.py:235
  77.2 15.4 %copy-start.5 = (bf16[8,512]{1,0:T(8,128)(2,1)S(1)}, bf16[8,512]{1,0:T(8,128)(2,1)}, u32[]{:S(2)}) copy-start(bf16[8,512]{1,0:T(8,128)(2,1)} %embed_ref.1) | copy-start | bytes 24580
  77.2 15.4 %copy-start.6 = (bf16[8,512]{1,0:T(8,128)(2,1)S(1)}, bf16[8,512]{1,0:T(8,128)(2,1)}, u32[]{:S(2)}) copy-start(bf16[8,512]{1,0:T(8,128)(2,1)} %grad_ref.1) | copy-start | bytes 24580
  77.2 28.2 %all-to-all-start.3 = ((bf16[64,8,512]{2,1,0:T(8,128)(2,1)}), bf16[64,8,512]{2,1,0:T(8,128)(2,1)S(1)}, u32[]{:S(2)}, u32[]{:S(2)}) async-start(bf16[64,8,512]{2,1,0:T(8,128)(2,1)} %bitcast.6), calls=%async_computation.3 | async-start | bytes 1048576 | tf_op jit(solution)/shard_map/all_to_all | solution.py:287
  82.9 8.5 %collective-permute-start.6 = (bf16[256,512]{1,0:T(8,128)(2,1)S(1)}, bf16[256,512]{1,0:T(8,128)(2,1)S(1)}, u32[]{:S(2)}, u32[]{:S(2)}) collective-permute-start(bf16[256,512]{1,0:T(8,128)(2,1)S(1)} %get-tuple-element.40), channel_id=1, source_target_pairs={{0,1},{1,0},{2,3},{3,2},{4,5},{5,4},{6,7},{7,6},{8,9},{9,8},{10,11... | collective-permute-start | bytes 786440 | tf_op jit(solution)/shard_map/ppermute | solution.py:292
  91.5 10.8 %collective-permute-start.7 = (bf16[256,512]{1,0:T(8,128)(2,1)S(1)}, bf16[256,512]{1,0:T(8,128)(2,1)S(1)}, u32[]{:S(2)}, u32[]{:S(2)}) collective-permute-start(bf16[256,512]{1,0:T(8,128)(2,1)S(1)} %shard_map.130.one_ref), channel_id=1, source_target_pairs={{0,2},{1,3},{2,0},{3,1},{4,6},{5,7},{6,4},{7,5},{8,10},{9,11},{10,... | collective-permute-start | bytes 786440 | tf_op jit(solution)/shard_map/ppermute | solution.py:294
  102.4 3.0 %collective-permute-start.8 = (bf16[256,512]{1,0:T(8,128)(2,1)S(1)}, bf16[256,512]{1,0:T(8,128)(2,1)S(1)}, u32[]{:S(2)}, u32[]{:S(2)}) collective-permute-start(bf16[256,512]{1,0:T(8,128)(2,1)S(1)} %shard_map.131.mine_ref), channel_id=1, source_target_pairs={{0,1},{1,0},{2,3},{3,2},{4,5},{5,4},{6,7},{7,6},{8,9},{9,8},{10,11... | collective-permute-start | bytes 786440 | tf_op jit(solution)/shard_map/ppermute | solution.py:296

commit v8 on v5

--- a/solution.py
+++ b/solution.py
@@ -53,8 +53,11 @@
 def spread_kernel(high_ref, own_ref, one_ref, two_ref, three_ref, *rest):
     column_ref, plane_ref = rest[-2:]
     refs = (own_ref, one_ref, two_ref, three_ref)
-    column = jnp.concatenate([r[...].astype(F32) for r in refs], axis=0)
-    column = pltpu.roll(column, high_ref[0] * own_ref.shape[0], 0).astype(BF16)
+    odd, upper = (high_ref[0] & 1) == 1, high_ref[0] >= 2
+    a, b, c, d = [r[...].astype(F32) for r in refs]
+    a, b, c, d = [jnp.where(odd, x, y) for x, y in ((b, a), (a, b), (d, c), (c, d))]
+    a, b, c, d = [jnp.where(upper, x, y) for x, y in ((c, a), (d, b), (a, c), (b, d))]
+    column = jnp.concatenate([a, b, c, d], axis=0).astype(BF16)
     column_ref[...] = column
     for i in range(plane_ref.shape[0]):
         plane_ref[i] = column[:, : plane_ref.shape[2]]
@@ -220,7 +223,7 @@
     s = jax.ShapeDtypeStruct
 
     def from_up(value, k):
-        return lax.ppermute(value, "high", [((i + k) % HIGH, i) for i in range(HIGH)])
+        return lax.ppermute(value, "high", [(i ^ k, i) for i in range(HIGH)])
 
     def exchange(value):
         parts = value.reshape(plane, column, value.shape[-1])

time: 108 us -> 108 us (level)
    ppermute x6, starting transfers between devices: 16.1 us -> 14.7 us  [from_up(): return lax.ppermute(value, 'high', [(i ^ k, i) for i in range(HIGH)])]
where the time goes in v8:
time: 108 us
  blocking collectives  41 us (38%)
  starting transfers between devices  31 us (29%)
  waiting for transfers between devices  16.7 us (15%)
  Pallas kernels  14.1 us (13%)
  between operations  2.04 us (2%)
  other arithmetic  1.38 us (1%)
  local copies, waits for them, and re-layouts  1.33 us (1%)
    all_to_all x3, blocking collectives, exchange(): return lax.all_to_all(parts, 'plane', 0, 0).reshape(rows, value.shape[-1])  41 us
    ppermute x6, starting transfers between devices, from_up(): return lax.ppermute(value, 'high', [(i ^ k, i) for i in range(HIGH)])  14.7 us
    ppermute x1, waiting for transfers between devices, shards(): got = lax.ppermute(pair, 'cand', swap_chip)  9.99 us
    ppermute x1, starting transfers between devices, shards(): got = lax.ppermute(other, 'cand', swap_core)  8.07 us
    pallas_call x1, Pallas kernels, shards(): call(backward_kernel, 'ssvvvvvv', [big, (s((half, width), F32), 'v'), hal...  7.45 us
    all_to_all x1, starting transfers between devices, shards(): lax.all_to_all(dq.reshape(plane * HIGH, own, width), ('plane', 'high'), 0...  5.95 us
    ppermute x6, waiting for transfers between devices, from_up(): return lax.ppermute(value, 'high', [(i ^ k, i) for i in range(HIGH)])  5.14 us
    pallas_call x1, Pallas kernels, shards(): call(forward_kernel, 'ssvvvv', [wide, wide, big, big], flops=1 << 31)  3.26 us
  transfers between devices with their start and end apart: 10, of which 6 were waited for; matrix products, arithmetic and copies ran while one was open for 0% of the time, Pallas kernels for 2%

profile of v8, /device:TPU:1, one launch (start us, length us, event | category | flops | bytes accessed | tf_op | source)
XLA Modules:
  0.0 107.6 jit_solution(11969981165747217734)
XLA Ops:
  0.6 0.7 convert_element_type.4
  1.3 0.1 broadcast_in_dim.2
  1.4 0.7 pad_maximum_fusion.own_ref
  2.1 3.8 %collective-permute-start = (bf16[8,1152]{1,0:T(8,128)(2,1)S(1)}, bf16[8,1152]{1,0:T(8,128)(2,1)S(1)}, u32[]{:S(2)}, u32[]{:S(2)}) collective-permute-start(bf16[8,1152]{1,0:T(8,128)(2,1)S(1)} %pad_maximum_fusion.own_ref), channel_id=1, source_target_pairs={{4,0},{0,4},{12,8},{8,12},{5,1},{1,5},{13,9},{9,13},{6,2},{2,6},{1... | collective-permute-start | bytes 55304 | tf_op jit(solution)/shard_map/ppermute | solution.py:226
  5.9 5.1 %collective-permute-start.1 = (bf16[8,1152]{1,0:T(8,128)(2,1)S(1)}, bf16[8,1152]{1,0:T(8,128)(2,1)S(1)}, u32[]{:S(2)}, u32[]{:S(2)}) collective-permute-start(bf16[8,1152]{1,0:T(8,128)(2,1)S(1)} %pad_maximum_fusion.own_ref), channel_id=1, source_target_pairs={{8,0},{12,4},{0,8},{4,12},{9,1},{13,5},{1,9},{5,13},{10,2},{14,6},... | collective-permute-start | bytes 55304 | tf_op jit(solution)/shard_map/ppermute | solution.py:226
  12.3 1.2 %copy-done.2 = bf16[512,1024]{1,0:T(8,128)(2,1)S(1)} copy-done((bf16[512,1024]{1,0:T(8,128)(2,1)S(1)}, bf16[512,1024]{1,0:T(8,128)(2,1)}, u32[]{:S(2)}) %copy-start.2) | copy-done | bytes 1048600
  13.6 2.2 %collective-permute-done.2.three_ref = bf16[8,1152]{1,0:T(8,128)(2,1)S(1)} collective-permute-done((bf16[8,1152]{1,0:T(8,128)(2,1)S(1)}, bf16[8,1152]{1,0:T(8,128)(2,1)S(1)}, u32[]{:S(2)}, u32[]{:S(2)}) %collective-permute-start.2) | collective-permute-done | bytes 18464 | tf_op jit(solution)/shard_map/ppermute | solution.py:226
  15.7 0.1 shard_map.122
  15.8 17.0 %all_to_all.20 = bf16[16,32,640]{2,1,0:T(8,128)(2,1)S(1)} all-to-all(bf16[16,32,640]{2,1,0:T(8,128)(2,1)S(1)} %get-tuple-element.20), channel_id=1, replica_groups=mesh['plane'=16,'high'=4,'cand'=4] {'plane'}, dimensions={0} | all-to-all | bytes 1310720 | tf_op jit(solution)/shard_map/all_to_all | solution.py:230
  32.9 3.3 %shard_map.123 = (bf16[4,1024,128]{2,1,0:T(8,128)(2,1)S(1)}, bf16[4,1024,128]{2,1,0:T(8,128)(2,1)S(1)}, bf16[512,512]{1,0:T(8,128)(2,1)S(1)}, bf16[512,512]{1,0:T(8,128)(2,1)S(1)}) custom-call(s32[1]{0:T(128)S(6)} %copy.13.rest_0_.user_ref, s32[1]{0:T(128)S(6)} %copy.14.rest_1_.length_ref, bf16[512,640]{1,0:T(8,128)(2,1)S(1)} %bitcast.10, ...), custom_call_target="tpu_custom_call" | custom-call | flops 2147483648 | bytes 1048576 | tf_op jit(solution)/shard_map/pallas_call | solution.py:255
  36.1 12.3 %all_to_all.21 = bf16[16,32,512]{2,1,0:T(8,128)(2,1)S(1)} all-to-all(bf16[16,32,512]{2,1,0:T(8,128)(2,1)S(1)} %bitcast.13), channel_id=1, replica_groups=mesh['plane'=16,'high'=4,'cand'=4] {'plane'}, dimensions={0} | all-to-all | bytes 1048576 | tf_op jit(solution)/shard_map/all_to_all | solution.py:230
  48.5 0.1 shard_map.124.own_ref
  48.5 1.3 %collective-permute-start.3 = (bf16[32,512]{1,0:T(8,128)(2,1)S(1)}, bf16[32,512]{1,0:T(8,128)(2,1)S(1)}, u32[]{:S(2)}, u32[]{:S(2)}) collective-permute-start(bf16[32,512]{1,0:T(8,128)(2,1)S(1)} %shard_map.124.own_ref), channel_id=1, source_target_pairs={{4,0},{0,4},{12,8},{8,12},{5,1},{1,5},{13,9},{9,13},{6,2},{2,6},{1... | collective-permute-start | bytes 98312 | tf_op jit(solution)/shard_map/ppermute | solution.py:226
  49.8 2.9 %collective-permute-start.4 = (bf16[32,512]{1,0:T(8,128)(2,1)S(1)}, bf16[32,512]{1,0:T(8,128)(2,1)S(1)}, u32[]{:S(2)}, u32[]{:S(2)}) collective-permute-start(bf16[32,512]{1,0:T(8,128)(2,1)S(1)} %shard_map.124.own_ref), channel_id=1, source_target_pairs={{8,0},{12,4},{0,8},{4,12},{9,1},{13,5},{1,9},{5,13},{10,2},{14,6},... | collective-permute-start | bytes 98312 | tf_op jit(solution)/shard_map/ppermute | solution.py:226
  52.7 1.6 %collective-permute-start.5 = (bf16[32,512]{1,0:T(8,128)(2,1)S(1)}, bf16[32,512]{1,0:T(8,128)(2,1)S(1)}, u32[]{:S(2)}, u32[]{:S(2)}) collective-permute-start(bf16[32,512]{1,0:T(8,128)(2,1)S(1)} %shard_map.124.own_ref), channel_id=1, source_target_pairs={{12,0},{8,4},{4,8},{0,12},{13,1},{9,5},{5,9},{1,13},{14,2},{10,6},... | collective-permute-start | bytes 98312 | tf_op jit(solution)/shard_map/ppermute | solution.py:226
  54.3 0.3 shard_map.125
  54.7 1.8 %collective-permute-done.4.two_ref = bf16[32,512]{1,0:T(8,128)(2,1)S(1)} collective-permute-done((bf16[32,512]{1,0:T(8,128)(2,1)S(1)}, bf16[32,512]{1,0:T(8,128)(2,1)S(1)}, u32[]{:S(2)}, u32[]{:S(2)}) %collective-permute-start.4) | collective-permute-done | bytes 32800 | tf_op jit(solution)/shard_map/ppermute | solution.py:226
  56.5 1.1 %collective-permute-done.5.three_ref = bf16[32,512]{1,0:T(8,128)(2,1)S(1)} collective-permute-done((bf16[32,512]{1,0:T(8,128)(2,1)S(1)}, bf16[32,512]{1,0:T(8,128)(2,1)S(1)}, u32[]{:S(2)}, u32[]{:S(2)}) %collective-permute-start.5) | collective-permute-done | bytes 32800 | tf_op jit(solution)/shard_map/ppermute | solution.py:226
  57.6 0.3 shard_map.126
  57.9 11.7 %all_to_all.22 = bf16[16,32,512]{2,1,0:T(8,128)(2,1)S(1)} all-to-all(bf16[16,32,512]{2,1,0:T(8,128)(2,1)S(1)} %get-tuple-element.30), channel_id=1, replica_groups=mesh['plane'=16,'high'=4,'cand'=4] {'plane'}, dimensions={0} | all-to-all | bytes 1048576 | tf_op jit(solution)/shard_map/all_to_all | solution.py:230
  69.6 7.5 %shard_map.128 = (bf16[512,512]{1,0:T(8,128)(2,1)}, f32[256,512]{1,0:T(8,128)S(1)}, bf16[256,512]{1,0:T(8,128)(2,1)S(1)}) custom-call(s32[1]{0:T(128)S(6)} %copy.13.rest_0_.user_ref, s32[1]{0:T(128)} %bitcast.1.rest_2_.core_ref, bf16[512,640]{1,0:T(8,128)(2,1)S(1)} %bitcast.11, bf16[512,512]{1,0:T(8,128)(2,1)S(1)} %get-tuple-element.29.query_ref, ...), custom_call_target="tpu_custom_call" | custom-call | flops 4294967296 | bytes 1048576 | tf_op jit(solution)/shard_map/pallas_call | solution.py:269
  77.0 5.9 %all-to-all-start.3 = ((bf16[64,8,512]{2,1,0:T(8,128)(2,1)}), bf16[64,8,512]{2,1,0:T(8,128)(2,1)S(1)}, u32[]{:S(2)}, u32[]{:S(2)}) async-start(bf16[64,8,512]{2,1,0:T(8,128)(2,1)} %bitcast.6), calls=%async_computation.3 | async-start | bytes 1048576 | tf_op jit(solution)/shard_map/all_to_all | solution.py:276
  83.0 8.1 %collective-permute-start.6 = (bf16[256,512]{1,0:T(8,128)(2,1)S(1)}, bf16[256,512]{1,0:T(8,128)(2,1)S(1)}, u32[]{:S(2)}, u32[]{:S(2)}) collective-permute-start(bf16[256,512]{1,0:T(8,128)(2,1)S(1)} %get-tuple-element.34), channel_id=1, source_target_pairs={{0,1},{1,0},{2,3},{3,2},{4,5},{5,4},{6,7},{7,6},{8,9},{9,8},{10,11... | collective-permute-start | bytes 786440 | tf_op jit(solution)/shard_map/ppermute | solution.py:281
  91.1 1.2 %collective-permute-done.6.two_ref = bf16[256,512]{1,0:T(8,128)(2,1)S(1)} collective-permute-done((bf16[256,512]{1,0:T(8,128)(2,1)S(1)}, bf16[256,512]{1,0:T(8,128)(2,1)S(1)}, u32[]{:S(2)}, u32[]{:S(2)}) %collective-permute-start.6) | collective-permute-done | bytes 262176 | tf_op jit(solution)/shard_map/ppermute | solution.py:281
  92.3 0.8 collective-permute-start.7
  93.1 10.0 %collective-permute-done.7.two_ref = bf16[256,512]{1,0:T(8,128)(2,1)S(1)} collective-permute-done((bf16[256,512]{1,0:T(8,128)(2,1)S(1)}, bf16[256,512]{1,0:T(8,128)(2,1)S(1)}, u32[]{:S(2)}, u32[]{:S(2)}) %collective-permute-start.7) | collective-permute-done | bytes 262176 | tf_op jit(solution)/shard_map/ppermute | solution.py:283
  103.1 0.1 shard_map.130.mine_ref
  103.2 1.5 %collective-permute-start.8 = (bf16[256,512]{1,0:T(8,128)(2,1)S(1)}, bf16[256,512]{1,0:T(8,128)(2,1)S(1)}, u32[]{:S(2)}, u32[]{:S(2)}) collective-permute-start(bf16[256,512]{1,0:T(8,128)(2,1)S(1)} %shard_map.130.mine_ref), channel_id=1, source_target_pairs={{0,1},{1,0},{2,3},{3,2},{4,5},{5,4},{6,7},{7,6},{8,9},{9,8},{10,11... | collective-permute-start | bytes 786440 | tf_op jit(solution)/shard_map/ppermute | solution.py:285
  104.7 0.8 shard_map.127
  105.5 0.4 collective-permute-done.8.other_ref
  105.9 0.8 shard_map.131
  106.7 0.9 shard_map.132
  (22 shorter events, 0.1 us)
Async XLA Ops:
  2.1 11.5 %collective-permute-start = (bf16[8,1152]{1,0:T(8,128)(2,1)S(1)}, bf16[8,1152]{1,0:T(8,128)(2,1)S(1)}, u32[]{:S(2)}, u32[]{:S(2)}) collective-permute-start(bf16[8,1152]{1,0:T(8,128)(2,1)S(1)} %pad_maximum_fusion.own_ref), channel_id=1, source_target_pairs={{4,0},{0,4},{12,8},{8,12},{5,1},{1,5},{13,9},{9,13},{6,2},{2,6},{1... | collective-permute-start | bytes 55304 | tf_op jit(solution)/shard_map/ppermute | solution.py:226
  5.9 7.7 %collective-permute-start.1 = (bf16[8,1152]{1,0:T(8,128)(2,1)S(1)}, bf16[8,1152]{1,0:T(8,128)(2,1)S(1)}, u32[]{:S(2)}, u32[]{:S(2)}) collective-permute-start(bf16[8,1152]{1,0:T(8,128)(2,1)S(1)} %pad_maximum_fusion.own_ref), channel_id=1, source_target_pairs={{8,0},{12,4},{0,8},{4,12},{9,1},{13,5},{1,9},{5,13},{10,2},{14,6},... | collective-permute-start | bytes 55304 | tf_op jit(solution)/shard_map/ppermute | solution.py:226
  11.0 4.7 %collective-permute-start.2 = (bf16[8,1152]{1,0:T(8,128)(2,1)S(1)}, bf16[8,1152]{1,0:T(8,128)(2,1)S(1)}, u32[]{:S(2)}, u32[]{:S(2)}) collective-permute-start(bf16[8,1152]{1,0:T(8,128)(2,1)S(1)} %pad_maximum_fusion.own_ref), channel_id=1, source_target_pairs={{12,0},{8,4},{4,8},{0,12},{13,1},{9,5},{5,9},{1,13},{14,2},{10,6},... | collective-permute-start | bytes 55304 | tf_op jit(solution)/shard_map/ppermute | solution.py:226
  12.3 1.2 %copy-start.2 = (bf16[512,1024]{1,0:T(8,128)(2,1)S(1)}, bf16[512,1024]{1,0:T(8,128)(2,1)}, u32[]{:S(2)}) copy-start(bf16[512,1024]{1,0:T(8,128)(2,1)} %kvw_ref.3) | copy-start | bytes 3145732
  13.5 19.3 %copy-start.3 = (bf16[512,1024]{1,0:T(8,128)(2,1)S(1)}, bf16[512,1024]{1,0:T(8,128)(2,1)}, u32[]{:S(2)}) copy-start(bf16[512,1024]{1,0:T(8,128)(2,1)} %kvw_ref.3) | copy-start | bytes 3145732
  15.8 17.1 %copy-start.4 = (bf16[512,512]{1,0:T(8,128)(2,1)S(1)}, bf16[512,512]{1,0:T(8,128)(2,1)}, u32[]{:S(2)}) copy-start(bf16[512,512]{1,0:T(8,128)(2,1)} %weight_ref.3) | copy-start | bytes 1572868
  15.8 17.1 %copy-start.7 = (bf16[512,512]{1,0:T(8,128)(2,1)S(1)}, bf16[512,512]{1,0:T(8,128)(2,1)}, u32[]{:S(2)}) copy-start(bf16[512,512]{1,0:T(8,128)(2,1)} %hist_ref.1) | copy-start | bytes 1572868
  36.1 18.2 %copy-start.1 = (bf16[512,512]{1,0:T(8,128)(2,1)S(1)}, bf16[512,512]{1,0:T(8,128)(2,1)}, u32[]{:S(2)}) copy-start(bf16[512,512]{1,0:T(8,128)(2,1)} %out_ref.3) | copy-start | bytes 1572868
  48.5 5.8 %copy-start = (bf16[512,512]{1,0:T(8,128)(2,1)S(1)}, bf16[512,512]{1,0:T(8,128)(2,1)}, u32[]{:S(2)}) copy-start(bf16[512,512]{1,0:T(8,128)(2,1)} %unit_ref.3) | copy-start | bytes 1572868
  48.5 6.1 %collective-permute-start.3 = (bf16[32,512]{1,0:T(8,128)(2,1)S(1)}, bf16[32,512]{1,0:T(8,128)(2,1)S(1)}, u32[]{:S(2)}, u32[]{:S(2)}) collective-permute-start(bf16[32,512]{1,0:T(8,128)(2,1)S(1)} %shard_map.124.own_ref), channel_id=1, source_target_pairs={{4,0},{0,4},{12,8},{8,12},{5,1},{1,5},{13,9},{9,13},{6,2},{2,6},{1... | collective-permute-start | bytes 98312 | tf_op jit(solution)/shard_map/ppermute | solution.py:226
  49.8 6.7 %collective-permute-start.4 = (bf16[32,512]{1,0:T(8,128)(2,1)S(1)}, bf16[32,512]{1,0:T(8,128)(2,1)S(1)}, u32[]{:S(2)}, u32[]{:S(2)}) collective-permute-start(bf16[32,512]{1,0:T(8,128)(2,1)S(1)} %shard_map.124.own_ref), channel_id=1, source_target_pairs={{8,0},{12,4},{0,8},{4,12},{9,1},{13,5},{1,9},{5,13},{10,2},{14,6},... | collective-permute-start | bytes 98312 | tf_op jit(solution)/shard_map/ppermute | solution.py:226
  52.7 4.9 %collective-permute-start.5 = (bf16[32,512]{1,0:T(8,128)(2,1)S(1)}, bf16[32,512]{1,0:T(8,128)(2,1)S(1)}, u32[]{:S(2)}, u32[]{:S(2)}) collective-permute-start(bf16[32,512]{1,0:T(8,128)(2,1)S(1)} %shard_map.124.own_ref), channel_id=1, source_target_pairs={{12,0},{8,4},{4,8},{0,12},{13,1},{9,5},{5,9},{1,13},{14,2},{10,6},... | collective-permute-start | bytes 98312 | tf_op jit(solution)/shard_map/ppermute | solution.py:226
  77.0 29.6 %all-to-all-start.3 = ((bf16[64,8,512]{2,1,0:T(8,128)(2,1)}), bf16[64,8,512]{2,1,0:T(8,128)(2,1)S(1)}, u32[]{:S(2)}, u32[]{:S(2)}) async-start(bf16[64,8,512]{2,1,0:T(8,128)(2,1)} %bitcast.6), calls=%async_computation.3 | async-start | bytes 1048576 | tf_op jit(solution)/shard_map/all_to_all | solution.py:276
  83.0 9.2 %collective-permute-start.6 = (bf16[256,512]{1,0:T(8,128)(2,1)S(1)}, bf16[256,512]{1,0:T(8,128)(2,1)S(1)}, u32[]{:S(2)}, u32[]{:S(2)}) collective-permute-start(bf16[256,512]{1,0:T(8,128)(2,1)S(1)} %get-tuple-element.34), channel_id=1, source_target_pairs={{0,1},{1,0},{2,3},{3,2},{4,5},{5,4},{6,7},{7,6},{8,9},{9,8},{10,11... | collective-permute-start | bytes 786440 | tf_op jit(solution)/shard_map/ppermute | solution.py:281
  92.3 10.8 %collective-permute-start.7 = (bf16[256,512]{1,0:T(8,128)(2,1)S(1)}, bf16[256,512]{1,0:T(8,128)(2,1)S(1)}, u32[]{:S(2)}, u32[]{:S(2)}) collective-permute-start(bf16[256,512]{1,0:T(8,128)(2,1)S(1)} %shard_map.129.one_ref), channel_id=1, source_target_pairs={{0,2},{1,3},{2,0},{3,1},{4,6},{5,7},{6,4},{7,5},{8,10},{9,11},{10,... | collective-permute-start | bytes 786440 | tf_op jit(solution)/shard_map/ppermute | solution.py:283
  103.1 1.6 %copy-start.5 = (bf16[8,512]{1,0:T(8,128)(2,1)S(1)}, bf16[8,512]{1,0:T(8,128)(2,1)}, u32[]{:S(2)}) copy-start(bf16[8,512]{1,0:T(8,128)(2,1)} %embed_ref.1) | copy-start | bytes 24580
  103.1 1.6 %copy-start.6 = (bf16[8,512]{1,0:T(8,128)(2,1)S(1)}, bf16[8,512]{1,0:T(8,128)(2,1)}, u32[]{:S(2)}) copy-start(bf16[8,512]{1,0:T(8,128)(2,1)} %grad_ref.1) | copy-start | bytes 24580
  103.2 2.7 %collective-permute-start.8 = (bf16[256,512]{1,0:T(8,128)(2,1)S(1)}, bf16[256,512]{1,0:T(8,128)(2,1)S(1)}, u32[]{:S(2)}, u32[]{:S(2)}) collective-permute-start(bf16[256,512]{1,0:T(8,128)(2,1)S(1)} %shard_map.130.mine_ref), channel_id=1, source_target_pairs={{0,1},{1,0},{2,3},{3,2},{4,5},{5,4},{6,7},{7,6},{8,9},{9,8},{10,11... | collective-permute-start | bytes 786440 | tf_op jit(solution)/shard_map/ppermute | solution.py:285
